TPU v7x, 128 devices: a whole 4x4x4 slice. The times are simulated.
128 devices in a mesh: blk: 16 (over y, x_hi, core), head: 8 (over x_lo, z).
Axes of the slice: x: 4 (x_hi: 2, x_lo: 2; x = x_hi * 2 + x_lo), y: 4, z: 4, core: 2. Of those that a mesh axis runs over, the one named last changes fastest.
Arguments:
- queries: bfloat16 [1, 16384, 2048], P(None, ('blk', 'head')), may hold values from -5 to 5
- keys: bfloat16 [1, 16384, 512], P(None, ('blk', 'head')), may hold values from -5 to 5
- values: bfloat16 [1, 16384, 512], P(None, ('blk', 'head')), may hold values from -6 to 6
- upstream: bfloat16 [1, 16384, 2048], P(None, ('blk', 'head')), may hold values from -6 to 6
- tile_mask: int32 [1, 128, 128], replicated, may hold values from 0 to 1, as said below
- tile_order: int32 [1, 128], replicated, may hold values from 0 to 127, as said below
Outputs:
- attended: bfloat16 [1, 16384, 2048], P(None, ('blk', 'head'))
- grad_queries: bfloat16 [1, 16384, 2048], P(None, ('blk', 'head'))
- grad_keys: bfloat16 [1, 16384, 512], P(None, ('blk', 'head'))
- grad_values: bfloat16 [1, 16384, 512], P(None, ('blk', 'head'))
Inputs may be any that keep to these rules, and one draw needn't show every extreme that they name: With b(i) = i // 8 the position block of tile i: tile_mask[s, i, j] is 1 where i == j or j == 0, 0 where j > i, and 0 where b(i) - b(j) >= 3 and b(j) > 0. Whole position blocks of 8 tiles keep their inner order: tile_order[s, k * 8 + t] = p[k] * 8 + t for a permutation p of the position blocks.
All inputs are finite; a program needn't handle non-finite values.
Results may differ from a plain program's by a relative error of at most 0.012.
The roundings to bfloat16 on the way count: a program that leaves them out, or rounds other values in their place, can miss the bound.
Values may be sent and summed in bfloat16 or wider, within the bound.
No kernel may reach another device: no remote copies, remote signals or barrier semaphores. Data moves between devices by JAX's collectives and lax.ppermute only.
A program may use at most 128 MiB of HBM per device.

v0:
```python
import math

import jax
import jax.numpy as jnp
from jax import lax
from jax.sharding import PartitionSpec as P

HD = 128
TILE = 128


masked_floor = -1e30


def from_behind(array, axis, by):
    length = lax.axis_size(axis)
    return lax.ppermute(array, axis, [(i, (i + by) % length) for i in range(length)])


def on_device(queries, keys, values, upstream, tile_mask, tile_order):
    seq_count, piece_len, query_width = queries.shape
    head_size = HD
    tile_len = TILE
    head_devs = lax.axis_size("head")
    cycle_len = lax.axis_size("blk")
    kv_count = keys.shape[2] // head_size
    local_heads = query_width // head_size // head_devs
    sharing = head_devs // kv_count
    row_count = piece_len * head_devs
    tiles_per = row_count // tile_len
    tile_total = tile_order.shape[1]
    inv_root = 1.0 / math.sqrt(head_size)
    slot_keys = jnp.repeat(keys.reshape(seq_count, piece_len, kv_count, head_size), sharing, axis=2)
    slot_values = jnp.repeat(
        values.reshape(seq_count, piece_len, kv_count, head_size), sharing, axis=2
    )
    query_split = queries.reshape(seq_count, piece_len, head_devs, local_heads * head_size)
    upstream_split = upstream.reshape(seq_count, piece_len, head_devs, local_heads * head_size)
    head_query, head_keys, head_values, head_upstream = (
        lax.all_to_all(query_split, "head", split_axis=2, concat_axis=1, tiled=True),
        lax.all_to_all(slot_keys, "head", split_axis=2, concat_axis=1, tiled=True),
        lax.all_to_all(slot_values, "head", split_axis=2, concat_axis=1, tiled=True),
        lax.all_to_all(upstream_split, "head", split_axis=2, concat_axis=1, tiled=True),
    )
    head_query = head_query.reshape(seq_count, row_count, local_heads, head_size)
    head_upstream = head_upstream.reshape(seq_count, row_count, local_heads, head_size)
    kv_local = jnp.stack(
        [
            head_keys.reshape(seq_count, row_count, head_size),
            head_values.reshape(seq_count, row_count, head_size),
        ]
    )
    cycle_index = lax.axis_index("blk")
    tile_table = tile_mask.astype(jnp.float32)
    tile_ids = lax.iota(jnp.int32, tile_total)
    offsets = lax.iota(jnp.int32, tile_len)

    def tiles_of(block_index):
        return lax.dynamic_slice_in_dim(tile_order, block_index * tiles_per, tiles_per, 1)

    def places_of(tile_rows):
        return (tile_rows[:, :, None] * tile_len + offsets[None, None, :]).reshape(
            seq_count, row_count
        )

    own_tiles = tiles_of(cycle_index)
    own_places = places_of(own_tiles)
    own_onehot = (own_tiles[:, :, None] == tile_ids[None, None, :]).astype(jnp.float32)
    own_table = jnp.einsum("sqa,sab->sqb", own_onehot, tile_table)

    def position(cycle_step):
        return (cycle_index - cycle_step + cycle_len) % cycle_len

    def visible(block_index):
        other_tiles = tiles_of(block_index)
        other_onehot = (other_tiles[:, :, None] == tile_ids[None, None, :]).astype(jnp.float32)
        tile_live = jnp.einsum("sqb,skb->sqk", own_table, other_onehot) > 0.5
        tile_live = jnp.repeat(jnp.repeat(tile_live, tile_len, axis=1), tile_len, axis=2)
        causal = places_of(other_tiles)[:, None, :] <= own_places[:, :, None]
        return (tile_live & causal)[:, None, :, :]

    def block_scores(key_block):
        return (
            jnp.einsum("sqhd,skd->shqk", head_query, key_block, preferred_element_type=jnp.float32)
            * inv_root
        )

    def guarded(seen_mask, compute_block, current):
        return lax.cond(jnp.any(seen_mask), compute_block, lambda unchanged: unchanged, current)

    def stats_step(statistics, key_block, cycle_step):
        seen_mask = visible(position(cycle_step))

        def compute_block(current):
            running_top, running_sum = current
            scores = block_scores(key_block)
            block_top = jnp.max(jnp.where(seen_mask, scores, masked_floor), axis=3)
            new_top = jnp.maximum(running_top, block_top)
            weights = jnp.exp(jnp.where(seen_mask, scores - new_top[..., None], masked_floor))
            return (
                new_top,
                running_sum * jnp.exp(running_top - new_top) + jnp.sum(weights, axis=3),
            )

        return guarded(seen_mask, compute_block, statistics)

    stats_init = (
        jnp.full((seq_count, local_heads, row_count), masked_floor, jnp.float32),
        jnp.zeros((seq_count, local_heads, row_count), jnp.float32),
    )

    def stats_turn(cycle_step, loop_state):
        statistics, key_block = loop_state
        statistics = stats_step(statistics, key_block, cycle_step)
        return (statistics, from_behind(key_block, "blk", 1))

    statistics, key_last = lax.fori_loop(0, cycle_len - 1, stats_turn, (stats_init, kv_local[0]))
    statistics = stats_step(statistics, key_last, cycle_len - 1)
    running_top, running_sum = statistics
    log_total = running_top + jnp.log(running_sum)

    def value_step(accumulated, kv_block, cycle_step):
        seen_mask = visible(position(cycle_step))

        def compute_block(current):
            scores = block_scores(kv_block[0])
            weights = jnp.exp(
                jnp.where(seen_mask, scores - log_total[..., None], masked_floor)
            ).astype(jnp.bfloat16)
            return current + jnp.einsum(
                "shqk,skd->sqhd", weights, kv_block[1], preferred_element_type=jnp.float32
            )

        return guarded(seen_mask, compute_block, accumulated)

    accum_init = jnp.zeros((seq_count, row_count, local_heads, head_size), jnp.float32)

    def value_turn(cycle_step, loop_state):
        accumulated, kv_block = loop_state
        accumulated = value_step(accumulated, kv_block, cycle_step)
        return (accumulated, from_behind(kv_block, "blk", 1))

    accumulated, kv_last = lax.fori_loop(0, cycle_len - 1, value_turn, (accum_init, kv_local))
    accumulated = value_step(accumulated, kv_last, cycle_len - 1)
    attended_rows = accumulated.astype(jnp.bfloat16)
    attended = lax.all_to_all(
        attended_rows.reshape(seq_count, row_count, 1, local_heads * head_size),
        "head",
        split_axis=1,
        concat_axis=2,
        tiled=True,
    ).reshape(seq_count, piece_len, query_width)
    row_delta = jnp.sum(
        head_upstream.astype(jnp.float32) * attended_rows.astype(jnp.float32), axis=3
    ).transpose(0, 2, 1)

    def grad_step(carried, kv_block, cycle_step):
        seen_mask = visible(position(cycle_step))

        def compute_block(current):
            grad_query, grad_pair = current
            scores = block_scores(kv_block[0])
            probs = jnp.exp(jnp.where(seen_mask, scores - log_total[..., None], masked_floor))
            probs_low = probs.astype(jnp.bfloat16)
            grad_value = jnp.einsum(
                "shqk,sqhd->skd", probs_low, head_upstream, preferred_element_type=jnp.float32
            )
            grad_probs = jnp.einsum(
                "sqhd,skd->shqk", head_upstream, kv_block[1], preferred_element_type=jnp.float32
            )
            grad_scores = (probs * (grad_probs - row_delta[..., None])).astype(jnp.bfloat16)
            grad_query = grad_query + jnp.einsum(
                "shqk,skd->sqhd", grad_scores, kv_block[0], preferred_element_type=jnp.float32
            )
            grad_key = jnp.einsum(
                "shqk,sqhd->skd", grad_scores, head_query, preferred_element_type=jnp.float32
            )
            return (grad_query, grad_pair + jnp.stack([grad_key, grad_value]))

        return guarded(seen_mask, compute_block, carried)

    def pass_grads(grad_pair):
        return from_behind(grad_pair, "blk", 1)

    grads_init = (
        jnp.zeros((seq_count, row_count, local_heads, head_size), jnp.float32),
        jnp.zeros((2, seq_count, row_count, head_size), jnp.float32),
    )

    def grad_turn(cycle_step, loop_state):
        carried, kv_block = loop_state
        grad_query, grad_pair = grad_step(carried, kv_block, cycle_step)
        kv_next = from_behind(kv_block, "blk", 1)
        return ((grad_query, pass_grads(grad_pair)), kv_next)

    carried, kv_last = lax.fori_loop(0, cycle_len - 1, grad_turn, (grads_init, kv_local))
    grad_query, grad_pair = grad_step(carried, kv_last, cycle_len - 1)
    grad_pair = pass_grads(grad_pair)
    query_grad_rows = (
        (grad_query * inv_root)
        .astype(jnp.bfloat16)
        .reshape(seq_count, row_count, 1, local_heads * head_size)
    )
    grad_queries = lax.all_to_all(
        query_grad_rows, "head", split_axis=1, concat_axis=2, tiled=True
    ).reshape(seq_count, piece_len, query_width)
    pair_scale = jnp.array([inv_root, 1.0], jnp.float32)[:, None, None, None]
    scaled_pair = (grad_pair * pair_scale).reshape(2, seq_count, row_count, 1, head_size)
    returned = lax.all_to_all(
        scaled_pair.astype(jnp.bfloat16), "head", split_axis=2, concat_axis=3, tiled=True
    ).astype(scaled_pair.dtype)
    summed = returned.reshape(2, seq_count, piece_len, kv_count, sharing, head_size).sum(axis=4)
    grad_keys = summed[0].reshape(seq_count, piece_len, kv_count * head_size).astype(jnp.bfloat16)
    grad_values = summed[1].reshape(seq_count, piece_len, kv_count * head_size).astype(jnp.bfloat16)
    return (attended, grad_queries, grad_keys, grad_values)


def solution(mesh):
    return jax.shard_map(
        on_device,
        mesh=mesh,
        in_specs=(
            P(None, ("blk", "head"), None),
            P(None, ("blk", "head"), None),
            P(None, ("blk", "head"), None),
            P(None, ("blk", "head"), None),
            P(),
            P(),
        ),
        out_specs=(
            P(None, ("blk", "head"), None),
            P(None, ("blk", "head"), None),
            P(None, ("blk", "head"), None),
            P(None, ("blk", "head"), None),
        ),
        check_vma=False,
    )
```

profile of v0, /device:TPU:1, one launch (start us, length us, event | category | flops | bytes accessed | tf_op | source)
XLA Modules:
  0.0 952.4 jit_solution(1697788855799082427)
XLA Ops:
  44.9 159.0 %while.67 = (s32[]{:T(128)}, f32[1,2,1024]{2,1,0:T(2,128)S(1)}, f32[1,2,1024]{2,1,0:T(2,128)S(1)}, bf16[1,1024,128]{2,1,0:T(8,128)(2,1)S(1)}, s32[]{:T(128)}, /*...) while((s32[]{:T(128)}, f32[1,2,1024]{2,1,0:T(2,128)S(1)}, ...), condition=%wide.region_7.8_spmd.clone.clone, body=%wide.region_1.7_spmd.clone.clone.sunk | while | flops 556818496 | bytes 22470584 | solution.py:117
  106.6 8.6 collective-permute-start
  205.5 195.6 %while.68 = (s32[]{:T(128)}, f32[1,1024,2,128]{3,1,2,0:T(8,128)}, bf16[2,1,1024,128]{3,2,1,0:T(8,128)(2,1)S(1)}, s32[]{:T(128)}, s32[1,128]{1,0:T(1,128)S(1)}, /...) while((s32[]{:T(128)}, f32[1,1024,2,128]{3,1,2,0:T(8,128)}, ...), condition=%wide.region_16.17_spmd.clone.clone, body=%wide.region_12.16_spmd.clone.clone.sunk | while | flops 1087656064 | bytes 8478618 | solution.py:143
  275.1 6.9 collective-permute-done.1
  301.6 6.9 collective-permute-done.1
  341.2 6.9 collective-permute-done.1
  367.7 6.9 collective-permute-done.1
  405.5 488.4 %while.69 = (s32[]{:T(128)}, f32[1,1024,2,128]{3,1,2,0:T(8,128)S(1)}, f32[2,1,1024,128]{3,2,1,0:T(8,128)S(1)}, bf16[2,1,1024,128]{3,2,1,0:T(8,128)(2,1)S(1)}, s3...) while((s32[]{:T(128)}, ...), condition=%wide.region_24.25_spmd.clone.clone, body=%wide.region_20.0_spmd.clone.clone.sunk | while | flops 2711375872 | bytes 63807560 | solution.py:196
  411.0 11.3 %conditional.20 = ((f32[1,1024,2,128]{3,1,2,0:T(8,128)S(1)}, f32[2,1,1024,128]{3,2,1,0:T(8,128)S(1)})) conditional(s32[]{:T(128)} %convert_element_type.215, (f32[1,1024,2,128]{3,1,2,0:T(8,128)S(1)}, f32[2,1,1024,128]{3,2,1,0:T(8,128)S(1)}) %tuple.260, (pred[1024,8]{0,1:T(8,128)(4,1)S(1)}, s32[8]{0:T(128)S(1)}, s32[128]{0:T(128)S(1)}, ...), branch_computations={%region_22.22_spmd, %region_23.23_spmd} | conditional | flops 2708210688 | bytes 54317680 | solution.py:89
  422.4 13.7 %collective-permute-done.2 = f32[2,1,1024,128]{3,2,1,0:T(8,128)} collective-permute-done((f32[2,1,1024,128]{3,2,1,0:T(8,128)S(1)}, f32[2,1,1024,128]{3,2,1,0:T(8,128)}, u32[]{:S(2)}, u32[]{:S(2)}) %collective-permute-start.2) | collective-permute-done | bytes 1048608 | tf_op jit(solution)/shard_map/while/body/eval_jaxpr/ppermute | solution.py:17
  449.3 15.8 %collective-permute-done.2 = f32[2,1,1024,128]{3,2,1,0:T(8,128)} collective-permute-done((f32[2,1,1024,128]{3,2,1,0:T(8,128)S(1)}, f32[2,1,1024,128]{3,2,1,0:T(8,128)}, u32[]{:S(2)}, u32[]{:S(2)}) %collective-permute-start.2) | collective-permute-done | bytes 1048608 | tf_op jit(solution)/shard_map/while/body/eval_jaxpr/ppermute | solution.py:17
  472.1 15.3 %collective-permute-start.2 = (f32[2,1,1024,128]{3,2,1,0:T(8,128)S(1)}, f32[2,1,1024,128]{3,2,1,0:T(8,128)}, u32[]{:S(2)}, u32[]{:S(2)}) collective-permute-start(f32[2,1,1024,128]{3,2,1,0:T(8,128)S(1)} %get-tuple-element.1880), channel_id=1, source_target_pairs={{0,8},{8,16},{16,24},{24,32},{32,40},{40,48},{48,56},{56,64},{64,7... | collective-permute-start | bytes 3145736 | tf_op jit(solution)/shard_map/while/body/eval_jaxpr/ppermute | solution.py:17
  487.5 11.8 %collective-permute-done.2 = f32[2,1,1024,128]{3,2,1,0:T(8,128)} collective-permute-done((f32[2,1,1024,128]{3,2,1,0:T(8,128)S(1)}, f32[2,1,1024,128]{3,2,1,0:T(8,128)}, u32[]{:S(2)}, u32[]{:S(2)}) %collective-permute-start.2) | collective-permute-done | bytes 1048608 | tf_op jit(solution)/shard_map/while/body/eval_jaxpr/ppermute | solution.py:17
  514.5 13.9 %collective-permute-done.2 = f32[2,1,1024,128]{3,2,1,0:T(8,128)} collective-permute-done((f32[2,1,1024,128]{3,2,1,0:T(8,128)S(1)}, f32[2,1,1024,128]{3,2,1,0:T(8,128)}, u32[]{:S(2)}, u32[]{:S(2)}) %collective-permute-start.2) | collective-permute-done | bytes 1048608 | tf_op jit(solution)/shard_map/while/body/eval_jaxpr/ppermute | solution.py:17
  541.3 9.6 %collective-permute-start.3 = (bf16[2,1,1024,128]{3,2,1,0:T(8,128)(2,1)S(1)}, bf16[2,1,1024,128]{3,2,1,0:T(8,128)(2,1)S(1)}, u32[]{:S(2)}, u32[]{:S(2)}) collective-permute-start(bf16[2,1,1024,128]{3,2,1,0:T(8,128)(2,1)S(1)} %copy.262), channel_id=1, source_target_pairs={{0,8},{8,16},{16,24},{24,32},{32,40},{40,48},{48,56},{56,64},{64,7... | collective-permute-start | bytes 1572872 | tf_op jit(solution)/shard_map/while/body/eval_jaxpr/ppermute | solution.py:17
  550.9 17.8 %collective-permute-done.2 = f32[2,1,1024,128]{3,2,1,0:T(8,128)} collective-permute-done((f32[2,1,1024,128]{3,2,1,0:T(8,128)S(1)}, f32[2,1,1024,128]{3,2,1,0:T(8,128)}, u32[]{:S(2)}, u32[]{:S(2)}) %collective-permute-start.2) | collective-permute-done | bytes 1048608 | tf_op jit(solution)/shard_map/while/body/eval_jaxpr/ppermute | solution.py:17
  575.6 22.1 %collective-permute-done.2 = f32[2,1,1024,128]{3,2,1,0:T(8,128)} collective-permute-done((f32[2,1,1024,128]{3,2,1,0:T(8,128)S(1)}, f32[2,1,1024,128]{3,2,1,0:T(8,128)}, u32[]{:S(2)}, u32[]{:S(2)}) %collective-permute-start.2) | collective-permute-done | bytes 1048608 | tf_op jit(solution)/shard_map/while/body/eval_jaxpr/ppermute | solution.py:17
  604.4 11.3 %conditional.20 = ((f32[1,1024,2,128]{3,1,2,0:T(8,128)S(1)}, f32[2,1,1024,128]{3,2,1,0:T(8,128)S(1)})) conditional(s32[]{:T(128)} %convert_element_type.215, (f32[1,1024,2,128]{3,1,2,0:T(8,128)S(1)}, f32[2,1,1024,128]{3,2,1,0:T(8,128)S(1)}) %tuple.260, (pred[1024,8]{0,1:T(8,128)(4,1)S(1)}, s32[8]{0:T(128)S(1)}, s32[128]{0:T(128)S(1)}, ...), branch_computations={%region_22.22_spmd, %region_23.23_spmd} | conditional | flops 2708210688 | bytes 54317680 | solution.py:89
  615.9 11.7 %collective-permute-done.2 = f32[2,1,1024,128]{3,2,1,0:T(8,128)} collective-permute-done((f32[2,1,1024,128]{3,2,1,0:T(8,128)S(1)}, f32[2,1,1024,128]{3,2,1,0:T(8,128)}, u32[]{:S(2)}, u32[]{:S(2)}) %collective-permute-start.2) | collective-permute-done | bytes 1048608 | tf_op jit(solution)/shard_map/while/body/eval_jaxpr/ppermute | solution.py:17
  642.8 13.0 %collective-permute-done.2 = f32[2,1,1024,128]{3,2,1,0:T(8,128)} collective-permute-done((f32[2,1,1024,128]{3,2,1,0:T(8,128)S(1)}, f32[2,1,1024,128]{3,2,1,0:T(8,128)}, u32[]{:S(2)}, u32[]{:S(2)}) %collective-permute-start.2) | collective-permute-done | bytes 1048608 | tf_op jit(solution)/shard_map/while/body/eval_jaxpr/ppermute | solution.py:17
  665.6 11.3 %conditional.20 = ((f32[1,1024,2,128]{3,1,2,0:T(8,128)S(1)}, f32[2,1,1024,128]{3,2,1,0:T(8,128)S(1)})) conditional(s32[]{:T(128)} %convert_element_type.215, (f32[1,1024,2,128]{3,1,2,0:T(8,128)S(1)}, f32[2,1,1024,128]{3,2,1,0:T(8,128)S(1)}) %tuple.260, (pred[1024,8]{0,1:T(8,128)(4,1)S(1)}, s32[8]{0:T(128)S(1)}, s32[128]{0:T(128)S(1)}, ...), branch_computations={%region_22.22_spmd, %region_23.23_spmd} | conditional | flops 2708210688 | bytes 54317680 | solution.py:89
  677.0 24.2 %collective-permute-done.2 = f32[2,1,1024,128]{3,2,1,0:T(8,128)} collective-permute-done((f32[2,1,1024,128]{3,2,1,0:T(8,128)S(1)}, f32[2,1,1024,128]{3,2,1,0:T(8,128)}, u32[]{:S(2)}, u32[]{:S(2)}) %collective-permute-start.2) | collective-permute-done | bytes 1048608 | tf_op jit(solution)/shard_map/while/body/eval_jaxpr/ppermute | solution.py:17
  708.0 11.3 %conditional.20 = ((f32[1,1024,2,128]{3,1,2,0:T(8,128)S(1)}, f32[2,1,1024,128]{3,2,1,0:T(8,128)S(1)})) conditional(s32[]{:T(128)} %convert_element_type.215, (f32[1,1024,2,128]{3,1,2,0:T(8,128)S(1)}, f32[2,1,1024,128]{3,2,1,0:T(8,128)S(1)}) %tuple.260, (pred[1024,8]{0,1:T(8,128)(4,1)S(1)}, s32[8]{0:T(128)S(1)}, s32[128]{0:T(128)S(1)}, ...), branch_computations={%region_22.22_spmd, %region_23.23_spmd} | conditional | flops 2708210688 | bytes 54317680 | solution.py:89
  719.4 11.7 %collective-permute-done.2 = f32[2,1,1024,128]{3,2,1,0:T(8,128)} collective-permute-done((f32[2,1,1024,128]{3,2,1,0:T(8,128)S(1)}, f32[2,1,1024,128]{3,2,1,0:T(8,128)}, u32[]{:S(2)}, u32[]{:S(2)}) %collective-permute-start.2) | collective-permute-done | bytes 1048608 | tf_op jit(solution)/shard_map/while/body/eval_jaxpr/ppermute | solution.py:17
  742.2 15.3 %collective-permute-start.2 = (f32[2,1,1024,128]{3,2,1,0:T(8,128)S(1)}, f32[2,1,1024,128]{3,2,1,0:T(8,128)}, u32[]{:S(2)}, u32[]{:S(2)}) collective-permute-start(f32[2,1,1024,128]{3,2,1,0:T(8,128)S(1)} %get-tuple-element.1880), channel_id=1, source_target_pairs={{0,8},{8,16},{16,24},{24,32},{32,40},{40,48},{48,56},{56,64},{64,7... | collective-permute-start | bytes 3145736 | tf_op jit(solution)/shard_map/while/body/eval_jaxpr/ppermute | solution.py:17
  757.6 13.0 %collective-permute-done.2 = f32[2,1,1024,128]{3,2,1,0:T(8,128)} collective-permute-done((f32[2,1,1024,128]{3,2,1,0:T(8,128)S(1)}, f32[2,1,1024,128]{3,2,1,0:T(8,128)}, u32[]{:S(2)}, u32[]{:S(2)}) %collective-permute-start.2) | collective-permute-done | bytes 1048608 | tf_op jit(solution)/shard_map/while/body/eval_jaxpr/ppermute | solution.py:17
  784.5 15.1 %collective-permute-done.2 = f32[2,1,1024,128]{3,2,1,0:T(8,128)} collective-permute-done((f32[2,1,1024,128]{3,2,1,0:T(8,128)S(1)}, f32[2,1,1024,128]{3,2,1,0:T(8,128)}, u32[]{:S(2)}, u32[]{:S(2)}) %collective-permute-start.2) | collective-permute-done | bytes 1048608 | tf_op jit(solution)/shard_map/while/body/eval_jaxpr/ppermute | solution.py:17
  807.3 15.3 %collective-permute-start.2 = (f32[2,1,1024,128]{3,2,1,0:T(8,128)S(1)}, f32[2,1,1024,128]{3,2,1,0:T(8,128)}, u32[]{:S(2)}, u32[]{:S(2)}) collective-permute-start(f32[2,1,1024,128]{3,2,1,0:T(8,128)S(1)} %get-tuple-element.1880), channel_id=1, source_target_pairs={{0,8},{8,16},{16,24},{24,32},{32,40},{40,48},{48,56},{56,64},{64,7... | collective-permute-start | bytes 3145736 | tf_op jit(solution)/shard_map/while/body/eval_jaxpr/ppermute | solution.py:17
  822.7 11.7 %collective-permute-done.2 = f32[2,1,1024,128]{3,2,1,0:T(8,128)} collective-permute-done((f32[2,1,1024,128]{3,2,1,0:T(8,128)S(1)}, f32[2,1,1024,128]{3,2,1,0:T(8,128)}, u32[]{:S(2)}, u32[]{:S(2)}) %collective-permute-start.2) | collective-permute-done | bytes 1048608 | tf_op jit(solution)/shard_map/while/body/eval_jaxpr/ppermute | solution.py:17
  849.6 11.7 %collective-permute-done.2 = f32[2,1,1024,128]{3,2,1,0:T(8,128)} collective-permute-done((f32[2,1,1024,128]{3,2,1,0:T(8,128)S(1)}, f32[2,1,1024,128]{3,2,1,0:T(8,128)}, u32[]{:S(2)}, u32[]{:S(2)}) %collective-permute-start.2) | collective-permute-done | bytes 1048608 | tf_op jit(solution)/shard_map/while/body/eval_jaxpr/ppermute | solution.py:17
  876.6 11.7 %collective-permute-done.2 = f32[2,1,1024,128]{3,2,1,0:T(8,128)} collective-permute-done((f32[2,1,1024,128]{3,2,1,0:T(8,128)S(1)}, f32[2,1,1024,128]{3,2,1,0:T(8,128)}, u32[]{:S(2)}, u32[]{:S(2)}) %collective-permute-start.2) | collective-permute-done | bytes 1048608 | tf_op jit(solution)/shard_map/while/body/eval_jaxpr/ppermute | solution.py:17
  896.2 10.1 %collective-permute-start.4 = (f32[2,1,1024,128]{3,0,2,1:T(2,128)}, f32[2,1,1024,128]{3,0,2,1:T(2,128)}, u32[]{:S(2)}, u32[]{:S(2)}) collective-permute-start(f32[2,1,1024,128]{3,0,2,1:T(2,128)} %copy.187), channel_id=1, source_target_pairs={{0,8},{8,16},{16,24},{24,32},{32,40},{40,48},{48,56},{56,64},{64,7... | collective-permute-start | bytes 3145736 | tf_op jit(solution)/shard_map/ppermute | solution.py:17
  (803 shorter events, 648.0 us)
Async XLA Ops:
  39.5 364.0 %all-to-all-start.4 = ((bf16[1,128,8,256]{1,3,0,2:T(8,128)(2,1)}), bf16[1,128,8,256]{1,3,0,2:T(8,128)(2,1)S(1)}, u32[]{:S(2)}, u32[]{:S(2)}) async-start(bf16[1,128,8,256]{1,3,0,2:T(8,128)(2,1)} %bitcast.122), calls=%async_computation.4 | async-start | bytes 1048576 | tf_op jit(solution)/shard_map/all_to_all | solution.py:43
  45.7 15.9 %collective-permute-start = (bf16[1,1024,128]{2,1,0:T(8,128)(2,1)}, bf16[1,1024,128]{2,1,0:T(8,128)(2,1)S(1)}, u32[]{:S(2)}, u32[]{:S(2)}) collective-permute-start(bf16[1,1024,128]{2,1,0:T(8,128)(2,1)} %copy.235), channel_id=1, source_target_pairs={{0,8},{8,16},{16,24},{24,32},{32,40},{40,48},{48,56},{56,64},{64,7... | collective-permute-start | bytes 786440 | tf_op jit(solution)/shard_map/while/body/eval_jaxpr/ppermute | solution.py:17
  106.6 19.7 %collective-permute-start = (bf16[1,1024,128]{2,1,0:T(8,128)(2,1)}, bf16[1,1024,128]{2,1,0:T(8,128)(2,1)S(1)}, u32[]{:S(2)}, u32[]{:S(2)}) collective-permute-start(bf16[1,1024,128]{2,1,0:T(8,128)(2,1)} %copy.235), channel_id=1, source_target_pairs={{0,8},{8,16},{16,24},{24,32},{32,40},{40,48},{48,56},{56,64},{64,7... | collective-permute-start | bytes 786440 | tf_op jit(solution)/shard_map/while/body/eval_jaxpr/ppermute | solution.py:17
  206.2 14.3 %collective-permute-start.1 = (bf16[2,1,1024,128]{3,2,1,0:T(8,128)(2,1)}, bf16[2,1,1024,128]{3,2,1,0:T(8,128)(2,1)S(1)}, u32[]{:S(2)}, u32[]{:S(2)}) collective-permute-start(bf16[2,1,1024,128]{3,2,1,0:T(8,128)(2,1)} %copy.249), channel_id=1, source_target_pairs={{0,8},{8,16},{16,24},{24,32},{32,40},{40,48},{48,56},{56,64},{64,7... | collective-permute-start | bytes 1572872 | tf_op jit(solution)/shard_map/while/body/eval_jaxpr/ppermute | solution.py:17
  422.3 17.4 %collective-permute-start.3 = (bf16[2,1,1024,128]{3,2,1,0:T(8,128)(2,1)S(1)}, bf16[2,1,1024,128]{3,2,1,0:T(8,128)(2,1)S(1)}, u32[]{:S(2)}, u32[]{:S(2)}) collective-permute-start(bf16[2,1,1024,128]{3,2,1,0:T(8,128)(2,1)S(1)} %copy.262), channel_id=1, source_target_pairs={{0,8},{8,16},{16,24},{24,32},{32,40},{40,48},{48,56},{56,64},{64,7... | collective-permute-start | bytes 1572872 | tf_op jit(solution)/shard_map/while/body/eval_jaxpr/ppermute | solution.py:17
  445.2 19.9 %collective-permute-start.2 = (f32[2,1,1024,128]{3,2,1,0:T(8,128)S(1)}, f32[2,1,1024,128]{3,2,1,0:T(8,128)}, u32[]{:S(2)}, u32[]{:S(2)}) collective-permute-start(f32[2,1,1024,128]{3,2,1,0:T(8,128)S(1)} %get-tuple-element.1880), channel_id=1, source_target_pairs={{0,8},{8,16},{16,24},{24,32},{32,40},{40,48},{48,56},{56,64},{64,7... | collective-permute-start | bytes 3145736 | tf_op jit(solution)/shard_map/while/body/eval_jaxpr/ppermute | solution.py:17
  449.3 17.4 %collective-permute-start.3 = (bf16[2,1,1024,128]{3,2,1,0:T(8,128)(2,1)S(1)}, bf16[2,1,1024,128]{3,2,1,0:T(8,128)(2,1)S(1)}, u32[]{:S(2)}, u32[]{:S(2)}) collective-permute-start(bf16[2,1,1024,128]{3,2,1,0:T(8,128)(2,1)S(1)} %copy.262), channel_id=1, source_target_pairs={{0,8},{8,16},{16,24},{24,32},{32,40},{40,48},{48,56},{56,64},{64,7... | collective-permute-start | bytes 1572872 | tf_op jit(solution)/shard_map/while/body/eval_jaxpr/ppermute | solution.py:17
  472.1 27.2 %collective-permute-start.2 = (f32[2,1,1024,128]{3,2,1,0:T(8,128)S(1)}, f32[2,1,1024,128]{3,2,1,0:T(8,128)}, u32[]{:S(2)}, u32[]{:S(2)}) collective-permute-start(f32[2,1,1024,128]{3,2,1,0:T(8,128)S(1)} %get-tuple-element.1880), channel_id=1, source_target_pairs={{0,8},{8,16},{16,24},{24,32},{32,40},{40,48},{48,56},{56,64},{64,7... | collective-permute-start | bytes 3145736 | tf_op jit(solution)/shard_map/while/body/eval_jaxpr/ppermute | solution.py:17
  487.4 17.4 %collective-permute-start.3 = (bf16[2,1,1024,128]{3,2,1,0:T(8,128)(2,1)S(1)}, bf16[2,1,1024,128]{3,2,1,0:T(8,128)(2,1)S(1)}, u32[]{:S(2)}, u32[]{:S(2)}) collective-permute-start(bf16[2,1,1024,128]{3,2,1,0:T(8,128)(2,1)S(1)} %copy.262), channel_id=1, source_target_pairs={{0,8},{8,16},{16,24},{24,32},{32,40},{40,48},{48,56},{56,64},{64,7... | collective-permute-start | bytes 1572872 | tf_op jit(solution)/shard_map/while/body/eval_jaxpr/ppermute | solution.py:17
  510.3 18.1 %collective-permute-start.2 = (f32[2,1,1024,128]{3,2,1,0:T(8,128)S(1)}, f32[2,1,1024,128]{3,2,1,0:T(8,128)}, u32[]{:S(2)}, u32[]{:S(2)}) collective-permute-start(f32[2,1,1024,128]{3,2,1,0:T(8,128)S(1)} %get-tuple-element.1880), channel_id=1, source_target_pairs={{0,8},{8,16},{16,24},{24,32},{32,40},{40,48},{48,56},{56,64},{64,7... | collective-permute-start | bytes 3145736 | tf_op jit(solution)/shard_map/while/body/eval_jaxpr/ppermute | solution.py:17
  514.4 17.4 %collective-permute-start.3 = (bf16[2,1,1024,128]{3,2,1,0:T(8,128)(2,1)S(1)}, bf16[2,1,1024,128]{3,2,1,0:T(8,128)(2,1)S(1)}, u32[]{:S(2)}, u32[]{:S(2)}) collective-permute-start(bf16[2,1,1024,128]{3,2,1,0:T(8,128)(2,1)S(1)} %copy.262), channel_id=1, source_target_pairs={{0,8},{8,16},{16,24},{24,32},{32,40},{40,48},{48,56},{56,64},{64,7... | collective-permute-start | bytes 1572872 | tf_op jit(solution)/shard_map/while/body/eval_jaxpr/ppermute | solution.py:17
  537.2 31.5 %collective-permute-start.2 = (f32[2,1,1024,128]{3,2,1,0:T(8,128)S(1)}, f32[2,1,1024,128]{3,2,1,0:T(8,128)}, u32[]{:S(2)}, u32[]{:S(2)}) collective-permute-start(f32[2,1,1024,128]{3,2,1,0:T(8,128)S(1)} %get-tuple-element.1880), channel_id=1, source_target_pairs={{0,8},{8,16},{16,24},{24,32},{32,40},{40,48},{48,56},{56,64},{64,7... | collective-permute-start | bytes 3145736 | tf_op jit(solution)/shard_map/while/body/eval_jaxpr/ppermute | solution.py:17
  541.3 28.6 %collective-permute-start.3 = (bf16[2,1,1024,128]{3,2,1,0:T(8,128)(2,1)S(1)}, bf16[2,1,1024,128]{3,2,1,0:T(8,128)(2,1)S(1)}, u32[]{:S(2)}, u32[]{:S(2)}) collective-permute-start(bf16[2,1,1024,128]{3,2,1,0:T(8,128)(2,1)S(1)} %copy.262), channel_id=1, source_target_pairs={{0,8},{8,16},{16,24},{24,32},{32,40},{40,48},{48,56},{56,64},{64,7... | collective-permute-start | bytes 1572872 | tf_op jit(solution)/shard_map/while/body/eval_jaxpr/ppermute | solution.py:17
  575.4 22.3 %collective-permute-start.2 = (f32[2,1,1024,128]{3,2,1,0:T(8,128)S(1)}, f32[2,1,1024,128]{3,2,1,0:T(8,128)}, u32[]{:S(2)}, u32[]{:S(2)}) collective-permute-start(f32[2,1,1024,128]{3,2,1,0:T(8,128)S(1)} %get-tuple-element.1880), channel_id=1, source_target_pairs={{0,8},{8,16},{16,24},{24,32},{32,40},{40,48},{48,56},{56,64},{64,7... | collective-permute-start | bytes 3145736 | tf_op jit(solution)/shard_map/while/body/eval_jaxpr/ppermute | solution.py:17
  575.5 23.4 %collective-permute-start.3 = (bf16[2,1,1024,128]{3,2,1,0:T(8,128)(2,1)S(1)}, bf16[2,1,1024,128]{3,2,1,0:T(8,128)(2,1)S(1)}, u32[]{:S(2)}, u32[]{:S(2)}) collective-permute-start(bf16[2,1,1024,128]{3,2,1,0:T(8,128)(2,1)S(1)} %copy.262), channel_id=1, source_target_pairs={{0,8},{8,16},{16,24},{24,32},{32,40},{40,48},{48,56},{56,64},{64,7... | collective-permute-start | bytes 1572872 | tf_op jit(solution)/shard_map/while/body/eval_jaxpr/ppermute | solution.py:17
  615.8 17.4 %collective-permute-start.3 = (bf16[2,1,1024,128]{3,2,1,0:T(8,128)(2,1)S(1)}, bf16[2,1,1024,128]{3,2,1,0:T(8,128)(2,1)S(1)}, u32[]{:S(2)}, u32[]{:S(2)}) collective-permute-start(bf16[2,1,1024,128]{3,2,1,0:T(8,128)(2,1)S(1)} %copy.262), channel_id=1, source_target_pairs={{0,8},{8,16},{16,24},{24,32},{32,40},{40,48},{48,56},{56,64},{64,7... | collective-permute-start | bytes 1572872 | tf_op jit(solution)/shard_map/while/body/eval_jaxpr/ppermute | solution.py:17
  638.7 17.1 %collective-permute-start.2 = (f32[2,1,1024,128]{3,2,1,0:T(8,128)S(1)}, f32[2,1,1024,128]{3,2,1,0:T(8,128)}, u32[]{:S(2)}, u32[]{:S(2)}) collective-permute-start(f32[2,1,1024,128]{3,2,1,0:T(8,128)S(1)} %get-tuple-element.1880), channel_id=1, source_target_pairs={{0,8},{8,16},{16,24},{24,32},{32,40},{40,48},{48,56},{56,64},{64,7... | collective-permute-start | bytes 3145736 | tf_op jit(solution)/shard_map/while/body/eval_jaxpr/ppermute | solution.py:17
  642.7 17.4 %collective-permute-start.3 = (bf16[2,1,1024,128]{3,2,1,0:T(8,128)(2,1)S(1)}, bf16[2,1,1024,128]{3,2,1,0:T(8,128)(2,1)S(1)}, u32[]{:S(2)}, u32[]{:S(2)}) collective-permute-start(bf16[2,1,1024,128]{3,2,1,0:T(8,128)(2,1)S(1)} %copy.262), channel_id=1, source_target_pairs={{0,8},{8,16},{16,24},{24,32},{32,40},{40,48},{48,56},{56,64},{64,7... | collective-permute-start | bytes 1572872 | tf_op jit(solution)/shard_map/while/body/eval_jaxpr/ppermute | solution.py:17
  676.9 24.4 %collective-permute-start.2 = (f32[2,1,1024,128]{3,2,1,0:T(8,128)S(1)}, f32[2,1,1024,128]{3,2,1,0:T(8,128)}, u32[]{:S(2)}, u32[]{:S(2)}) collective-permute-start(f32[2,1,1024,128]{3,2,1,0:T(8,128)S(1)} %get-tuple-element.1880), channel_id=1, source_target_pairs={{0,8},{8,16},{16,24},{24,32},{32,40},{40,48},{48,56},{56,64},{64,7... | collective-permute-start | bytes 3145736 | tf_op jit(solution)/shard_map/while/body/eval_jaxpr/ppermute | solution.py:17
  677.0 25.5 %collective-permute-start.3 = (bf16[2,1,1024,128]{3,2,1,0:T(8,128)(2,1)S(1)}, bf16[2,1,1024,128]{3,2,1,0:T(8,128)(2,1)S(1)}, u32[]{:S(2)}, u32[]{:S(2)}) collective-permute-start(bf16[2,1,1024,128]{3,2,1,0:T(8,128)(2,1)S(1)} %copy.262), channel_id=1, source_target_pairs={{0,8},{8,16},{16,24},{24,32},{32,40},{40,48},{48,56},{56,64},{64,7... | collective-permute-start | bytes 1572872 | tf_op jit(solution)/shard_map/while/body/eval_jaxpr/ppermute | solution.py:17
  719.4 17.4 %collective-permute-start.3 = (bf16[2,1,1024,128]{3,2,1,0:T(8,128)(2,1)S(1)}, bf16[2,1,1024,128]{3,2,1,0:T(8,128)(2,1)S(1)}, u32[]{:S(2)}, u32[]{:S(2)}) collective-permute-start(bf16[2,1,1024,128]{3,2,1,0:T(8,128)(2,1)S(1)} %copy.262), channel_id=1, source_target_pairs={{0,8},{8,16},{16,24},{24,32},{32,40},{40,48},{48,56},{56,64},{64,7... | collective-permute-start | bytes 1572872 | tf_op jit(solution)/shard_map/while/body/eval_jaxpr/ppermute | solution.py:17
  742.2 28.4 %collective-permute-start.2 = (f32[2,1,1024,128]{3,2,1,0:T(8,128)S(1)}, f32[2,1,1024,128]{3,2,1,0:T(8,128)}, u32[]{:S(2)}, u32[]{:S(2)}) collective-permute-start(f32[2,1,1024,128]{3,2,1,0:T(8,128)S(1)} %get-tuple-element.1880), channel_id=1, source_target_pairs={{0,8},{8,16},{16,24},{24,32},{32,40},{40,48},{48,56},{56,64},{64,7... | collective-permute-start | bytes 3145736 | tf_op jit(solution)/shard_map/while/body/eval_jaxpr/ppermute | solution.py:17
  757.5 17.4 %collective-permute-start.3 = (bf16[2,1,1024,128]{3,2,1,0:T(8,128)(2,1)S(1)}, bf16[2,1,1024,128]{3,2,1,0:T(8,128)(2,1)S(1)}, u32[]{:S(2)}, u32[]{:S(2)}) collective-permute-start(bf16[2,1,1024,128]{3,2,1,0:T(8,128)(2,1)S(1)} %copy.262), channel_id=1, source_target_pairs={{0,8},{8,16},{16,24},{24,32},{32,40},{40,48},{48,56},{56,64},{64,7... | collective-permute-start | bytes 1572872 | tf_op jit(solution)/shard_map/while/body/eval_jaxpr/ppermute | solution.py:17
  780.4 19.2 %collective-permute-start.2 = (f32[2,1,1024,128]{3,2,1,0:T(8,128)S(1)}, f32[2,1,1024,128]{3,2,1,0:T(8,128)}, u32[]{:S(2)}, u32[]{:S(2)}) collective-permute-start(f32[2,1,1024,128]{3,2,1,0:T(8,128)S(1)} %get-tuple-element.1880), channel_id=1, source_target_pairs={{0,8},{8,16},{16,24},{24,32},{32,40},{40,48},{48,56},{56,64},{64,7... | collective-permute-start | bytes 3145736 | tf_op jit(solution)/shard_map/while/body/eval_jaxpr/ppermute | solution.py:17
  784.5 17.4 %collective-permute-start.3 = (bf16[2,1,1024,128]{3,2,1,0:T(8,128)(2,1)S(1)}, bf16[2,1,1024,128]{3,2,1,0:T(8,128)(2,1)S(1)}, u32[]{:S(2)}, u32[]{:S(2)}) collective-permute-start(bf16[2,1,1024,128]{3,2,1,0:T(8,128)(2,1)S(1)} %copy.262), channel_id=1, source_target_pairs={{0,8},{8,16},{16,24},{24,32},{32,40},{40,48},{48,56},{56,64},{64,7... | collective-permute-start | bytes 1572872 | tf_op jit(solution)/shard_map/while/body/eval_jaxpr/ppermute | solution.py:17
  807.3 27.1 %collective-permute-start.2 = (f32[2,1,1024,128]{3,2,1,0:T(8,128)S(1)}, f32[2,1,1024,128]{3,2,1,0:T(8,128)}, u32[]{:S(2)}, u32[]{:S(2)}) collective-permute-start(f32[2,1,1024,128]{3,2,1,0:T(8,128)S(1)} %get-tuple-element.1880), channel_id=1, source_target_pairs={{0,8},{8,16},{16,24},{24,32},{32,40},{40,48},{48,56},{56,64},{64,7... | collective-permute-start | bytes 3145736 | tf_op jit(solution)/shard_map/while/body/eval_jaxpr/ppermute | solution.py:17
  822.6 17.4 %collective-permute-start.3 = (bf16[2,1,1024,128]{3,2,1,0:T(8,128)(2,1)S(1)}, bf16[2,1,1024,128]{3,2,1,0:T(8,128)(2,1)S(1)}, u32[]{:S(2)}, u32[]{:S(2)}) collective-permute-start(bf16[2,1,1024,128]{3,2,1,0:T(8,128)(2,1)S(1)} %copy.262), channel_id=1, source_target_pairs={{0,8},{8,16},{16,24},{24,32},{32,40},{40,48},{48,56},{56,64},{64,7... | collective-permute-start | bytes 1572872 | tf_op jit(solution)/shard_map/while/body/eval_jaxpr/ppermute | solution.py:17
  845.5 15.8 %collective-permute-start.2 = (f32[2,1,1024,128]{3,2,1,0:T(8,128)S(1)}, f32[2,1,1024,128]{3,2,1,0:T(8,128)}, u32[]{:S(2)}, u32[]{:S(2)}) collective-permute-start(f32[2,1,1024,128]{3,2,1,0:T(8,128)S(1)} %get-tuple-element.1880), channel_id=1, source_target_pairs={{0,8},{8,16},{16,24},{24,32},{32,40},{40,48},{48,56},{56,64},{64,7... | collective-permute-start | bytes 3145736 | tf_op jit(solution)/shard_map/while/body/eval_jaxpr/ppermute | solution.py:17
  849.6 17.4 %collective-permute-start.3 = (bf16[2,1,1024,128]{3,2,1,0:T(8,128)(2,1)S(1)}, bf16[2,1,1024,128]{3,2,1,0:T(8,128)(2,1)S(1)}, u32[]{:S(2)}, u32[]{:S(2)}) collective-permute-start(bf16[2,1,1024,128]{3,2,1,0:T(8,128)(2,1)S(1)} %copy.262), channel_id=1, source_target_pairs={{0,8},{8,16},{16,24},{24,32},{32,40},{40,48},{48,56},{56,64},{64,7... | collective-permute-start | bytes 1572872 | tf_op jit(solution)/shard_map/while/body/eval_jaxpr/ppermute | solution.py:17
  872.4 15.8 %collective-permute-start.2 = (f32[2,1,1024,128]{3,2,1,0:T(8,128)S(1)}, f32[2,1,1024,128]{3,2,1,0:T(8,128)}, u32[]{:S(2)}, u32[]{:S(2)}) collective-permute-start(f32[2,1,1024,128]{3,2,1,0:T(8,128)S(1)} %get-tuple-element.1880), channel_id=1, source_target_pairs={{0,8},{8,16},{16,24},{24,32},{32,40},{40,48},{48,56},{56,64},{64,7... | collective-permute-start | bytes 3145736 | tf_op jit(solution)/shard_map/while/body/eval_jaxpr/ppermute | solution.py:17
  876.5 17.4 %collective-permute-start.3 = (bf16[2,1,1024,128]{3,2,1,0:T(8,128)(2,1)S(1)}, bf16[2,1,1024,128]{3,2,1,0:T(8,128)(2,1)S(1)}, u32[]{:S(2)}, u32[]{:S(2)}) collective-permute-start(bf16[2,1,1024,128]{3,2,1,0:T(8,128)(2,1)S(1)} %copy.262), channel_id=1, source_target_pairs={{0,8},{8,16},{16,24},{24,32},{32,40},{40,48},{48,56},{56,64},{64,7... | collective-permute-start | bytes 1572872 | tf_op jit(solution)/shard_map/while/body/eval_jaxpr/ppermute | solution.py:17
  896.2 32.0 %collective-permute-start.4 = (f32[2,1,1024,128]{3,0,2,1:T(2,128)}, f32[2,1,1024,128]{3,0,2,1:T(2,128)}, u32[]{:S(2)}, u32[]{:S(2)}) collective-permute-start(f32[2,1,1024,128]{3,0,2,1:T(2,128)} %copy.187), channel_id=1, source_target_pairs={{0,8},{8,16},{16,24},{24,32},{32,40},{40,48},{48,56},{56,64},{64,7... | collective-permute-start | bytes 3145736 | tf_op jit(solution)/shard_map/ppermute | solution.py:17
  (55 other events, 898.2 us)
where the time goes:
time: 971 us; the launch traced here: 952 us
  waiting for transfers between devices  342 us (35%)
  other arithmetic  223 us (23%)
  starting transfers between devices  179 us (18%)
  local copies, waits for them, and re-layouts  87.5 us (9%)
  matrix products  85.1 us (9%)
  loops' own time  33.3 us (3%)
    ppermute x61, waiting for transfers between devices, from_behind(): lax.ppermute(array, axis, [(i, (i + by) % length) for i in range(length)])  324 us
    reduce_or x46, other arithmetic, guarded(): jnp.any(seen_mask)  181 us
    ppermute x61, starting transfers between devices, from_behind(): lax.ppermute(array, axis, [(i, (i + by) % length) for i in range(length)])  146 us
    while x60, local copies, waits for them, and re-layouts  41.4 us
    dot_general x4, matrix products, compute_block(): jnp.einsum('shqk,skd->sqhd', weights, kv_block[1], preferred_element_type...  23.8 us
    dot_general x8, matrix products, block_scores(): jnp.einsum('sqhd,skd->shqk', head_query, key_block, preferred_element_typ...  20.5 us
  transfers between devices with their start and end apart: 68, of which 47 were waited for; matrix products, arithmetic and copies ran while one was open for 28% of the time, Pallas kernels for 0%

commit v1 on v0

v1 whole, which is shorter than its diff:
```python
import math

import jax
import jax.numpy as jnp
from jax import lax
from jax.experimental import pallas as pl
from jax.experimental.pallas import tpu as pltpu
from jax.sharding import PartitionSpec as P

HD = 128
TILE = 128
BT = 8
NB = 16
SL = 8
GROUP = 2
SLOTS = 32
INV_ROOT = 1.0 / math.sqrt(HD)
SCORE_SCALE = INV_ROOT * math.log2(math.e)
FLOOR = -1e30

NT = (((1,), (1,)), ((), ()))


def dot(a, b):
    return jnp.dot(a, b, preferred_element_type=jnp.float32)


def dot_nt(a, b):
    return lax.dot_general(a, b, NT, preferred_element_type=jnp.float32)


def block_of(order_ref, index):
    return lax.shift_right_logical(order_ref[index * BT], 3)


def invert_blocks(order_ref, where_ref):
    for k in range(NB):
        where_ref[block_of(order_ref, k)] = k


def gather_kernel(order_ref, pieces_ref, out_ref, where_ref):
    invert_blocks(order_ref, where_ref)

    @pl.loop(0, NB)
    def _(k):
        b = block_of(order_ref, k)
        for j in range(3):
            src = jnp.maximum(b - 1 - j, 0) if j < 2 else 0
            out_ref[k, j] = pieces_ref[where_ref[src]]


def sum_kernel(order_ref, parts_ref, out_ref, where_ref):
    invert_blocks(order_ref, where_ref)

    @pl.loop(0, NB)
    def _(k):
        b = block_of(order_ref, k)
        near = parts_ref[where_ref[jnp.minimum(b + 1, NB - 1)], 0].astype(jnp.float32)
        far = parts_ref[where_ref[jnp.minimum(b + 2, NB - 1)], 1].astype(jnp.float32)
        total = jnp.where(b + 1 < NB, near, 0.0) + jnp.where(b + 2 < NB, far, 0.0)
        out_ref[k] = total.astype(jnp.bfloat16)

    first = where_ref[0]
    total = parts_ref[where_ref[1], 0].astype(jnp.float32)
    total = total + parts_ref[where_ref[2], 1].astype(jnp.float32)
    for b in range(3, NB):
        total = total + parts_ref[where_ref[b], 2].astype(jnp.float32)
    out_ref[first] = total.astype(jnp.bfloat16)


def attend_kernel(
    order_ref, mask_ref, rows_ref, far_ref, out_ref, dfar_ref,
    k_s, v_s, kt_s, vt_s, s_buf, dk_s, dv_s, dq_s, mask_s, list_s, count_s, sem,
):
    b = block_of(order_ref, lax.axis_index("blk"))
    copy = pltpu.make_async_copy(mask_ref.at[pl.ds(pl.multiple_of(b * BT, BT), BT)], mask_s, sem)
    copy.start()
    dk_s[...] = jnp.zeros_like(dk_s)
    dv_s[...] = jnp.zeros_like(dv_s)

    @pl.loop(0, BT)
    def _(t):
        key = rows_ref[t, :, 512:640]
        value = rows_ref[t, :, 640:768]
        k_s[t] = key
        v_s[t] = value
        kt_s[t] = key.T
        vt_s[t] = value.T

    @pl.loop(0, SLOTS - BT)
    def _(c):
        key = jnp.concatenate([far_ref[0, s, c] for s in range(SL)], axis=0)
        value = jnp.concatenate([far_ref[1, s, c] for s in range(SL)], axis=0)
        k_s[BT + c] = key
        v_s[BT + c] = value
        kt_s[BT + c] = key.T
        vt_s[BT + c] = value.T

    copy.wait()

    @pl.loop(0, BT)
    def _(r):
        count = jnp.int32(0)
        for c in range(SLOTS):
            j, t = divmod(c, BT)
            if j == 0:
                live = (mask_s[r, b * BT + t] == 1) & (t < r)
            elif j < 3:
                live = (mask_s[r, jnp.maximum(b - j, 0) * BT + t] == 1) & (b >= j)
            else:
                live = (mask_s[r, t] == 1) & (b >= 3)
            list_s[r, count] = c
            count = count + live.astype(jnp.int32)
        count_s[r] = count

    q_pos = lax.broadcasted_iota(jnp.int32, (TILE, 2 * TILE), 1) % TILE
    k_pos = lax.broadcasted_iota(jnp.int32, (TILE, 2 * TILE), 0)
    causal = k_pos <= q_pos

    def fold(x, op):
        return op(x.reshape(-1, 8, 2 * TILE), axis=0)

    @pl.loop(0, BT)
    def _(r):
        def stacked(lo):
            return jnp.concatenate(
                [rows_ref[r, :, lo : lo + HD], rows_ref[r, :, lo + HD : lo + 2 * HD]], axis=0
            )

        query = stacked(0)
        upstream = stacked(256)
        others = count_s[r]
        extra = lax.rem(others, GROUP)
        group_count = lax.div(others, GROUP)

        first_tiles = [r] + [
            jnp.where(u < extra, list_s[r, jnp.minimum(u, SLOTS - 1)], r) for u in range(GROUP - 1)
        ]

        def tiles_of(g):
            return [list_s[r, extra + g * GROUP + u] for u in range(GROUP)]

        def joined(ref, tiles, axis):
            return jnp.concatenate([ref[t] for t in tiles], axis=axis)

        scores = dot_nt(joined(k_s, first_tiles, 0), query) * SCORE_SCALE
        seen = jnp.concatenate(
            [causal] + [jnp.broadcast_to(u < extra, causal.shape) for u in range(GROUP - 1)], axis=0
        )
        scores = jnp.where(seen, scores, FLOOR)
        s_buf[0] = scores

        def score_group(g, top):
            scores = dot_nt(joined(k_s, tiles_of(g), 0), query) * SCORE_SCALE
            s_buf[g + 1] = scores
            return jnp.maximum(top, fold(scores, jnp.max))

        top = lax.fori_loop(0, group_count, score_group, fold(scores, jnp.max))
        top = jnp.max(top, axis=0, keepdims=True)

        def weigh(slot, tiles, carry):
            total, acc = carry
            weights = jnp.exp2(s_buf[slot] - top)
            s_buf[slot] = weights
            acc = acc + dot(joined(vt_s, tiles, 1), weights.astype(jnp.bfloat16))
            return total + fold(weights, jnp.sum), acc

        carry = (jnp.zeros((8, 2 * TILE), jnp.float32), jnp.zeros((HD, 2 * TILE), jnp.float32))
        carry = weigh(0, first_tiles, carry)
        total, acc = lax.fori_loop(0, group_count, lambda g, c: weigh(g + 1, tiles_of(g), c), carry)
        inverse = 1.0 / jnp.sum(total, axis=0, keepdims=True)
        attended_t = (acc * inverse).astype(jnp.bfloat16).astype(jnp.float32)
        up32 = upstream.astype(jnp.float32)
        upstream_t = jnp.concatenate([up32[:TILE].T, up32[TILE:].T], axis=1)
        delta = jnp.sum(attended_t * upstream_t, axis=0, keepdims=True)
        out_ref[r, :, 0:HD] = attended_t[:, :TILE].T.astype(jnp.bfloat16)
        out_ref[r, :, HD : 2 * HD] = attended_t[:, TILE:].T.astype(jnp.bfloat16)

        def gradients(slot, tiles, dq):
            probs = s_buf[slot] * inverse
            grad_probs = dot_nt(joined(v_s, tiles, 0), upstream)
            grad_scores = (probs * (grad_probs - delta)).astype(jnp.bfloat16)
            grad_value = dot(probs.astype(jnp.bfloat16), upstream)
            grad_key = dot(grad_scores, query)
            for u, t in enumerate(tiles):
                dv_s[t] += grad_value[u * TILE : (u + 1) * TILE]
                dk_s[t] += grad_key[u * TILE : (u + 1) * TILE]
            return dq + dot(joined(kt_s, tiles, 1), grad_scores)

        dq = gradients(0, first_tiles, jnp.zeros((HD, 2 * TILE), jnp.float32))
        dq = lax.fori_loop(0, group_count, lambda g, c: gradients(g + 1, tiles_of(g), c), dq)
        dq = dq * INV_ROOT
        out_ref[r, :, 256 : 256 + HD] = dq[:, :TILE].T.astype(jnp.bfloat16)
        out_ref[r, :, 256 + HD : 512] = dq[:, TILE:].T.astype(jnp.bfloat16)

    @pl.loop(0, BT)
    def _(t):
        out_ref[t, :, 512:640] = (dk_s[t] * INV_ROOT).astype(jnp.bfloat16)
        out_ref[t, :, 640:768] = dv_s[t].astype(jnp.bfloat16)

    @pl.loop(0, SLOTS - BT)
    def _(c):
        grad_key = (dk_s[BT + c] * INV_ROOT).astype(jnp.bfloat16)
        grad_value = dv_s[BT + c].astype(jnp.bfloat16)
        for s in range(SL):
            dfar_ref[0, s, c] = grad_key[s * 16 : (s + 1) * 16]
            dfar_ref[1, s, c] = grad_value[s * 16 : (s + 1) * 16]


VMEM = pl.BlockSpec(memory_space=pltpu.VMEM)
SMEM = pl.BlockSpec(memory_space=pltpu.SMEM)
ANY = pl.BlockSpec(memory_space=pl.ANY)


def attend(order, mask, rows, far):
    bf16, f32 = jnp.bfloat16, jnp.float32
    tiles = (SLOTS, TILE, HD)
    return pl.pallas_call(
        attend_kernel,
        out_shape=(
            jax.ShapeDtypeStruct((BT, TILE, 768), bf16),
            jax.ShapeDtypeStruct((2, SL, 24, 16, HD), bf16),
        ),
        in_specs=[SMEM, ANY, VMEM, VMEM],
        out_specs=(VMEM, VMEM),
        scratch_shapes=[
            pltpu.VMEM(tiles, bf16),
            pltpu.VMEM(tiles, bf16),
            pltpu.VMEM(tiles, bf16),
            pltpu.VMEM(tiles, bf16),
            pltpu.VMEM((SLOTS // GROUP + 1, GROUP * TILE, 2 * TILE), f32),
            pltpu.VMEM(tiles, f32),
            pltpu.VMEM(tiles, f32),
            pltpu.VMEM((HD, 2 * TILE), f32),
            pltpu.SMEM((BT, 128), jnp.int32),
            pltpu.SMEM((BT, SLOTS + 1), jnp.int32),
            pltpu.SMEM((BT,), jnp.int32),
            pltpu.SemaphoreType.DMA,
        ],
        compiler_params=pltpu.CompilerParams(vmem_limit_bytes=40 * 1024 * 1024),
        cost_estimate=pl.CostEstimate(flops=20_000_000_000, bytes_accessed=6_000_000, transcendentals=0),
    )(order, mask, rows, far)


def routed(kernel, order, array, out_shape):
    return pl.pallas_call(
        kernel,
        out_shape=jax.ShapeDtypeStruct(out_shape, jnp.bfloat16),
        in_specs=[SMEM, VMEM],
        out_specs=VMEM,
        scratch_shapes=[pltpu.SMEM((NB,), jnp.int32)],
        compiler_params=pltpu.CompilerParams(vmem_limit_bytes=16 * 1024 * 1024),
    )(order, array)


def swap(array, axis):
    return lax.all_to_all(array, axis, split_axis=0, concat_axis=0, tiled=True)


def on_device(queries, keys, values, upstream, tile_mask, tile_order):
    order = tile_order[0]
    mask = tile_mask[0]
    by_head = jnp.concatenate(
        [
            queries.reshape(TILE, 8, 256),
            upstream.reshape(TILE, 8, 256),
            jnp.repeat(keys.reshape(TILE, 4, HD), 2, axis=1),
            jnp.repeat(values.reshape(TILE, 4, HD), 2, axis=1),
        ],
        axis=2,
    ).transpose(1, 0, 2)
    rows = swap(by_head, "head")
    pair = rows[:, :, 512:].reshape(BT, SL, 16, 2, HD).transpose(3, 1, 0, 2, 4)
    pieces = swap(pair.reshape(NB, BT, 16, HD), "blk")
    chosen = routed(gather_kernel, order, pieces, (NB, 3, BT, 16, HD))
    far = swap(chosen, "blk").reshape(2, SL, 24, 16, HD)
    out, dfar = attend(order, mask, rows, far)
    parts = swap(dfar.reshape(NB, 3, BT, 16, HD), "blk")
    summed = routed(sum_kernel, order, parts, (NB, BT, 16, HD))
    home = swap(summed, "blk").reshape(2, SL, BT, 16, HD)
    home = home.transpose(2, 1, 3, 0, 4).reshape(BT, TILE, 256)
    pair_out = (out[:, :, 512:].astype(jnp.float32) + home.astype(jnp.float32)).astype(jnp.bfloat16)
    back = swap(jnp.concatenate([out[:, :, :512], pair_out], axis=2), "head")
    attended = back[:, :, :256].transpose(1, 0, 2).reshape(1, TILE, 2048)
    grad_queries = back[:, :, 256:512].transpose(1, 0, 2).reshape(1, TILE, 2048)
    grads = back[:, :, 512:].astype(jnp.float32).reshape(4, 2, TILE, 2, HD).sum(axis=1)
    grads = grads.astype(jnp.bfloat16).transpose(2, 1, 0, 3).reshape(2, 1, TILE, 512)
    return (attended, grad_queries, grads[0], grads[1])


def solution(mesh):
    split = P(None, ("blk", "head"), None)
    return jax.shard_map(
        on_device,
        mesh=mesh,
        in_specs=(split, split, split, split, P(), P()),
        out_specs=(split, split, split, split),
        check_vma=False,
    )
```

time: 971 us -> 220 us (0.23); the launches traced: 952 us -> 217 us
  waiting for transfers between devices: 342 us -> 11.3 us
  other arithmetic: 223 us -> 2.66 us
  starting transfers between devices: 179 us -> 4.53 us
  blocking collectives: 0 us -> 121 us
  matrix products: 85.1 us -> 0 us
  local copies, waits for them, and re-layouts: 87.5 us -> 14.4 us
  Pallas kernels: 0 us -> 62.8 us
  loops' own time: 33.3 us -> 0 us
    ppermute x61 -> x0, waiting for transfers between devices: 324 us -> none  [from_behind(): lax.ppermute(array, axis, [(i, (i + by) % length) for i in range(length)])]
    reduce_or x46 -> x0, other arithmetic: 181 us -> none  [guarded(): jnp.any(seen_mask)]
    ppermute x61 -> x0, starting transfers between devices: 146 us -> none  [from_behind(): lax.ppermute(array, axis, [(i, (i + by) % length) for i in range(length)])]
    all_to_all x0 -> x5, blocking collectives: none -> 121 us  [swap(): return lax.all_to_all(array, axis, split_axis=0, concat_axis=0, tiled=True)]
    dot_general x75 -> x0, matrix products: 85.1 us -> none  [the longest x4 23.8 us: compute_block(): jnp.einsum('shqk,skd->sqhd', weights, kv_block[1], preferred_element_type...]
    pallas_call x0 -> x3, Pallas kernels: none -> 62.8 us  [the longest x1 60.1 us: attend(): pl.pallas_call(attend_kernel, out_shape=(jax.ShapeDtypeStruct((BT, TILE,...]
    while x60 -> x0, local copies, waits for them, and re-layouts: 41.4 us -> none
    another operation x51 -> x0, loops' own time: 33.3 us -> none  [the longest x1 10.5 us: on_device(): lax.fori_loop(0, cycle_len - 1, stats_turn, (stats_init, kv_local[0]))]
  transfers between devices with their start and end apart: 68 -> 1, of which waited for: 47 -> 1; matrix products, arithmetic and copies ran while one was open for 28% -> 0% of each run, Pallas kernels for 0% -> 0%
where the time goes in v1:
time: 220 us; the launch traced here: 217 us
  blocking collectives  121 us (55%)
  Pallas kernels  62.8 us (29%)
  local copies, waits for them, and re-layouts  14.4 us (7%)
  waiting for transfers between devices  11.3 us (5%)
  starting transfers between devices  4.53 us (2%)
  other arithmetic  2.66 us (1%)
    all_to_all x5, blocking collectives, swap(): return lax.all_to_all(array, axis, split_axis=0, concat_axis=0, tiled=True)  121 us
    pallas_call x1, Pallas kernels, attend(): pl.pallas_call(attend_kernel, out_shape=(jax.ShapeDtypeStruct((BT, TILE,...  60.1 us
    all_to_all x1, waiting for transfers between devices, swap(): return lax.all_to_all(array, axis, split_axis=0, concat_axis=0, tiled=True)  11.3 us
    unnamed x12, local copies, waits for them, and re-layouts  5.17 us
    convert_element_type x2, local copies, waits for them, and re-layouts, on_device(): home.astype(jnp.float32)  4.87 us
    all_to_all x1, starting transfers between devices, swap(): return lax.all_to_all(array, axis, split_axis=0, concat_axis=0, tiled=True)  4.53 us
  transfers between devices with their start and end apart: 1, of which 1 were waited for; matrix products, arithmetic and copies ran while one was open for 0% of the time, Pallas kernels for 0%

profile of v1, /device:TPU:1, one launch (start us, length us, event | category | flops | bytes accessed | tf_op | source)
XLA Modules:
  0.0 217.1 jit_solution(8947683317871554579)
XLA Ops:
  0.6 1.0 reshape.63
  1.7 0.9 reshape.65
  2.6 1.3 copy.38
  4.0 0.2 copy.42
  4.2 0.3 copy.39
  4.5 0.2 copy.43
  4.8 0.1 maximum_bitcast_fusion
  4.9 26.6 %all_to_all.30.rows_ref = bf16[8,128,768]{2,1,0:T(8,128)(2,1)S(1)} all-to-all(bf16[8,128,768]{2,1,0:T(8,128)(2,1)S(1)} %maximum_bitcast_fusion), channel_id=1, replica_groups=mesh['blk'=16,'head'=8] {'head'}, dimensions={0} | all-to-all | bytes 3145728 | tf_op jit(solution)/shard_map/all_to_all | solution.py:257
  31.8 20.2 %all_to_all.31.pieces_ref = bf16[16,8,16,128]{3,2,1,0:T(8,128)(2,1)S(1)} all-to-all(bf16[16,8,16,128]{3,2,1,0:T(8,128)(2,1)S(1)} %bitcast.34), channel_id=1, replica_groups=mesh['blk'=16,'head'=8] {'blk'}, dimensions={0} | all-to-all | bytes 1048576 | tf_op jit(solution)/shard_map/all_to_all | solution.py:257
  52.0 0.8 shard_map.93
  52.8 26.4 %all_to_all.32 = bf16[16,3,8,16,128]{4,3,2,1,0:T(8,128)(2,1)S(1)} all-to-all(bf16[16,3,8,16,128]{4,3,2,1,0:T(8,128)(2,1)S(1)} %shard_map.93), channel_id=1, replica_groups=mesh['blk'=16,'head'=8] {'blk'}, dimensions={0} | all-to-all | bytes 3145728 | tf_op jit(solution)/shard_map/all_to_all | solution.py:257
  79.2 60.1 %shard_map.94 = (bf16[8,128,768]{2,1,0:T(8,128)(2,1)S(1)}, bf16[2,8,24,16,128]{4,3,2,1,0:T(8,128)(2,1)S(1)}) custom-call(s32[128]{0:T(128)S(1)} %bitcast.28, s32[128,128]{1,0:T(8,128)S(1)} %bitcast.30, bf16[8,128,768]{2,1,0:T(8,128)(2,1)S(1)} %all_to_all.30.rows_ref, bf16[2,8,24,16,128]{4,3,2,1,0:T(8,128)(2,1)S(1)} %bitcast.25), custom_call_target="tpu_custom_call" | custom-call | flops 20000000000 | bytes 6000000 | tf_op jit(solution)/shard_map/pallas_call | solution.py:218
  139.3 25.6 %all_to_all.33.parts_ref = bf16[16,3,8,16,128]{4,3,2,1,0:T(8,128)(2,1)S(1)} all-to-all(bf16[16,3,8,16,128]{4,3,2,1,0:T(8,128)(2,1)S(1)} %bitcast.26), channel_id=1, replica_groups=mesh['blk'=16,'head'=8] {'blk'}, dimensions={0} | all-to-all | bytes 3145728 | tf_op jit(solution)/shard_map/all_to_all | solution.py:257
  164.9 1.8 shard_map.95
  166.7 4.5 %all-to-all-start.4 = ((bf16[16,8,16,128]{3,2,1,0:T(8,128)(2,1)}), bf16[16,8,16,128]{3,2,1,0:T(8,128)(2,1)S(1)}, u32[]{:S(2)}, u32[]{:S(2)}) async-start(bf16[16,8,16,128]{3,2,1,0:T(8,128)(2,1)} %shard_map.95), calls=%async_computation.4 | async-start | bytes 1048576 | tf_op jit(solution)/shard_map/all_to_all | solution.py:257
  171.3 11.3 %all-to-all-done.4 = bf16[16,8,16,128]{3,2,1,0:T(8,128)(2,1)S(1)} async-done(((bf16[16,8,16,128]{3,2,1,0:T(8,128)(2,1)}), bf16[16,8,16,128]{3,2,1,0:T(8,128)(2,1)S(1)}, u32[]{:S(2)}, u32[]{:S(2)}) %all-to-all-start.4) | async-done | bytes 524320 | tf_op jit(solution)/shard_map/all_to_all | solution.py:257
  182.7 1.8 copy.45
  184.5 3.1 %reshape.75 = f32[8,128,256]{2,1,0:T(8,128)} reshape(f32[8,8,16,2,128]{4,3,2,1,0:T(2,128)} %copy.45) | data formatting | bytes 2097152 | tf_op jit(solution)/shard_map/convert_element_type | solution.py:282
  187.6 1.3 add_convert_fusion
  189.1 22.0 %all_to_all.34 = bf16[8,128,768]{2,1,0:T(8,128)(2,1)S(1)} all-to-all(bf16[8,128,768]{2,1,0:T(8,128)(2,1)S(1)} %pad_maximum_fusion), channel_id=1, replica_groups=mesh['blk'=16,'head'=8] {'head'}, dimensions={0} | all-to-all | bytes 3145728 | tf_op jit(solution)/shard_map/all_to_all | solution.py:257
  211.0 0.2 fusion
  211.2 0.1 reshape.73
  211.4 1.0 reduce
  212.3 0.4 fusion.1
  212.7 0.1 copy.49
  212.9 0.8 copy.53
  213.6 0.1 copy.48
  213.8 0.8 copy.52
  214.6 0.3 copy.47
  214.8 1.0 copy.51
  215.9 0.3 copy.46
  216.1 1.0 copy.50
  (16 shorter events, 0.7 us)
Async XLA Ops:
  0.6 3.6 %copy-start.2 = (bf16[1,128,2048]{2,1,0:T(8,128)(2,1)S(1)}, bf16[1,128,2048]{2,1,0:T(8,128)(2,1)}, u32[]{:S(2)}) copy-start(bf16[1,128,2048]{2,1,0:T(8,128)(2,1)} %param.9) | copy-start | bytes 1572868
  31.5 20.4 %copy-start = (s32[1,128]{1,0:T(1,128)S(1)}, s32[1,128]{1,0:T(1,128)}, u32[]{:S(2)}) copy-start(s32[1,128]{1,0:T(1,128)} %param.11) | copy-start | bytes 1540
  52.8 26.4 %copy-start.1 = (s32[1,128,128]{2,1,0:T(8,128)S(1)}, s32[1,128,128]{2,1,0:T(8,128)}, u32[]{:S(2)}) copy-start(s32[1,128,128]{2,1,0:T(8,128)} %param.10) | copy-start | bytes 196612
  166.7 15.9 %all-to-all-start.4 = ((bf16[16,8,16,128]{3,2,1,0:T(8,128)(2,1)}), bf16[16,8,16,128]{3,2,1,0:T(8,128)(2,1)S(1)}, u32[]{:S(2)}, u32[]{:S(2)}) async-start(bf16[16,8,16,128]{3,2,1,0:T(8,128)(2,1)} %shard_map.95), calls=%async_computation.4 | async-start | bytes 1048576 | tf_op jit(solution)/shard_map/all_to_all | solution.py:257

commit v2 on v1

v2 whole, which is shorter than its diff:
```python
import math

import jax
import jax.numpy as jnp
from jax import lax
from jax.experimental import pallas as pl
from jax.experimental.pallas import tpu as pltpu
from jax.sharding import PartitionSpec as P

HD = 128
TILE = 128
WIDE = 256
BT = 8
NB = 16
FAR = 24
WORK = 8
REST = 4
INV_ROOT = 1.0 / math.sqrt(HD)
SCORE_SCALE = INV_ROOT * math.log2(math.e)
FLOOR = -1e30

OWN_COUNT, FAR_COUNT, OWN_LIST, FAR_LIST, PLAN = 0, 1, 8, 16, 64

NT = (((1,), (1,)), ((), ()))


def dot(a, b):
    return jnp.dot(a, b, preferred_element_type=jnp.float32)


def dot_nt(a, b):
    return lax.dot_general(a, b, NT, preferred_element_type=jnp.float32)


def block_of(order_ref, index):
    return lax.shift_right_logical(order_ref[index * BT], 3)


def invert_blocks(order_ref, where_ref):
    for k in range(NB):
        where_ref[block_of(order_ref, k)] = k


def pack_kernel(q_ref, d_ref, k_ref, v_ref, out_ref):
    for u in range(2):
        cols = slice(u * WIDE, (u + 1) * WIDE)
        out_ref[u, :, 0:256] = q_ref[:, cols]
        out_ref[u, :, 256:512] = d_ref[:, cols]
        out_ref[u, :, 512:640] = k_ref[...]
        out_ref[u, :, 640:768] = v_ref[...]


def unpack_kernel(back_ref, o_ref, dq_ref, dk_ref, dv_ref):
    for u in range(2):
        cols = slice(u * WIDE, (u + 1) * WIDE)
        o_ref[:, cols] = back_ref[u, :, 0:256]
        dq_ref[:, cols] = back_ref[u, :, 256:512]

    def both(lo):
        a = back_ref[0, :, lo : lo + HD].astype(jnp.float32)
        return (a + back_ref[1, :, lo : lo + HD].astype(jnp.float32)).astype(jnp.bfloat16)

    dk_ref[...] = both(512)
    dv_ref[...] = both(640)


def add_kernel(pair_ref, home_ref, out_ref):
    for part in range(2):
        cols = slice(part * HD, (part + 1) * HD)
        own = pair_ref[:, :, cols].astype(jnp.float32)
        out_ref[:, :, cols] = (own + home_ref[part].astype(jnp.float32)).astype(jnp.bfloat16)


def gather_kernel(order_ref, pieces_ref, out_ref, where_ref):
    invert_blocks(order_ref, where_ref)

    @pl.loop(0, NB)
    def _(k):
        b = block_of(order_ref, k)
        for j in range(3):
            src = jnp.maximum(b - 1 - j, 0) if j < 2 else 0
            out_ref[k, j] = pieces_ref[where_ref[src]]


def sum_kernel(order_ref, parts_ref, out_ref, where_ref):
    invert_blocks(order_ref, where_ref)

    @pl.loop(0, NB)
    def _(k):
        b = block_of(order_ref, k)
        near = parts_ref[where_ref[jnp.minimum(b + 1, NB - 1)], 0].astype(jnp.float32)
        far = parts_ref[where_ref[jnp.minimum(b + 2, NB - 1)], 1].astype(jnp.float32)
        total = jnp.where(b + 1 < NB, near, 0.0) + jnp.where(b + 2 < NB, far, 0.0)
        out_ref[k] = total.astype(jnp.bfloat16)

    total = parts_ref[where_ref[1], 0].astype(jnp.float32)
    total = total + parts_ref[where_ref[2], 1].astype(jnp.float32)
    for b in range(3, NB):
        total = total + parts_ref[where_ref[b], 2].astype(jnp.float32)
    out_ref[where_ref[0]] = total.astype(jnp.bfloat16)


def fold(x, op):
    return op(x.reshape(-1, 8, WIDE), axis=0)


def spread(x):
    return jnp.broadcast_to(x, (8, WIDE))


def joined(refs, axis):
    return jnp.concatenate(refs, axis=axis)


def stacked(rows_ref, r, lo):
    return joined([rows_ref[r, :, lo : lo + HD], rows_ref[r, :, lo + HD : lo + 2 * HD]], 0)


def own_seen(count):
    k_pos = lax.broadcasted_iota(jnp.int32, (BT * TILE, WIDE), 0)
    q_pos = lax.broadcasted_iota(jnp.int32, (BT * TILE, WIDE), 1) % TILE
    limit = jnp.where(k_pos < TILE, q_pos + 1, (count + 1) * TILE)
    return k_pos < limit


def own_tiles(plan_ref, r):
    count = plan_ref[r, OWN_COUNT]
    rest = [jnp.where(u < count, plan_ref[r, OWN_LIST + u], r) for u in range(BT - 1)]
    return count, [r] + rest


def near_kernel(order_ref, mask_ref, rows_ref, plan_ref, top_ref, total_ref, acc_ref, upt_ref, vt_s, mask_s, sem):
    b = block_of(order_ref, lax.axis_index("blk"))
    copy = pltpu.make_async_copy(mask_ref.at[pl.ds(pl.multiple_of(b * BT, BT), BT)], mask_s, sem)
    copy.start()

    @pl.loop(0, BT)
    def _(t):
        vt_s[t] = rows_ref[t, :, 640:768].T

    copy.wait()

    @pl.loop(0, BT)
    def _(r):
        own = jnp.int32(0)
        for t in range(BT - 1):
            plan_ref[r, OWN_LIST + own] = t
            own = own + ((mask_s[r, b * BT + t] == 1) & (t < r)).astype(jnp.int32)
        plan_ref[r, OWN_COUNT] = own
        far = jnp.int32(0)
        for t in range(BT):
            for j in range(3):
                column = jnp.maximum(b - 1 - j, 0) * BT + t if j < 2 else t
                plan_ref[r, FAR_LIST + far] = t * 3 + j
                far = far + ((mask_s[r, column] == 1) & (b > j)).astype(jnp.int32)
        plan_ref[r, FAR_COUNT] = far

    @pl.loop(0, BT)
    def _(r):
        query = stacked(rows_ref, r, 0)
        count, tiles = own_tiles(plan_ref, r)
        scores = dot_nt(joined([rows_ref[t, :, 512:640] for t in tiles], 0), query) * SCORE_SCALE
        scores = jnp.where(own_seen(count), scores, FLOOR)
        top = jnp.max(fold(scores, jnp.max), axis=0, keepdims=True)
        weights = jnp.exp2(scores - top)
        top_ref[r] = spread(top)
        total_ref[r] = fold(weights, jnp.sum)
        acc_ref[r] = dot(joined([vt_s[t] for t in tiles], 1), weights.astype(jnp.bfloat16))
        upt_ref[r] = joined([rows_ref[r, :, 256:384].T, rows_ref[r, :, 384:512].T], 1)


def far_steps(plan_ref, r, step):
    count = plan_ref[r, FAR_COUNT]
    whole = lax.shift_right_logical(count, 3)
    rest = count & (WORK - 1)

    @pl.loop(0, whole)
    def _(g):
        step(g * WORK, [plan_ref[r, FAR_LIST + g * WORK + u] for u in range(WORK)], None)

    def partly(width):
        base = whole * WORK
        tiles = [
            jnp.where(u < rest, plan_ref[r, FAR_LIST + jnp.minimum(base + u, FAR - 1)], 0)
            for u in range(width)
        ]
        step(base, tiles, rest)

    @pl.when(rest > REST)
    def _():
        partly(WORK)

    @pl.when((rest > 0) & (rest <= REST))
    def _():
        partly(REST)


def only(scores, live):
    if live is None:
        return scores
    row = lax.broadcasted_iota(jnp.int32, scores.shape, 0)
    return jnp.where(row < live * TILE, scores, FLOOR)


def far_kernel(
    plan_ref, rows_ref, far_ref, top_ref, total_ref, acc_ref, upt_ref,
    dfar_ref, ot_ref, lse_ref, delta_ref,
    vt_s, s_buf, dk_s, dv_s, top_s, total_s, acc_s,
):
    dk_s[...] = jnp.zeros_like(dk_s)
    dv_s[...] = jnp.zeros_like(dv_s)

    @pl.loop(0, FAR, unroll=4)
    def _(c):
        vt_s[c] = far_ref[1, c].T

    @pl.loop(0, BT)
    def _(r):
        query = stacked(rows_ref, r, 0)
        upstream = stacked(rows_ref, r, 256)
        top_s[...] = top_ref[r]

        def score(slot, tiles, live):
            width = len(tiles)
            scores = dot_nt(joined([far_ref[0, t] for t in tiles], 0), query) * SCORE_SCALE
            scores = only(scores, live)
            s_buf[pl.ds(slot, width)] = scores.reshape(width, TILE, WIDE)
            top_s[...] = jnp.maximum(top_s[...], fold(scores, jnp.max))

        far_steps(plan_ref, r, score)
        near_top = top_ref[r][:1]
        top = jnp.max(top_s[...], axis=0, keepdims=True)
        shrink = jnp.exp2(near_top - top)
        total_s[...] = total_ref[r] * shrink
        acc_s[...] = acc_ref[r] * shrink

        def weigh(slot, tiles, live):
            width = len(tiles)
            weights = jnp.exp2(s_buf[pl.ds(slot, width)].reshape(width * TILE, WIDE) - top)
            s_buf[pl.ds(slot, width)] = weights.reshape(width, TILE, WIDE)
            total_s[...] += fold(weights, jnp.sum)
            acc_s[...] += dot(joined([vt_s[t] for t in tiles], 1), weights.astype(jnp.bfloat16))

        far_steps(plan_ref, r, weigh)
        total = jnp.sum(total_s[...], axis=0, keepdims=True)
        inverse = 1.0 / total
        attended = (acc_s[...] * inverse).astype(jnp.bfloat16)
        ot_ref[r] = attended
        delta = attended.astype(jnp.float32) * upt_ref[r].astype(jnp.float32)
        delta = jnp.sum(fold(delta, jnp.sum), axis=0, keepdims=True)
        lse_ref[r] = spread(top + jnp.log2(total))
        delta_ref[r] = spread(delta)

        def gradients(slot, tiles, live):
            width = len(tiles)
            probs = s_buf[pl.ds(slot, width)].reshape(width * TILE, WIDE) * inverse
            grad_probs = dot_nt(joined([far_ref[1, t] for t in tiles], 0), upstream)
            grad_scores = (probs * (grad_probs - delta)).astype(jnp.bfloat16)
            grad_value = dot(probs.astype(jnp.bfloat16), upstream)
            grad_key = dot(grad_scores, query)
            for u, t in enumerate(tiles):
                dv_s[t] += grad_value[u * TILE : (u + 1) * TILE]
                dk_s[t] += grad_key[u * TILE : (u + 1) * TILE]

        far_steps(plan_ref, r, gradients)

    dfar_ref[0] = (dk_s[...] * INV_ROOT).astype(jnp.bfloat16)
    dfar_ref[1] = dv_s[...].astype(jnp.bfloat16)


def rest_kernel(
    plan_ref, rows_ref, far_ref, ot_ref, lse_ref, delta_ref, out_ref,
    kt_s, fkt_s, dk_s, dv_s, dq_s,
):
    dk_s[...] = jnp.zeros_like(dk_s)
    dv_s[...] = jnp.zeros_like(dv_s)

    @pl.loop(0, BT)
    def _(t):
        kt_s[t] = rows_ref[t, :, 512:640].T

    @pl.loop(0, FAR, unroll=4)
    def _(c):
        fkt_s[c] = far_ref[0, c].T

    @pl.loop(0, BT)
    def _(r):
        query = stacked(rows_ref, r, 0)
        upstream = stacked(rows_ref, r, 256)
        lse = lse_ref[r][:1]
        delta = delta_ref[r][:1]
        attended = ot_ref[r].astype(jnp.float32)
        out_ref[r, :, 0:HD] = attended[:, :TILE].T.astype(jnp.bfloat16)
        out_ref[r, :, HD : 2 * HD] = attended[:, TILE:].T.astype(jnp.bfloat16)

        def common(scores, value):
            probs = jnp.exp2(scores - lse)
            grad_probs = dot_nt(value, upstream)
            return probs, (probs * (grad_probs - delta)).astype(jnp.bfloat16)

        count, tiles = own_tiles(plan_ref, r)
        scores = dot_nt(joined([rows_ref[t, :, 512:640] for t in tiles], 0), query) * SCORE_SCALE
        scores = jnp.where(own_seen(count), scores, FLOOR)
        probs, grad_scores = common(scores, joined([rows_ref[t, :, 640:768] for t in tiles], 0))
        grad_value = dot(probs.astype(jnp.bfloat16), upstream)
        grad_key = dot(grad_scores, query)
        for u, t in enumerate(tiles):
            dv_s[t] += grad_value[u * TILE : (u + 1) * TILE]
            dk_s[t] += grad_key[u * TILE : (u + 1) * TILE]
        dq_s[...] = dot(joined([kt_s[t] for t in tiles], 1), grad_scores)

        def queries(slot, tiles, live):
            scores = dot_nt(joined([far_ref[0, t] for t in tiles], 0), query) * SCORE_SCALE
            _, grad_scores = common(only(scores, live), joined([far_ref[1, t] for t in tiles], 0))
            dq_s[...] += dot(joined([fkt_s[t] for t in tiles], 1), grad_scores)

        far_steps(plan_ref, r, queries)
        dq = dq_s[...] * INV_ROOT
        out_ref[r, :, 256 : 256 + HD] = dq[:, :TILE].T.astype(jnp.bfloat16)
        out_ref[r, :, 256 + HD : 512] = dq[:, TILE:].T.astype(jnp.bfloat16)

    @pl.loop(0, BT)
    def _(t):
        out_ref[t, :, 512:640] = (dk_s[t] * INV_ROOT).astype(jnp.bfloat16)
        out_ref[t, :, 640:768] = dv_s[t].astype(jnp.bfloat16)


VMEM = pl.BlockSpec(memory_space=pltpu.VMEM)
SMEM = pl.BlockSpec(memory_space=pltpu.SMEM)
ANY = pl.BlockSpec(memory_space=pl.ANY)
BF16, F32 = jnp.bfloat16, jnp.float32


def shape(dims, dtype):
    return jax.ShapeDtypeStruct(dims, dtype)


def limit(mib):
    return pltpu.CompilerParams(vmem_limit_bytes=mib * 1024 * 1024)


def cost(us):
    return pl.CostEstimate(flops=us * 1_000_000_000, bytes_accessed=us * 100_000, transcendentals=0)


def pack(queries, upstream, keys, values):
    wide = pl.BlockSpec((TILE, 512), lambda g: (0, g))
    slim = pl.BlockSpec((TILE, HD), lambda g: (0, g))
    return pl.pallas_call(
        pack_kernel,
        grid=(4,),
        out_shape=shape((8, TILE, 768), BF16),
        in_specs=[wide, wide, slim, slim],
        out_specs=pl.BlockSpec((2, TILE, 768), lambda g: (g, 0, 0)),
    )(queries, upstream, keys, values)


def unpack(back):
    wide = pl.BlockSpec((TILE, 512), lambda g: (0, g))
    slim = pl.BlockSpec((TILE, HD), lambda g: (0, g))
    return pl.pallas_call(
        unpack_kernel,
        grid=(4,),
        out_shape=(shape((TILE, 2048), BF16),) * 2 + (shape((TILE, 512), BF16),) * 2,
        in_specs=[pl.BlockSpec((2, TILE, 768), lambda g: (g, 0, 0))],
        out_specs=(wide, wide, slim, slim),
    )(back)


def add_home(out, home):
    pair = pl.BlockSpec((BT, TILE, 256), lambda g: (0, 0, 2))
    return pl.pallas_call(
        add_kernel,
        grid=(1,),
        out_shape=shape((BT, TILE, 768), BF16),
        in_specs=[pair, pl.BlockSpec((2, BT, TILE, HD), lambda g: (0, 0, 0, 0))],
        out_specs=pair,
        input_output_aliases={0: 0},
    )(out, home)


def near(order, mask, rows):
    return pl.pallas_call(
        near_kernel,
        out_shape=(
            shape((BT, PLAN), jnp.int32),
            shape((BT, 8, WIDE), F32),
            shape((BT, 8, WIDE), F32),
            shape((BT, HD, WIDE), F32),
            shape((BT, HD, WIDE), BF16),
        ),
        in_specs=[SMEM, ANY, VMEM],
        out_specs=(SMEM, VMEM, VMEM, VMEM, VMEM),
        scratch_shapes=[
            pltpu.VMEM((BT, HD, TILE), BF16),
            pltpu.SMEM((BT, 128), jnp.int32),
            pltpu.SemaphoreType.DMA,
        ],
        compiler_params=limit(32),
        cost_estimate=cost(12),
    )(order, mask, rows)


def far_part(plan, rows, far, top, total, acc, upt):
    return pl.pallas_call(
        far_kernel,
        out_shape=(
            shape((2, FAR, TILE, HD), BF16),
            shape((BT, HD, WIDE), BF16),
            shape((BT, 8, WIDE), F32),
            shape((BT, 8, WIDE), F32),
        ),
        in_specs=[SMEM] + [VMEM] * 6,
        out_specs=(VMEM,) * 4,
        scratch_shapes=[
            pltpu.VMEM((FAR, HD, TILE), BF16),
            pltpu.VMEM((FAR, TILE, WIDE), F32),
            pltpu.VMEM((FAR, TILE, HD), F32),
            pltpu.VMEM((FAR, TILE, HD), F32),
            pltpu.VMEM((8, WIDE), F32),
            pltpu.VMEM((8, WIDE), F32),
            pltpu.VMEM((HD, WIDE), F32),
        ],
        compiler_params=limit(40),
        cost_estimate=cost(25),
    )(plan, rows, far, top, total, acc, upt)


def rest_part(plan, rows, far, ot, lse, delta):
    return pl.pallas_call(
        rest_kernel,
        out_shape=shape((BT, TILE, 768), BF16),
        in_specs=[SMEM] + [VMEM] * 5,
        out_specs=VMEM,
        scratch_shapes=[
            pltpu.VMEM((BT, HD, TILE), BF16),
            pltpu.VMEM((FAR, HD, TILE), BF16),
            pltpu.VMEM((BT, TILE, HD), F32),
            pltpu.VMEM((BT, TILE, HD), F32),
            pltpu.VMEM((HD, WIDE), F32),
        ],
        compiler_params=limit(40),
        cost_estimate=cost(25),
    )(plan, rows, far, ot, lse, delta)


def routed(kernel, order, array, out_shape):
    return pl.pallas_call(
        kernel,
        out_shape=shape(out_shape, BF16),
        in_specs=[SMEM, VMEM],
        out_specs=VMEM,
        scratch_shapes=[pltpu.SMEM((NB,), jnp.int32)],
        compiler_params=limit(16),
    )(order, array)


def swap(array, axis):
    return lax.all_to_all(array, axis, split_axis=0, concat_axis=0, tiled=True)


def on_device(queries, keys, values, upstream, tile_mask, tile_order):
    order = tile_order[0]
    rows = swap(pack(queries[0], upstream[0], keys[0], values[0]), "head")
    pair = rows[:, :, 512:].reshape(BT, TILE, 2, HD).transpose(2, 0, 1, 3)
    pieces = swap(pair.reshape(NB, TILE, HD), "blk")
    chosen = routed(gather_kernel, order, pieces, (NB, 3, TILE, HD))
    far = swap(chosen, "blk").reshape(2, FAR, TILE, HD)
    plan, top, total, acc, upt = near(order, tile_mask[0], rows)
    dfar, ot, lse, delta = far_part(plan, rows, far, top, total, acc, upt)
    parts = swap(dfar.reshape(NB, 3, TILE, HD), "blk")
    out = rest_part(plan, rows, far, ot, lse, delta)
    parts, out = lax.optimization_barrier((parts, out))
    summed = routed(sum_kernel, order, parts, (NB, TILE, HD))
    home = swap(summed, "blk").reshape(2, BT, TILE, HD)
    back = swap(add_home(out, home), "head")
    return tuple(array[None] for array in unpack(back))


def solution(mesh):
    split = P(None, ("blk", "head"), None)
    return jax.shard_map(
        on_device,
        mesh=mesh,
        in_specs=(split, split, split, split, P(), P()),
        out_specs=(split, split, split, split),
        check_vma=False,
    )
```

time: 220 us -> 187 us (0.85)
  blocking collectives: 121 us -> 89.9 us
  starting transfers between devices: 4.53 us -> 11.1 us
  local copies, waits for them, and re-layouts: 14.4 us -> 10.4 us
  other arithmetic: 2.66 us -> 0 us
    all_to_all x5 -> x4, blocking collectives: 121 us -> 89.9 us  [swap(): return lax.all_to_all(array, axis, split_axis=0, concat_axis=0, tiled=True)]
    all_to_all x1 -> x2, starting transfers between devices: 4.53 us -> 11.1 us  [swap(): return lax.all_to_all(array, axis, split_axis=0, concat_axis=0, tiled=True)]
    unnamed x12 -> x24, local copies, waits for them, and re-layouts: 5.17 us -> 10.2 us
    convert_element_type x2 -> x0, local copies, waits for them, and re-layouts: 4.87 us -> none  [on_device(): home.astype(jnp.float32)]
    reshape x8 -> x1, local copies, waits for them, and re-layouts: 2.67 us -> 0.12 us  [on_device(): pair = rows[:, :, 512:].reshape(BT, TILE, 2, HD).transpose(2, 0, 1, 3)]
    pallas_call x3 -> x8, Pallas kernels: 62.8 us -> 61.1 us  [the longest x1 20.7 us: far_part(): pl.pallas_call(far_kernel, out_shape=(shape((2, FAR, TILE, HD), BF16), sh...]
    all_to_all x1 -> x2, waiting for transfers between devices: 11.3 us -> 12.3 us  [swap(): return lax.all_to_all(array, axis, split_axis=0, concat_axis=0, tiled=True)]
  transfers between devices with their start and end apart: 1 -> 2, of which waited for: 1 -> 2; matrix products, arithmetic and copies ran while one was open for 0% -> 0% of each run, Pallas kernels for 0% -> 15%
where the time goes in v2:
time: 187 us; the launch traced here: 186 us
  blocking collectives  89.9 us (48%)
  Pallas kernels  61.1 us (33%)
  waiting for transfers between devices  12.3 us (7%)
  starting transfers between devices  11.1 us (6%)
  local copies, waits for them, and re-layouts  10.4 us (6%)
    all_to_all x4, blocking collectives, swap(): return lax.all_to_all(array, axis, split_axis=0, concat_axis=0, tiled=True)  89.9 us
    pallas_call x1, Pallas kernels, far_part(): pl.pallas_call(far_kernel, out_shape=(shape((2, FAR, TILE, HD), BF16), sh...  20.7 us
    pallas_call x1, Pallas kernels, rest_part(): pl.pallas_call(rest_kernel, out_shape=shape((BT, TILE, 768), BF16), in_sp...  19.2 us
    all_to_all x2, waiting for transfers between devices, swap(): return lax.all_to_all(array, axis, split_axis=0, concat_axis=0, tiled=True)  12.3 us
    all_to_all x2, starting transfers between devices, swap(): return lax.all_to_all(array, axis, split_axis=0, concat_axis=0, tiled=True)  11.1 us
    unnamed x24, local copies, waits for them, and re-layouts  10.2 us
    pallas_call x1, Pallas kernels, near(): pl.pallas_call(near_kernel, out_shape=(shape((BT, PLAN), jnp.int32), shap...  8.93 us
  transfers between devices with their start and end apart: 2, of which 2 were waited for; matrix products, arithmetic and copies ran while one was open for 0% of the time, Pallas kernels for 15%

profile of v2, /device:TPU:1, one launch (start us, length us, event | category | flops | bytes accessed | tf_op | source)
XLA Modules:
  0.0 185.6 jit_solution(8693737293058292108)
XLA Ops:
  0.6 3.6 %shard_map.93 = bf16[8,128,768]{2,1,0:T(8,128)(2,1)} custom-call(bf16[128,2048]{1,0:T(8,128)(2,1)} %bitcast.25, bf16[128,2048]{1,0:T(8,128)(2,1)} %bitcast.26, bf16[128,512]{1,0:T(8,128)(2,1)} %bitcast.27, bf16[128,512]{1,0:T(8,128)(2,1)} %bitcast.28), custom_call_target="tpu_custom_call" | custom-call | tf_op jit(solution)/shard_map/pallas_call | solution.py:349
  4.2 26.8 %all_to_all.30.rows_ref = bf16[8,128,768]{2,1,0:T(8,128)(2,1)S(1)} all-to-all(bf16[8,128,768]{2,1,0:T(8,128)(2,1)} %shard_map.93), channel_id=1, replica_groups=mesh['blk'=16,'head'=8] {'head'}, dimensions={0} | all-to-all | bytes 3145728 | tf_op jit(solution)/shard_map/all_to_all | solution.py:459
  31.0 0.0 copy-start.4
  31.0 0.1 reshape.23
  31.1 0.1 copy.11
  31.2 20.2 %all_to_all.31.pieces_ref = bf16[16,128,128]{2,1,0:T(8,128)(2,1)S(1)} all-to-all(bf16[16,128,128]{2,1,0:T(8,128)(2,1)S(1)} %bitcast.24), channel_id=1, replica_groups=mesh['blk'=16,'head'=8] {'blk'}, dimensions={0} | all-to-all | bytes 1048576 | tf_op jit(solution)/shard_map/all_to_all | solution.py:459
  51.4 0.0 copy-done.4
  51.4 2.0 %shard_map.95 = bf16[16,3,128,128]{3,2,1,0:T(8,128)(2,1)} custom-call(s32[128]{0:T(128)S(1)} %bitcast.18, bf16[16,128,128]{2,1,0:T(8,128)(2,1)S(1)} %all_to_all.31.pieces_ref), custom_call_target="tpu_custom_call" | custom-call | tf_op jit(solution)/shard_map/pallas_call | solution.py:448
  53.4 4.8 %all-to-all-start.2 = ((bf16[16,3,128,128]{3,2,1,0:T(8,128)(2,1)}), bf16[16,3,128,128]{3,2,1,0:T(8,128)(2,1)S(1)}, u32[]{:S(2)}, u32[]{:S(2)}) async-start(bf16[16,3,128,128]{3,2,1,0:T(8,128)(2,1)} %shard_map.95), calls=%async_computation.2 | async-start | bytes 3145728 | tf_op jit(solution)/shard_map/all_to_all | solution.py:459
  58.2 0.0 copy-done.5
  58.2 8.9 %shard_map.94 = (s32[8,64]{1,0:T(8,128)S(1)}, f32[8,8,256]{2,1,0:T(8,128)S(1)}, f32[8,8,256]{2,1,0:T(8,128)S(1)}, f32[8,128,256]{2,1,0:T(8,128)S(1)}, bf16[8,128,256]{2,1,0:T(8,128)(2,1)S(1)}) custom-call(s32[128]{0:T(128)S(1)} %bitcast.19, s32[128,128]{1,0:T(8,128)S(1)} %bitcast.21, bf16[8,128,768]{2,1,0:T(8,128)(2,1)S(1)} %all_to_all.30.rows_ref), custom_call_target="tpu_custom_call" | custom-call | flops 12000000000 | bytes 1200000 | tf_op jit(solution)/shard_map/pallas_call | solution.py:383
  67.2 0.0 copy-start.6
  67.2 1.0 copy-done.6
  68.2 0.8 copy-done.8
  69.0 12.2 %all-to-all-done.2 = bf16[16,3,128,128]{3,2,1,0:T(8,128)(2,1)S(1)} async-done(((bf16[16,3,128,128]{3,2,1,0:T(8,128)(2,1)}), bf16[16,3,128,128]{3,2,1,0:T(8,128)(2,1)S(1)}, u32[]{:S(2)}, u32[]{:S(2)}) %all-to-all-start.2) | async-done | bytes 1572896 | tf_op jit(solution)/shard_map/all_to_all | solution.py:459
  81.2 1.8 copy-done.7
  83.0 1.0 copy-done.9
  84.0 20.7 %shard_map.96 = (bf16[2,24,128,128]{3,2,1,0:T(8,128)(2,1)S(1)}, bf16[8,128,256]{2,1,0:T(8,128)(2,1)S(1)}, f32[8,8,256]{2,1,0:T(8,128)S(1)}, f32[8,8,256]{2,1,0:T(8,128)S(1)}) custom-call(s32[8,64]{1,0:T(8,128)S(1)} %get-tuple-element.19.plan_ref, bf16[8,128,768]{2,1,0:T(8,128)(2,1)S(1)} %all_to_all.30.rows_ref, bf16[2,24,128,128]{3,2,1,0:T(8,128)(2,1)S(1)} %bitcast.15, ...), custom_call_target="tpu_custom_call" | custom-call | flops 24999999488 | bytes 2500000 | tf_op jit(solution)/shard_map/pallas_call | solution.py:405
  104.7 1.1 copy-done.3
  105.9 0.8 copy-done.10
  106.6 6.3 %all-to-all-start.3 = ((bf16[16,3,128,128]{3,2,1,0:T(8,128)(2,1)}), bf16[16,3,128,128]{3,2,1,0:T(8,128)(2,1)S(1)}, u32[]{:S(2)}, u32[]{:S(2)}) async-start(bf16[16,3,128,128]{3,2,1,0:T(8,128)(2,1)} %bitcast.17), calls=%async_computation.3 | async-start | bytes 3145728 | tf_op jit(solution)/shard_map/all_to_all | solution.py:459
  113.0 1.4 copy-done.2
  114.4 1.0 copy-done.11
  115.4 19.2 %shard_map.97.pair_ref = bf16[8,128,768]{2,1,0:T(8,128)(2,1)S(1)} custom-call(s32[8,64]{1,0:T(8,128)S(1)} %get-tuple-element.19.plan_ref, bf16[8,128,768]{2,1,0:T(8,128)(2,1)S(1)} %all_to_all.30.rows_ref, bf16[2,24,128,128]{3,2,1,0:T(8,128)(2,1)S(1)} %bitcast.16, bf16[8,128,256]{2,1,0:T(8,128)(2,1)S(1)} %copy-done.11, ...), custom_call_target="tpu_custom_call" | custom-call | flops 24999999488 | bytes 2500000 | tf_op jit(solution)/shard_map/pallas_call | solution.py:430
  134.6 0.0 copy-start
  134.6 1.2 copy-done
  135.8 0.1 all-to-all-done.3.parts_ref
  135.9 1.1 shard_map.98
  137.0 19.1 %all_to_all.32 = bf16[16,128,128]{2,1,0:T(8,128)(2,1)} all-to-all(bf16[16,128,128]{2,1,0:T(8,128)(2,1)S(1)} %shard_map.98), channel_id=1, replica_groups=mesh['blk'=16,'head'=8] {'blk'}, dimensions={0} | all-to-all | bytes 1048576 | tf_op jit(solution)/shard_map/all_to_all | solution.py:459
  156.1 2.2 %shard_map.99 = bf16[8,128,768]{2,1,0:T(8,128)(2,1)} custom-call(bf16[8,128,768]{2,1,0:T(8,128)(2,1)} %copy-done, bf16[2,8,128,128]{3,2,1,0:T(8,128)(2,1)} %bitcast.22), custom_call_target="tpu_custom_call", output_to_operand_aliasing={{}: (0, {})} | custom-call | tf_op jit(solution)/shard_map/pallas_call | solution.py:372
  158.3 23.8 %all_to_all.33.back_ref = bf16[8,128,768]{2,1,0:T(8,128)(2,1)} all-to-all(bf16[8,128,768]{2,1,0:T(8,128)(2,1)} %shard_map.99), channel_id=1, replica_groups=mesh['blk'=16,'head'=8] {'head'}, dimensions={0} | all-to-all | bytes 3145728 | tf_op jit(solution)/shard_map/all_to_all | solution.py:459
  182.1 3.5 %shard_map.100 = (bf16[128,2048]{1,0:T(8,128)(2,1)}, bf16[128,2048]{1,0:T(8,128)(2,1)}, bf16[128,512]{1,0:T(8,128)(2,1)}, bf16[128,512]{1,0:T(8,128)(2,1)}) custom-call(bf16[8,128,768]{2,1,0:T(8,128)(2,1)} %all_to_all.33.back_ref), custom_call_target="tpu_custom_call" | custom-call | tf_op jit(solution)/shard_map/pallas_call | solution.py:361
  (11 shorter events, 0.1 us)
Async XLA Ops:
  31.0 20.4 %copy-start.4 = (s32[1,128]{1,0:T(1,128)S(1)}, s32[1,128]{1,0:T(1,128)}, u32[]{:S(2)}) copy-start(s32[1,128]{1,0:T(1,128)} %param.11) | copy-start | bytes 1540
  53.4 4.8 %copy-start.5 = (s32[1,128,128]{2,1,0:T(8,128)S(1)}, s32[1,128,128]{2,1,0:T(8,128)}, u32[]{:S(2)}) copy-start(s32[1,128,128]{2,1,0:T(8,128)} %param.10) | copy-start | bytes 196612
  53.4 27.7 %all-to-all-start.2 = ((bf16[16,3,128,128]{3,2,1,0:T(8,128)(2,1)}), bf16[16,3,128,128]{3,2,1,0:T(8,128)(2,1)S(1)}, u32[]{:S(2)}, u32[]{:S(2)}) async-start(bf16[16,3,128,128]{3,2,1,0:T(8,128)(2,1)} %shard_map.95), calls=%async_computation.2 | async-start | bytes 3145728 | tf_op jit(solution)/shard_map/all_to_all | solution.py:459
  67.2 1.0 copy-start.6
  68.2 0.8 copy-start.8
  81.2 23.5 %copy-start.1 = (bf16[16,3,128,128]{3,2,1,0:T(8,128)(2,1)}, bf16[16,3,128,128]{3,2,1,0:T(8,128)(2,1)S(1)}, u32[]{:S(2)}) copy-start(bf16[16,3,128,128]{3,2,1,0:T(8,128)(2,1)S(1)} %all-to-all-done.2) | copy-start | bytes 4718596
  81.2 1.8 copy-start.7
  83.0 1.0 copy-start.9
  104.7 1.1 copy-start.3
  105.8 0.8 copy-start.10
  106.6 29.3 %all-to-all-start.3 = ((bf16[16,3,128,128]{3,2,1,0:T(8,128)(2,1)}), bf16[16,3,128,128]{3,2,1,0:T(8,128)(2,1)S(1)}, u32[]{:S(2)}, u32[]{:S(2)}) async-start(bf16[16,3,128,128]{3,2,1,0:T(8,128)(2,1)} %bitcast.17), calls=%async_computation.3 | async-start | bytes 3145728 | tf_op jit(solution)/shard_map/all_to_all | solution.py:459
  113.0 1.4 copy-start.2
  114.4 1.0 copy-start.11
  134.6 1.2 copy-start

commit v3 on v2

v3 whole, which is shorter than its diff:
```python
import functools
import math

import jax
import jax.numpy as jnp
from jax import lax
from jax.experimental import pallas as pl
from jax.experimental.pallas import tpu as pltpu
from jax.sharding import PartitionSpec as P

HD = 128
TILE = 128
WIDE = 256
BT = 8
NB = 16
FAR = 24
HALF = 64
EARLY = 4
WORK = 8
REST = 4
STEP = 4
INV_ROOT = 1.0 / math.sqrt(HD)
SCORE_SCALE = INV_ROOT * math.log2(math.e)
FLOOR = -1e30

OWN_COUNT, FAR_COUNT, OWN_LIST, FAR_LIST, PLAN = 0, 1, 8, 16, 64

NT = (((1,), (1,)), ((), ()))


def dot(a, b):
    return jnp.dot(a, b, preferred_element_type=jnp.float32)


def dot_nt(a, b):
    return lax.dot_general(a, b, NT, preferred_element_type=jnp.float32)


def block_of(order_ref, index):
    return lax.shift_right_logical(order_ref[index * BT], 3)


def invert_blocks(order_ref, where_ref):
    for k in range(NB):
        where_ref[block_of(order_ref, k)] = k


def core():
    return lax.axis_index("blk") & 1


def served_block():
    return (lax.axis_index("blk") & ~1) + lax.shift_right_logical(lax.axis_index("head"), 2)


def pair_columns(group, which):
    return pl.ds(pl.multiple_of((2 * group + which) * WIDE, WIDE), WIDE)


def pack_kernel(*refs):
    sources, (keep_ref, send_ref), landed, sems = refs[:4], refs[4:6], refs[6:10], refs[10]
    copies = [
        pltpu.make_async_copy(source, target, sems.at[n])
        for n, (source, target) in enumerate(zip(sources, landed))
    ]
    for copy in copies:
        copy.start()
    for copy in copies:
        copy.wait()
    q_ref, d_ref, k_ref, v_ref = landed
    me = core()
    for g in range(4):
        for ref, which in ((keep_ref, me), (send_ref, 1 - me)):
            ref[g, :, 0:256] = q_ref[:, pair_columns(g, which)]
            ref[g, :, 256:512] = d_ref[:, pair_columns(g, which)]
        key = k_ref[:, g * HD : (g + 1) * HD]
        value = v_ref[:, g * HD : (g + 1) * HD]
        keep_ref[g, :, 512:640] = jnp.where(me == 0, key, value)
        send_ref[g, :, 512:640] = jnp.where(me == 0, value, key)


def merge_kernel(keep_ref, came_ref, out_ref):
    me = core()
    for g in range(4):
        out_ref[me * 4 + g] = keep_ref[g]
        out_ref[(1 - me) * 4 + g] = came_ref[g]


def pick_kernel(back_ref, send_ref):
    for g in range(4):
        send_ref[g] = back_ref[(1 - core()) * 4 + g]


def unpack_kernel(back_ref, came_ref, o_ref, dq_ref, dk_ref, dv_ref):
    me = core()
    for g in range(4):
        mine = back_ref[me * 4 + g]
        for piece, which in ((mine, me), (came_ref[g], 1 - me)):
            o_ref[:, pair_columns(g, which)] = piece[:, 0:256]
            dq_ref[:, pair_columns(g, which)] = piece[:, 256:512]
        a, b = mine[:, 512:640], came_ref[g, :, 512:640]
        dk_ref[:, g * HD : (g + 1) * HD] = jnp.where(me == 0, a, b)
        dv_ref[:, g * HD : (g + 1) * HD] = jnp.where(me == 0, b, a)


def pair_sum_kernel(keep_ref, came_ref, out_ref):
    total = keep_ref[...].astype(jnp.float32) + came_ref[...].astype(jnp.float32)
    out_ref[...] = total.astype(jnp.bfloat16)


def add_kernel(rows_ref, late_ref, keep_ref, came_ref, home_ref, out_ref):
    out_ref[EARLY:, :, 256:512] = late_ref[...]
    total = keep_ref[...] + came_ref[...].astype(jnp.float32) + home_ref[...].astype(jnp.float32)
    out_ref[:, :, 512:640] = total.astype(jnp.bfloat16)


def gather_kernel(order_ref, pieces_ref, out_ref, where_ref):
    invert_blocks(order_ref, where_ref)

    @pl.loop(0, NB)
    def _(k):
        b = block_of(order_ref, k)
        for j in range(3):
            src = jnp.maximum(b - 1 - j, 0) if j < 2 else 0
            out_ref[k, j] = pieces_ref[where_ref[src]]


def sum_kernel(order_ref, parts_ref, out_ref, where_ref):
    invert_blocks(order_ref, where_ref)

    @pl.loop(0, NB)
    def _(k):
        b = block_of(order_ref, k)
        near = parts_ref[where_ref[jnp.minimum(b + 1, NB - 1)], 0].astype(jnp.float32)
        far = parts_ref[where_ref[jnp.minimum(b + 2, NB - 1)], 1].astype(jnp.float32)
        total = jnp.where(b + 1 < NB, near, 0.0) + jnp.where(b + 2 < NB, far, 0.0)
        out_ref[k] = total.astype(jnp.bfloat16)

    total = parts_ref[where_ref[1], 0].astype(jnp.float32)
    total = total + parts_ref[where_ref[2], 1].astype(jnp.float32)
    for b in range(3, NB):
        total = total + parts_ref[where_ref[b], 2].astype(jnp.float32)
    out_ref[where_ref[0]] = total.astype(jnp.bfloat16)


def fold(x, op):
    return op(x.reshape(-1, 8, WIDE), axis=0)


def spread(x):
    return jnp.broadcast_to(x, (8, WIDE))


def joined(refs, axis):
    return jnp.concatenate(refs, axis=axis)


def stacked(rows_ref, r, lo):
    return joined([rows_ref[r, :, lo : lo + HD], rows_ref[r, :, lo + HD : lo + 2 * HD]], 0)


def own_seen(count):
    k_pos = lax.broadcasted_iota(jnp.int32, (BT * TILE, WIDE), 0)
    q_pos = lax.broadcasted_iota(jnp.int32, (BT * TILE, WIDE), 1) % TILE
    limit = jnp.where(k_pos < TILE, q_pos + 1, (count + 1) * TILE)
    return k_pos < limit


def own_tiles(plan_ref, r):
    count = plan_ref[r, OWN_COUNT]
    rest = [jnp.where(u < count, plan_ref[r, OWN_LIST + u], r) for u in range(BT - 1)]
    return count, [r] + rest


def near_kernel(
    order_ref, mask_ref, rows_ref, came_ref, plan_ref, top_ref, total_ref, acc_ref, upt_ref,
    own_s, vt_s, mask_s, sem,
):
    b = block_of(order_ref, served_block())
    copy = pltpu.make_async_copy(mask_ref.at[pl.ds(pl.multiple_of(b * BT, BT), BT)], mask_s, sem)
    copy.start()

    @pl.loop(0, BT)
    def _(t):
        own_s[core(), t] = rows_ref[t, :, 512:640]
        own_s[1 - core(), t] = came_ref[t]
        vt_s[t] = own_s[1, t].T

    copy.wait()

    @pl.loop(0, BT)
    def _(r):
        own = jnp.int32(0)
        for t in range(BT - 1):
            plan_ref[r, OWN_LIST + own] = t
            own = own + ((mask_s[r, b * BT + t] == 1) & (t < r)).astype(jnp.int32)
        plan_ref[r, OWN_COUNT] = own
        far = jnp.int32(0)
        for t in range(BT):
            for j in range(3):
                column = jnp.maximum(b - 1 - j, 0) * BT + t if j < 2 else t
                plan_ref[r, FAR_LIST + far] = t * 6 + j
                far = far + ((mask_s[r, column] == 1) & (b > j)).astype(jnp.int32)
        plan_ref[r, FAR_COUNT] = far

    @pl.loop(0, BT)
    def _(r):
        query = stacked(rows_ref, r, 0)
        count, tiles = own_tiles(plan_ref, r)
        scores = dot_nt(joined([own_s[0, t] for t in tiles], 0), query) * SCORE_SCALE
        scores = jnp.where(own_seen(count), scores, FLOOR)
        top = jnp.max(fold(scores, jnp.max), axis=0, keepdims=True)
        weights = jnp.exp2(scores - top)
        top_ref[r] = spread(top)
        total_ref[r] = fold(weights, jnp.sum)
        acc_ref[r] = dot(joined([vt_s[t] for t in tiles], 1), weights.astype(jnp.bfloat16))
        upt_ref[r] = joined([rows_ref[r, :, 256:384].T, rows_ref[r, :, 384:512].T], 1)


def far_steps(plan_ref, r, step):
    count = plan_ref[r, FAR_COUNT]
    whole = lax.shift_right_logical(count, 3)
    rest = count & (WORK - 1)

    @pl.loop(0, whole)
    def _(g):
        step(g * WORK, [plan_ref[r, FAR_LIST + g * WORK + u] for u in range(WORK)], None)

    def partly(width):
        base = whole * WORK
        tiles = [
            jnp.where(u < rest, plan_ref[r, FAR_LIST + jnp.minimum(base + u, FAR - 1)], 0)
            for u in range(width)
        ]
        step(base, tiles, rest)

    @pl.when(rest > REST)
    def _():
        partly(WORK)

    @pl.when((rest > 0) & (rest <= REST))
    def _():
        partly(REST)


def halves(ref, part, tiles):
    return [ref[part, t + 3 * half] for t in tiles for half in range(2)]


def only(scores, live):
    if live is None:
        return scores
    row = lax.broadcasted_iota(jnp.int32, scores.shape, 0)
    return jnp.where(row < live * TILE, scores, FLOOR)


def far_kernel(
    plan_ref, rows_ref, far_ref, came_ref, top_ref, total_ref, acc_ref, upt_ref,
    keep_ref, send_ref, ot_ref, lse_ref, delta_ref,
    kv_s, vt_s, s_buf, dk_s, dv_s,
):
    dk_s[...] = jnp.zeros_like(dk_s)
    dv_s[...] = jnp.zeros_like(dv_s)
    kv_s[core()] = far_ref[...]
    kv_s[1 - core()] = came_ref[...]

    @pl.loop(0, BT)
    def _(t):
        for j in range(3):
            vt_s[t * 6 + j] = joined(halves(kv_s, 1, [t * 6 + j]), 0).T

    def work(r, width):
        count = plan_ref[r, FAR_COUNT]
        listed = [plan_ref[r, FAR_LIST + u] for u in range(width)]
        sure = width - STEP
        tiles = [t if u <= sure else jnp.where(u < count, t, 0) for u, t in enumerate(listed)]
        query = stacked(rows_ref, r, 0)
        upstream_t = upt_ref[r].astype(jnp.float32)
        near_top = top_ref[r][:1]
        top = near_top
        if width:
            scores = dot_nt(joined(halves(kv_s, 0, tiles), 0), query) * SCORE_SCALE
            row = lax.broadcasted_iota(jnp.int32, (STEP * TILE, WIDE), 0)
            last = jnp.where(row < (count - sure) * TILE, scores[sure * TILE :], FLOOR)
            scores = joined([scores[: sure * TILE], last], 0) if sure else last
            s_buf[: width * TILE] = scores
            top = jnp.maximum(top, jnp.max(fold(scores, jnp.max), axis=0, keepdims=True))
        shrink = jnp.exp2(near_top - top)
        total = total_ref[r] * shrink
        acc = acc_ref[r] * shrink
        if width:
            weights = jnp.exp2(s_buf[: width * TILE] - top)
            s_buf[: width * TILE] = weights
            total = total + fold(weights, jnp.sum)
            acc = acc + dot(joined([vt_s[t] for t in tiles], 1), weights.astype(jnp.bfloat16))
        total = jnp.sum(total, axis=0, keepdims=True)
        inverse = 1.0 / total
        attended = (acc * inverse).astype(jnp.bfloat16)
        ot_ref[r] = attended
        delta = attended.astype(jnp.float32) * upstream_t
        delta = jnp.sum(fold(delta, jnp.sum), axis=0, keepdims=True)
        lse_ref[r] = spread(top + jnp.log2(total))
        delta_ref[r] = spread(delta)
        if width:
            probs = s_buf[: width * TILE] * inverse
            grad_probs = dot(joined(halves(kv_s, 1, tiles), 0), upt_ref[r])
            grad_scores = (probs * (grad_probs - delta)).astype(jnp.bfloat16)
            grad_value = dot_nt(probs.astype(jnp.bfloat16), upt_ref[r])
            grad_key = dot(grad_scores, query)
            for u, t in enumerate(tiles):
                for half in range(2):
                    part = slice(u * TILE + half * HALF, u * TILE + (half + 1) * HALF)
                    dv_s[t + 3 * half] += grad_value[part]
                    dk_s[t + 3 * half] += grad_key[part]

    dk_s[...] = jnp.zeros_like(dk_s)
    dv_s[...] = jnp.zeros_like(dv_s)

    @pl.loop(0, BT)
    def _(r):
        steps = lax.shift_right_logical(plan_ref[r, FAR_COUNT] + STEP - 1, 2)
        for width in range(0, FAR + 1, STEP):
            pl.when(steps == width // STEP)(functools.partial(work, r, width))

    grad_key = (dk_s[...] * INV_ROOT).astype(jnp.bfloat16)
    grad_value = dv_s[...].astype(jnp.bfloat16)
    keep_ref[...] = jnp.where(core() == 0, grad_key, grad_value)
    send_ref[...] = jnp.where(core() == 0, grad_value, grad_key)


def score_gradients(scores, value, upstream, lse, delta):
    probs = jnp.exp2(scores - lse)
    grad_probs = dot_nt(value, upstream)
    return probs, (probs * (grad_probs - delta)).astype(jnp.bfloat16)


def far_queries(plan_ref, kv_s, fkt_s, dq_s, r, query, upstream, lse, delta):
    def step(slot, tiles, live):
        scores = only(dot_nt(joined(halves(kv_s, 0, tiles), 0), query) * SCORE_SCALE, live)
        value = joined(halves(kv_s, 1, tiles), 0)
        _, grad_scores = score_gradients(scores, value, upstream, lse, delta)
        dq_s[...] += dot(joined([fkt_s[t] for t in tiles], 1), grad_scores)

    far_steps(plan_ref, r, step)


def turned(dq_s):
    dq = dq_s[...] * INV_ROOT
    return joined([dq[:, :TILE].T, dq[:, TILE:].T], 1).astype(jnp.bfloat16)


def rest_kernel(
    plan_ref, rows_ref, other_ref, far_ref, came_ref, ot_ref, lse_ref, delta_ref,
    out_ref, keep_ref, send_ref, part_ref,
    own_s, kv_s, kt_s, fkt_s, dk_s, dv_s, dq_s,
):
    dk_s[...] = jnp.zeros_like(dk_s)
    dv_s[...] = jnp.zeros_like(dv_s)
    kv_s[core()] = far_ref[...]
    kv_s[1 - core()] = came_ref[...]

    @pl.loop(0, BT)
    def _(t):
        own_s[core(), t] = rows_ref[t, :, 512:640]
        own_s[1 - core(), t] = other_ref[t]
        kt_s[t] = own_s[0, t].T
        for j in range(3):
            fkt_s[t * 6 + j] = joined(halves(kv_s, 0, [t * 6 + j]), 0).T

    @pl.loop(0, BT)
    def _(r):
        query = stacked(rows_ref, r, 0)
        upstream = stacked(rows_ref, r, 256)
        lse = lse_ref[r][:1]
        delta = delta_ref[r][:1]
        attended = ot_ref[r].astype(jnp.float32)
        out_ref[r, :, 0:HD] = attended[:, :TILE].T.astype(jnp.bfloat16)
        out_ref[r, :, HD : 2 * HD] = attended[:, TILE:].T.astype(jnp.bfloat16)

        count, tiles = own_tiles(plan_ref, r)
        scores = dot_nt(joined([own_s[0, t] for t in tiles], 0), query) * SCORE_SCALE
        scores = jnp.where(own_seen(count), scores, FLOOR)
        probs, grad_scores = score_gradients(
            scores, joined([own_s[1, t] for t in tiles], 0), upstream, lse, delta
        )
        grad_value = dot(probs.astype(jnp.bfloat16), upstream)
        grad_key = dot(grad_scores, query)
        for u, t in enumerate(tiles):
            dv_s[t] += grad_value[u * TILE : (u + 1) * TILE]
            dk_s[t] += grad_key[u * TILE : (u + 1) * TILE]
        dq_s[...] = dot(joined([kt_s[t] for t in tiles], 1), grad_scores)

        @pl.when(r < EARLY)
        def _():
            far_queries(plan_ref, kv_s, fkt_s, dq_s, r, query, upstream, lse, delta)
            out_ref[r, :, 256:512] = turned(dq_s)

        @pl.when(r >= EARLY)
        def _():
            part_ref[r - EARLY] = dq_s[...]

    grad_key = dk_s[...] * INV_ROOT
    grad_value = dv_s[...]
    keep_ref[...] = jnp.where(core() == 0, grad_key, grad_value)
    send_ref[...] = jnp.where(core() == 0, grad_value, grad_key).astype(jnp.bfloat16)


def late_kernel(
    plan_ref, rows_ref, far_ref, came_ref, lse_ref, delta_ref, part_ref, late_ref, kv_s, fkt_s, dq_s
):
    kv_s[core()] = far_ref[...]
    kv_s[1 - core()] = came_ref[...]

    @pl.loop(0, BT)
    def _(t):
        for j in range(3):
            fkt_s[t * 6 + j] = joined(halves(kv_s, 0, [t * 6 + j]), 0).T

    @pl.loop(EARLY, BT)
    def _(r):
        query = stacked(rows_ref, r, 0)
        upstream = stacked(rows_ref, r, 256)
        dq_s[...] = part_ref[r - EARLY]
        far_queries(
            plan_ref, kv_s, fkt_s, dq_s, r, query, upstream, lse_ref[r][:1], delta_ref[r][:1]
        )
        late_ref[r - EARLY] = turned(dq_s)


VMEM = pl.BlockSpec(memory_space=pltpu.VMEM)
SMEM = pl.BlockSpec(memory_space=pltpu.SMEM)
ANY = pl.BlockSpec(memory_space=pl.ANY)
HBM = pl.BlockSpec(memory_space=pltpu.HBM)
BF16, F32 = jnp.bfloat16, jnp.float32


def shape(dims, dtype):
    return jax.ShapeDtypeStruct(dims, dtype)


def limit(mib):
    return pltpu.CompilerParams(vmem_limit_bytes=mib * 1024 * 1024)


def cost(us):
    return pl.CostEstimate(flops=us * 1_000_000_000, bytes_accessed=us * 100_000, transcendentals=0)


def pack(queries, upstream, keys, values):
    return pl.pallas_call(
        pack_kernel,
        out_shape=(shape((4, TILE, 640), BF16),) * 2,
        in_specs=[ANY] * 4,
        out_specs=(VMEM, VMEM),
        scratch_shapes=[
            pltpu.VMEM((TILE, 2048), BF16),
            pltpu.VMEM((TILE, 2048), BF16),
            pltpu.VMEM((TILE, 512), BF16),
            pltpu.VMEM((TILE, 512), BF16),
            pltpu.SemaphoreType.DMA((4,)),
        ],
        compiler_params=limit(60),
    )(queries, upstream, keys, values)


def simple(kernel, out_shape, *arrays):
    return pl.pallas_call(
        kernel,
        out_shape=out_shape,
        in_specs=[VMEM] * len(arrays),
        out_specs=jax.tree.map(lambda _: VMEM, out_shape),
        compiler_params=limit(16),
    )(*arrays)


def add_home(out, late, keep, came, home):
    return pl.pallas_call(
        add_kernel,
        out_shape=shape((BT, TILE, 640), BF16),
        in_specs=[VMEM] * 5,
        out_specs=VMEM,
        input_output_aliases={0: 0},
        compiler_params=limit(16),
    )(out, late, keep, came, home)


def near(order, mask, rows, other):
    return pl.pallas_call(
        near_kernel,
        out_shape=(
            shape((BT, PLAN), jnp.int32),
            shape((BT, 8, WIDE), F32),
            shape((BT, 8, WIDE), F32),
            shape((BT, HD, WIDE), F32),
            shape((BT, HD, WIDE), BF16),
        ),
        in_specs=[SMEM, ANY, VMEM, VMEM],
        out_specs=(SMEM, VMEM, VMEM, VMEM, VMEM),
        scratch_shapes=[
            pltpu.VMEM((2, BT, TILE, HD), BF16),
            pltpu.VMEM((BT, HD, TILE), BF16),
            pltpu.SMEM((BT, 128), jnp.int32),
            pltpu.SemaphoreType.DMA,
        ],
        compiler_params=limit(60),
        cost_estimate=cost(12),
    )(order, mask, rows, other)


def far_part(plan, rows, far, came, top, total, acc, upt):
    return pl.pallas_call(
        far_kernel,
        out_shape=(
            shape((2 * FAR, HALF, HD), BF16),
            shape((2 * FAR, HALF, HD), BF16),
            shape((BT, HD, WIDE), BF16),
            shape((BT, 8, WIDE), F32),
            shape((BT, 8, WIDE), F32),
        ),
        in_specs=[SMEM] + [VMEM] * 7,
        out_specs=(VMEM,) * 5,
        scratch_shapes=[
            pltpu.VMEM((2, 2 * FAR, HALF, HD), BF16),
            pltpu.VMEM((2 * FAR, HD, TILE), BF16),
            pltpu.VMEM((FAR * TILE, WIDE), F32),
            pltpu.VMEM((2 * FAR, HALF, HD), F32),
            pltpu.VMEM((2 * FAR, HALF, HD), F32),
        ],
        compiler_params=limit(60),
        cost_estimate=cost(25),
    )(plan, rows, far, came, top, total, acc, upt)


def rest_part(plan, rows, other, far, came, ot, lse, delta):
    return pl.pallas_call(
        rest_kernel,
        out_shape=(
            shape((BT, TILE, 640), BF16),
            shape((BT, TILE, HD), F32),
            shape((BT, TILE, HD), BF16),
            shape((BT - EARLY, HD, WIDE), F32),
        ),
        in_specs=[SMEM] + [VMEM] * 7,
        out_specs=(VMEM,) * 4,
        scratch_shapes=[
            pltpu.VMEM((2, BT, TILE, HD), BF16),
            pltpu.VMEM((2, 2 * FAR, HALF, HD), BF16),
            pltpu.VMEM((BT, HD, TILE), BF16),
            pltpu.VMEM((2 * FAR, HD, TILE), BF16),
            pltpu.VMEM((BT, TILE, HD), F32),
            pltpu.VMEM((BT, TILE, HD), F32),
            pltpu.VMEM((HD, WIDE), F32),
        ],
        compiler_params=limit(60),
        cost_estimate=cost(18),
    )(plan, rows, other, far, came, ot, lse, delta)


def late_part(plan, rows, far, came, lse, delta, part):
    return pl.pallas_call(
        late_kernel,
        out_shape=shape((BT - EARLY, TILE, WIDE), BF16),
        in_specs=[SMEM] + [VMEM] * 6,
        out_specs=VMEM,
        scratch_shapes=[
            pltpu.VMEM((2, 2 * FAR, HALF, HD), BF16),
            pltpu.VMEM((2 * FAR, HD, TILE), BF16),
            pltpu.VMEM((HD, WIDE), F32),
        ],
        compiler_params=limit(60),
        cost_estimate=cost(10),
    )(plan, rows, far, came, lse, delta, part)


def routed(kernel, order, array, out_shape):
    return pl.pallas_call(
        kernel,
        out_shape=shape(out_shape, BF16),
        in_specs=[SMEM, VMEM],
        out_specs=VMEM,
        scratch_shapes=[pltpu.SMEM((NB,), jnp.int32)],
        compiler_params=limit(16),
    )(order, array)


def over_heads(array):
    return lax.all_to_all(array, "head", split_axis=0, concat_axis=0, tiled=True)


SERVING = [
    [(2 * chip + u) * 8 + beta * 4 + g for chip in range(8) for beta in range(2)]
    for u in range(2)
    for g in range(4)
]


def over_blocks(array):
    return lax.all_to_all(
        array, ("blk", "head"), split_axis=0, concat_axis=0, axis_index_groups=SERVING, tiled=True
    )


def to_other_core(array):
    return lax.ppermute(array, "blk", [(i, i ^ 1) for i in range(16)])


def on_device(queries, keys, values, upstream, tile_mask, tile_order):
    order = tile_order[0]
    keep, send = pack(queries[0], upstream[0], keys[0], values[0])
    both = simple(merge_kernel, shape((8, TILE, 640), BF16), keep, to_other_core(send))
    rows = over_heads(both)
    own = rows[:, :, 512:]
    other = to_other_core(own)
    pieces = over_blocks(own.reshape(NB, HALF, HD))
    chosen = routed(gather_kernel, order, pieces, (NB, 3, HALF, HD))
    far = over_blocks(chosen).reshape(2 * FAR, HALF, HD)
    begun = near(order, tile_mask[0], rows, other)
    far, *begun = lax.optimization_barrier((far, *begun))
    plan = begun[0]
    came = to_other_core(far)
    keep, send, ot, lse, delta = far_part(plan, rows, far, came, *begun[1:])
    dfar = simple(pair_sum_kernel, shape((2 * FAR, HALF, HD), BF16), keep, to_other_core(send))
    parts = over_blocks(dfar.reshape(NB, 3, HALF, HD))
    out, keep, send, part = rest_part(plan, rows, other, far, came, ot, lse, delta)
    parts, out, keep, send, part = lax.optimization_barrier((parts, out, keep, send, part))
    summed = routed(sum_kernel, order, parts, (NB, HALF, HD))
    summed, part = lax.optimization_barrier((summed, part))
    home = over_blocks(summed).reshape(BT, TILE, HD)
    late = late_part(plan, rows, far, came, lse, delta, part)
    back = over_heads(add_home(out, late, keep, to_other_core(send), home))
    came = to_other_core(simple(pick_kernel, shape((4, TILE, 640), BF16), back))
    wide, slim = shape((TILE, 2048), BF16), shape((TILE, 512), BF16)
    outs = simple(unpack_kernel, (wide, wide, slim, slim), back, came)
    return tuple(array[None] for array in outs)


def solution(mesh):
    split = P(None, ("blk", "head"), None)
    return jax.shard_map(
        on_device,
        mesh=mesh,
        in_specs=(split, split, split, split, P(), P()),
        out_specs=(split, split, split, split),
        check_vma=False,
    )
```

time: 187 us -> 168 us (0.90)
  blocking collectives: 89.9 us -> 58.6 us
  starting transfers between devices: 11.1 us -> 25.2 us
  Pallas kernels: 61.1 us -> 68.6 us
  local copies, waits for them, and re-layouts: 10.4 us -> 4.8 us
  waiting for transfers between devices: 12.3 us -> 9.54 us
    all_to_all x4 -> x3, blocking collectives: 89.9 us -> 58.6 us  [the longest x2 43.9 us: over_heads(): lax.all_to_all(array, 'head', split_axis=0, concat_axis=0, tiled=True)]
    all_to_all x2 -> x3, waiting for transfers between devices: 12.3 us -> 1.83 us  [over_blocks(): lax.all_to_all(array, ('blk', 'head'), split_axis=0, concat_axis=0, axis_...]
    ppermute x0 -> x6, starting transfers between devices: none -> 10 us  [to_other_core(): return lax.ppermute(array, 'blk', [(i, i ^ 1) for i in range(16)])]
    ppermute x0 -> x6, waiting for transfers between devices: none -> 7.7 us  [to_other_core(): return lax.ppermute(array, 'blk', [(i, i ^ 1) for i in range(16)])]
    pallas_call x5 -> x9, Pallas kernels: 49.1 us -> 54.8 us  [the longest x1 23.7 us: far_part(): pl.pallas_call(far_kernel, out_shape=(shape((2 * FAR, HALF, HD), BF16), s...]
    unnamed x24, local copies, waits for them, and re-layouts: 10.2 us -> 4.75 us
    all_to_all x2 -> x3, starting transfers between devices: 11.1 us -> 15.2 us  [over_blocks(): lax.all_to_all(array, ('blk', 'head'), split_axis=0, concat_axis=0, axis_...]
  transfers between devices with their start and end apart: 2 -> 9, of which waited for: 2 -> 5; matrix products, arithmetic and copies ran while one was open for 0% -> 0% of each run, Pallas kernels for 15% -> 23%
where the time goes in v3:
time: 168 us; the launch traced here: 167 us
  Pallas kernels  68.6 us (41%)
  blocking collectives  58.6 us (35%)
  starting transfers between devices  25.2 us (15%)
  waiting for transfers between devices  9.54 us (6%)
  local copies, waits for them, and re-layouts  4.8 us (3%)
    all_to_all x2, blocking collectives, over_heads(): lax.all_to_all(array, 'head', split_axis=0, concat_axis=0, tiled=True)  43.9 us
    pallas_call x1, Pallas kernels, far_part(): pl.pallas_call(far_kernel, out_shape=(shape((2 * FAR, HALF, HD), BF16), s...  23.7 us
    pallas_call x1, Pallas kernels, rest_part(): pl.pallas_call(rest_kernel, out_shape=(shape((BT, TILE, 640), BF16), shap...  17.3 us
    all_to_all x3, starting transfers between devices, over_blocks(): lax.all_to_all(array, ('blk', 'head'), split_axis=0, concat_axis=0, axis_...  15.2 us
    all_to_all x1, blocking collectives, over_blocks(): lax.all_to_all(array, ('blk', 'head'), split_axis=0, concat_axis=0, axis_...  14.8 us
    pallas_call x1, Pallas kernels, near(): pl.pallas_call(near_kernel, out_shape=(shape((BT, PLAN), jnp.int32), shap...  10.4 us
    ppermute x6, starting transfers between devices, to_other_core(): return lax.ppermute(array, 'blk', [(i, i ^ 1) for i in range(16)])  10 us
    pallas_call x1, Pallas kernels, late_part(): pl.pallas_call(late_kernel, out_shape=shape((BT - EARLY, TILE, WIDE), BF1...  8.76 us
  transfers between devices with their start and end apart: 9, of which 5 were waited for; matrix products, arithmetic and copies ran while one was open for 0% of the time, Pallas kernels for 23%

profile of v3, /device:TPU:1, one launch (start us, length us, event | category | flops | bytes accessed | tf_op | source)
XLA Modules:
  0.0 167.5 jit_solution(14987758039969232404)
XLA Ops:
  0.6 2.5 %shard_map.93 = (bf16[4,128,640]{2,1,0:T(8,128)(2,1)}, bf16[4,128,640]{2,1,0:T(8,128)(2,1)}) custom-call(bf16[128,2048]{1,0:T(8,128)(2,1)} %bitcast.23, bf16[128,2048]{1,0:T(8,128)(2,1)} %bitcast.24, bf16[128,512]{1,0:T(8,128)(2,1)} %bitcast.25, bf16[128,512]{1,0:T(8,128)(2,1)} %bitcast.26), custom_call_target="tpu_custom_call" | custom-call | tf_op jit(solution)/shard_map/pallas_call | solution.py:450
  3.2 1.5 collective-permute-start
  4.7 1.9 %collective-permute-done.came_ref = bf16[4,128,640]{2,1,0:T(8,128)(2,1)S(1)} collective-permute-done((bf16[4,128,640]{2,1,0:T(8,128)(2,1)}, bf16[4,128,640]{2,1,0:T(8,128)(2,1)S(1)}, u32[]{:S(2)}, u32[]{:S(2)}) %collective-permute-start) | collective-permute-done | bytes 655392 | tf_op jit(solution)/shard_map/ppermute | solution.py:604
  6.6 1.1 copy-done.2
  7.7 0.1 shard_map.94
  7.8 23.1 %all_to_all.30.rows_ref = bf16[8,128,640]{2,1,0:T(8,128)(2,1)S(1)} all-to-all(bf16[8,128,640]{2,1,0:T(8,128)(2,1)S(1)} %shard_map.94), channel_id=1, replica_groups=mesh['blk'=16,'head'=8] {'head'}, dimensions={0} | all-to-all | bytes 2621440 | tf_op jit(solution)/shard_map/all_to_all | solution.py:587
  31.0 2.2 %collective-permute-start.1 = (bf16[8,128,128]{2,1,0:T(8,128)(2,1)S(1)}, bf16[8,128,128]{2,1,0:T(8,128)(2,1)S(1)}, u32[]{:S(2)}, u32[]{:S(2)}) collective-permute-start(bf16[8,128,128]{2,1,0:T(8,128)(2,1)S(1)} %slice.4), channel_id=1, source_target_pairs={{0,8},{8,0},{16,24},{24,16},{32,40},{40,32},{48,56},{56,48},{64,72... | collective-permute-start | bytes 786440 | tf_op jit(solution)/shard_map/ppermute | solution.py:604
  33.2 14.8 %all_to_all.31.pieces_ref = bf16[16,64,128]{2,1,0:T(8,128)(2,1)S(1)} all-to-all(bf16[16,64,128]{2,1,0:T(8,128)(2,1)S(1)} %bitcast.18), channel_id=1, replica_groups={{0,4,16,20,32,36,48,52,64,68,80,84,96,100,112,116},{1,5,17,21,33,37,49,..., dimensions={0} | all-to-all | bytes 524288 | tf_op jit(solution)/shard_map/all_to_all | solution.py:598
  48.0 1.7 shard_map.95
  49.6 3.6 %all-to-all-start.2 = ((bf16[16,3,64,128]{3,2,1,0:T(8,128)(2,1)}), bf16[16,3,64,128]{3,2,1,0:T(8,128)(2,1)S(1)}, u32[]{:S(2)}, u32[]{:S(2)}) async-start(bf16[16,3,64,128]{3,2,1,0:T(8,128)(2,1)} %shard_map.95), calls=%async_computation.2 | async-start | bytes 1572864 | tf_op jit(solution)/shard_map/all_to_all | solution.py:598
  53.3 0.7 copy-done.10
  54.0 10.4 %shard_map.96 = (s32[8,64]{1,0:T(8,128)}, f32[8,8,256]{2,1,0:T(8,128)}, f32[8,8,256]{2,1,0:T(8,128)}, f32[8,128,256]{2,1,0:T(8,128)}, bf16[8,128,256]{2,1,0:T(8,128)(2,1)}) custom-call(s32[128]{0:T(128)} %bitcast.15, s32[128,128]{1,0:T(8,128)} %bitcast.31, bf16[8,128,640]{2,1,0:T(8,128)(2,1)} %copy-done.7, bf16[8,128,128]{2,1,0:T(8,128)(2,1)} %copy-done.10), custom_call_target="tpu_custom_call" | custom-call | flops 12000000000 | bytes 1200000 | tf_op jit(solution)/shard_map/pallas_call | solution.py:488
  64.4 1.8 %all-to-all-done.2 = bf16[16,3,64,128]{3,2,1,0:T(8,128)(2,1)S(1)} async-done(((bf16[16,3,64,128]{3,2,1,0:T(8,128)(2,1)}), bf16[16,3,64,128]{3,2,1,0:T(8,128)(2,1)S(1)}, u32[]{:S(2)}, u32[]{:S(2)}) %all-to-all-start.2) | async-done | bytes 786464 | tf_op jit(solution)/shard_map/all_to_all | solution.py:598
  66.2 2.4 %collective-permute-start.2 = (bf16[48,64,128]{2,1,0:T(8,128)(2,1)S(1)}, bf16[48,64,128]{2,1,0:T(8,128)(2,1)S(1)}, u32[]{:S(2)}, u32[]{:S(2)}) collective-permute-start(bf16[48,64,128]{2,1,0:T(8,128)(2,1)S(1)} %bitcast.19), channel_id=1, source_target_pairs={{0,8},{8,0},{16,24},{24,16},{32,40},{40,32},{48,56},{56,48},{64,72... | collective-permute-start | bytes 2359304 | tf_op jit(solution)/shard_map/ppermute | solution.py:604
  68.6 1.9 %collective-permute-done.2.came_ref = bf16[48,64,128]{2,1,0:T(8,128)(2,1)S(1)} collective-permute-done((bf16[48,64,128]{2,1,0:T(8,128)(2,1)S(1)}, bf16[48,64,128]{2,1,0:T(8,128)(2,1)S(1)}, u32[]{:S(2)}, u32[]{:S(2)}) %collective-permute-start.2) | collective-permute-done | bytes 786464 | tf_op jit(solution)/shard_map/ppermute | solution.py:604
  70.5 0.9 copy-done.9
  71.4 23.7 %shard_map.97 = (bf16[48,64,128]{2,1,0:T(8,128)(2,1)}, bf16[48,64,128]{2,1,0:T(8,128)(2,1)}, bf16[8,128,256]{2,1,0:T(8,128)(2,1)}, f32[8,8,256]{2,1,0:T(8,128)}, f32[8,8,256]{2,1,0:T(8,128)}) custom-call(s32[8,64]{1,0:T(8,128)} %get-tuple-element.44.plan_ref, bf16[8,128,640]{2,1,0:T(8,128)(2,1)} %copy-done.7, bf16[48,64,128]{2,1,0:T(8,128)(2,1)} %bitcast.20, ...), custom_call_target="tpu_custom_call" | custom-call | flops 24999999488 | bytes 2500000 | tf_op jit(solution)/shard_map/pallas_call | solution.py:511
  95.1 0.4 collective-permute-start.3
  95.5 2.1 %collective-permute-done.3.came_ref = bf16[48,64,128]{2,1,0:T(8,128)(2,1)S(1)} collective-permute-done((bf16[48,64,128]{2,1,0:T(8,128)(2,1)}, bf16[48,64,128]{2,1,0:T(8,128)(2,1)S(1)}, u32[]{:S(2)}, u32[]{:S(2)}) %collective-permute-start.3) | collective-permute-done | bytes 786464 | tf_op jit(solution)/shard_map/ppermute | solution.py:604
  97.6 1.1 copy-done.1
  98.7 1.1 shard_map.98
  99.8 5.5 %all-to-all-start.3 = ((bf16[16,3,64,128]{3,2,1,0:T(8,128)(2,1)}), bf16[16,3,64,128]{3,2,1,0:T(8,128)(2,1)S(1)}, u32[]{:S(2)}, u32[]{:S(2)}) async-start(bf16[16,3,64,128]{3,2,1,0:T(8,128)(2,1)} %bitcast.8), calls=%async_computation.3 | async-start | bytes 1572864 | tf_op jit(solution)/shard_map/all_to_all | solution.py:598
  105.3 17.3 %shard_map.99 = (bf16[8,128,640]{2,1,0:T(8,128)(2,1)}, f32[8,128,128]{2,1,0:T(8,128)}, bf16[8,128,128]{2,1,0:T(8,128)(2,1)}, f32[4,128,256]{2,1,0:T(8,128)}) custom-call(s32[8,64]{1,0:T(8,128)} %get-tuple-element.44.plan_ref, bf16[8,128,640]{2,1,0:T(8,128)(2,1)} %copy-done.7, bf16[8,128,128]{2,1,0:T(8,128)(2,1)} %copy-done.10, ...), custom_call_target="tpu_custom_call" | custom-call | flops 17999998976 | bytes 1800000 | tf_op jit(solution)/shard_map/pallas_call | solution.py:535
  122.7 1.6 shard_map.100
  124.3 6.0 %all-to-all-start.4 = ((bf16[16,64,128]{2,1,0:T(8,128)(2,1)}), bf16[16,64,128]{2,1,0:T(8,128)(2,1)S(1)}, u32[]{:S(2)}, u32[]{:S(2)}) async-start(bf16[16,64,128]{2,1,0:T(8,128)(2,1)} %shard_map.100), calls=%async_computation.4 | async-start | bytes 524288 | tf_op jit(solution)/shard_map/all_to_all | solution.py:598
  130.4 1.3 collective-permute-start.4
  131.7 8.8 %shard_map.101.late_ref = bf16[4,128,256]{2,1,0:T(8,128)(2,1)} custom-call(s32[8,64]{1,0:T(8,128)} %get-tuple-element.44.plan_ref, bf16[8,128,640]{2,1,0:T(8,128)(2,1)} %copy-done.7, bf16[48,64,128]{2,1,0:T(8,128)(2,1)} %bitcast.22, bf16[48,64,128]{2,1,0:T(8,128)(2,1)} %copy-done.9, f32[8,8,256]{2,1,0:T(8,128)} %get-tuple-element.53.lse_ref, ...), custom_call_target="tpu_custom_call" | custom-call | flops 10000000000 | bytes 1000000 | tf_op jit(solution)/shard_map/pallas_call | solution.py:560
  140.5 0.9 copy-done.4
  141.5 20.8 %all_to_all.32.back_ref = bf16[8,128,640]{2,1,0:T(8,128)(2,1)S(1)} all-to-all(bf16[8,128,640]{2,1,0:T(8,128)(2,1)S(1)} %shard_map.102), channel_id=1, replica_groups=mesh['blk'=16,'head'=8] {'head'}, dimensions={0} | all-to-all | bytes 2621440 | tf_op jit(solution)/shard_map/all_to_all | solution.py:587
  162.4 2.2 %collective-permute-start.5 = (bf16[4,128,640]{2,1,0:T(8,128)(2,1)S(1)}, bf16[4,128,640]{2,1,0:T(8,128)(2,1)S(1)}, u32[]{:S(2)}, u32[]{:S(2)}) collective-permute-start(bf16[4,128,640]{2,1,0:T(8,128)(2,1)S(1)} %shard_map.103), channel_id=1, source_target_pairs={{0,8},{8,0},{16,24},{24,16},{32,40},{40,32},{48,56},{56,48},{64,72... | collective-permute-start | bytes 1966088 | tf_op jit(solution)/shard_map/ppermute | solution.py:604
  164.6 1.7 %collective-permute-done.5.came_ref = bf16[4,128,640]{2,1,0:T(8,128)(2,1)S(1)} collective-permute-done((bf16[4,128,640]{2,1,0:T(8,128)(2,1)S(1)}, bf16[4,128,640]{2,1,0:T(8,128)(2,1)S(1)}, u32[]{:S(2)}, u32[]{:S(2)}) %collective-permute-start.5) | collective-permute-done | bytes 655392 | tf_op jit(solution)/shard_map/ppermute | solution.py:604
  166.3 1.2 shard_map.104
  (26 shorter events, 0.3 us)
Async XLA Ops:
  3.2 3.4 %collective-permute-start = (bf16[4,128,640]{2,1,0:T(8,128)(2,1)}, bf16[4,128,640]{2,1,0:T(8,128)(2,1)S(1)}, u32[]{:S(2)}, u32[]{:S(2)}) collective-permute-start(bf16[4,128,640]{2,1,0:T(8,128)(2,1)} %get-tuple-element.38), channel_id=1, source_target_pairs={{0,8},{8,0},{16,24},{24,16},{32,40},{40,32},{48,56},{56,48},{64,72... | collective-permute-start | bytes 1966088 | tf_op jit(solution)/shard_map/ppermute | solution.py:604
  6.6 1.1 copy-start.2
  7.8 40.1 %copy-start.5 = (s32[1,128]{1,0:T(1,128)S(1)}, s32[1,128]{1,0:T(1,128)}, u32[]{:S(2)}) copy-start(s32[1,128]{1,0:T(1,128)} %param.11) | copy-start | bytes 1540
  30.9 18.7 %copy-start.7 = (bf16[8,128,640]{2,1,0:T(8,128)(2,1)}, bf16[8,128,640]{2,1,0:T(8,128)(2,1)S(1)}, u32[]{:S(2)}) copy-start(bf16[8,128,640]{2,1,0:T(8,128)(2,1)S(1)} %all_to_all.30.rows_ref) | copy-start | bytes 3932164
  31.0 22.3 %collective-permute-start.1 = (bf16[8,128,128]{2,1,0:T(8,128)(2,1)S(1)}, bf16[8,128,128]{2,1,0:T(8,128)(2,1)S(1)}, u32[]{:S(2)}, u32[]{:S(2)}) collective-permute-start(bf16[8,128,128]{2,1,0:T(8,128)(2,1)S(1)} %slice.4), channel_id=1, source_target_pairs={{0,8},{8,0},{16,24},{24,16},{32,40},{40,32},{48,56},{56,48},{64,72... | collective-permute-start | bytes 786440 | tf_op jit(solution)/shard_map/ppermute | solution.py:604
  49.6 16.6 %all-to-all-start.2 = ((bf16[16,3,64,128]{3,2,1,0:T(8,128)(2,1)}), bf16[16,3,64,128]{3,2,1,0:T(8,128)(2,1)S(1)}, u32[]{:S(2)}, u32[]{:S(2)}) async-start(bf16[16,3,64,128]{3,2,1,0:T(8,128)(2,1)} %shard_map.95), calls=%async_computation.2 | async-start | bytes 1572864 | tf_op jit(solution)/shard_map/all_to_all | solution.py:598
  53.3 0.7 copy-start.10
  66.2 4.3 %copy-start.8 = (bf16[16,3,64,128]{3,2,1,0:T(8,128)(2,1)}, bf16[16,3,64,128]{3,2,1,0:T(8,128)(2,1)S(1)}, u32[]{:S(2)}) copy-start(bf16[16,3,64,128]{3,2,1,0:T(8,128)(2,1)S(1)} %all-to-all-done.2) | copy-start | bytes 2359300
  66.2 4.3 %collective-permute-start.2 = (bf16[48,64,128]{2,1,0:T(8,128)(2,1)S(1)}, bf16[48,64,128]{2,1,0:T(8,128)(2,1)S(1)}, u32[]{:S(2)}, u32[]{:S(2)}) collective-permute-start(bf16[48,64,128]{2,1,0:T(8,128)(2,1)S(1)} %bitcast.19), channel_id=1, source_target_pairs={{0,8},{8,0},{16,24},{24,16},{32,40},{40,32},{48,56},{56,48},{64,72... | collective-permute-start | bytes 2359304 | tf_op jit(solution)/shard_map/ppermute | solution.py:604
  70.5 0.9 copy-start.9
  95.1 2.5 %collective-permute-start.3 = (bf16[48,64,128]{2,1,0:T(8,128)(2,1)}, bf16[48,64,128]{2,1,0:T(8,128)(2,1)S(1)}, u32[]{:S(2)}, u32[]{:S(2)}) collective-permute-start(bf16[48,64,128]{2,1,0:T(8,128)(2,1)} %get-tuple-element.51), channel_id=1, source_target_pairs={{0,8},{8,0},{16,24},{24,16},{32,40},{40,32},{48,56},{56,48},{64,72... | collective-permute-start | bytes 2359304 | tf_op jit(solution)/shard_map/ppermute | solution.py:604
  97.6 1.1 copy-start.1
  99.8 22.9 %all-to-all-start.3 = ((bf16[16,3,64,128]{3,2,1,0:T(8,128)(2,1)}), bf16[16,3,64,128]{3,2,1,0:T(8,128)(2,1)S(1)}, u32[]{:S(2)}, u32[]{:S(2)}) async-start(bf16[16,3,64,128]{3,2,1,0:T(8,128)(2,1)} %bitcast.8), calls=%async_computation.3 | async-start | bytes 1572864 | tf_op jit(solution)/shard_map/all_to_all | solution.py:598
  105.3 17.3 %copy-start.6 = (s32[1,128]{1,0:T(1,128)S(1)}, s32[1,128]{1,0:T(1,128)}, u32[]{:S(2)}) copy-start(s32[1,128]{1,0:T(1,128)} %param.11) | copy-start | bytes 1540
  122.7 7.7 %copy-start.11 = (bf16[8,128,128]{2,1,0:T(8,128)(2,1)S(1)}, bf16[8,128,128]{2,1,0:T(8,128)(2,1)}, u32[]{:S(2)}) copy-start(bf16[8,128,128]{2,1,0:T(8,128)(2,1)} %get-tuple-element.64) | copy-start | bytes 786436
  124.3 16.1 %all-to-all-start.4 = ((bf16[16,64,128]{2,1,0:T(8,128)(2,1)}), bf16[16,64,128]{2,1,0:T(8,128)(2,1)S(1)}, u32[]{:S(2)}, u32[]{:S(2)}) async-start(bf16[16,64,128]{2,1,0:T(8,128)(2,1)} %shard_map.100), calls=%async_computation.4 | async-start | bytes 524288 | tf_op jit(solution)/shard_map/all_to_all | solution.py:598
  130.4 10.1 %copy-start = (bf16[8,128,640]{2,1,0:T(8,128)(2,1)S(1)}, bf16[8,128,640]{2,1,0:T(8,128)(2,1)}, u32[]{:S(2)}) copy-start(bf16[8,128,640]{2,1,0:T(8,128)(2,1)} %get-tuple-element.59.rows_ref) | copy-start | bytes 3932164
  130.4 10.1 %copy-start.3 = (f32[8,128,128]{2,1,0:T(8,128)S(1)}, f32[8,128,128]{2,1,0:T(8,128)}, u32[]{:S(2)}) copy-start(f32[8,128,128]{2,1,0:T(8,128)} %get-tuple-element.63.keep_ref) | copy-start | bytes 1572868
  130.4 10.0 %collective-permute-start.4 = (bf16[8,128,128]{2,1,0:T(8,128)(2,1)S(1)}, bf16[8,128,128]{2,1,0:T(8,128)(2,1)S(1)}, u32[]{:S(2)}, u32[]{:S(2)}) collective-permute-start(bf16[8,128,128]{2,1,0:T(8,128)(2,1)S(1)} %copy-done.11), channel_id=1, source_target_pairs={{0,8},{8,0},{16,24},{24,16},{32,40},{40,32},{48,56},{56,48},{64,72... | collective-permute-start | bytes 786440 | tf_op jit(solution)/shard_map/ppermute | solution.py:604
  140.5 1.0 copy-start.4
  162.4 3.9 %collective-permute-start.5 = (bf16[4,128,640]{2,1,0:T(8,128)(2,1)S(1)}, bf16[4,128,640]{2,1,0:T(8,128)(2,1)S(1)}, u32[]{:S(2)}, u32[]{:S(2)}) collective-permute-start(bf16[4,128,640]{2,1,0:T(8,128)(2,1)S(1)} %shard_map.103), channel_id=1, source_target_pairs={{0,8},{8,0},{16,24},{24,16},{32,40},{40,32},{48,56},{56,48},{64,72... | collective-permute-start | bytes 1966088 | tf_op jit(solution)/shard_map/ppermute | solution.py:604

commit v4 on v3

--- a/solution.py
+++ b/solution.py
@@ -15,9 +15,10 @@
 NB = 16
 FAR = 24
 HALF = 64
-EARLY = 4
+EARLY = 5
 WORK = 8
 REST = 4
+SUB = 4
 STEP = 4
 INV_ROOT = 1.0 / math.sqrt(HD)
 SCORE_SCALE = INV_ROOT * math.log2(math.e)
@@ -159,21 +160,21 @@
     return joined([rows_ref[r, :, lo : lo + HD], rows_ref[r, :, lo + HD : lo + 2 * HD]], 0)
 
 
-def own_seen(count):
-    k_pos = lax.broadcasted_iota(jnp.int32, (BT * TILE, WIDE), 0)
-    q_pos = lax.broadcasted_iota(jnp.int32, (BT * TILE, WIDE), 1) % TILE
+def own_seen(count, width):
+    k_pos = lax.broadcasted_iota(jnp.int32, (width * TILE, WIDE), 0)
+    q_pos = lax.broadcasted_iota(jnp.int32, (width * TILE, WIDE), 1) % TILE
     limit = jnp.where(k_pos < TILE, q_pos + 1, (count + 1) * TILE)
     return k_pos < limit
 
 
-def own_tiles(plan_ref, r):
+def own_tiles(plan_ref, r, width):
     count = plan_ref[r, OWN_COUNT]
-    rest = [jnp.where(u < count, plan_ref[r, OWN_LIST + u], r) for u in range(BT - 1)]
+    rest = [jnp.where(u < count, plan_ref[r, OWN_LIST + u], r) for u in range(width - 1)]
     return count, [r] + rest
 
 
 def near_kernel(
-    order_ref, mask_ref, rows_ref, came_ref, plan_ref, top_ref, total_ref, acc_ref, upt_ref,
+    order_ref, mask_ref, rows_ref, came_ref, plan_ref, top_ref, total_ref, acc_ref, upt_ref, qs_ref,
     own_s, vt_s, mask_s, sem,
 ):
     b = block_of(order_ref, served_block())
@@ -206,9 +207,10 @@
     @pl.loop(0, BT)
     def _(r):
         query = stacked(rows_ref, r, 0)
-        count, tiles = own_tiles(plan_ref, r)
+        qs_ref[r] = query
+        count, tiles = own_tiles(plan_ref, r, BT)
         scores = dot_nt(joined([own_s[0, t] for t in tiles], 0), query) * SCORE_SCALE
-        scores = jnp.where(own_seen(count), scores, FLOOR)
+        scores = jnp.where(own_seen(count, BT), scores, FLOOR)
         top = jnp.max(fold(scores, jnp.max), axis=0, keepdims=True)
         weights = jnp.exp2(scores - top)
         top_ref[r] = spread(top)
@@ -255,9 +257,9 @@
 
 
 def far_kernel(
-    plan_ref, rows_ref, far_ref, came_ref, top_ref, total_ref, acc_ref, upt_ref,
+    plan_ref, far_ref, came_ref, top_ref, total_ref, acc_ref, upt_ref, qs_ref,
     keep_ref, send_ref, ot_ref, lse_ref, delta_ref,
-    kv_s, vt_s, s_buf, dk_s, dv_s,
+    kv_s, vt_s, s_buf, w_buf, dk_s, dv_s,
 ):
     dk_s[...] = jnp.zeros_like(dk_s)
     dv_s[...] = jnp.zeros_like(dv_s)
@@ -274,40 +276,42 @@
         listed = [plan_ref[r, FAR_LIST + u] for u in range(width)]
         sure = width - STEP
         tiles = [t if u <= sure else jnp.where(u < count, t, 0) for u, t in enumerate(listed)]
-        query = stacked(rows_ref, r, 0)
-        upstream_t = upt_ref[r].astype(jnp.float32)
+        parts = [(lo, min(lo + SUB, width)) for lo in range(0, width, SUB)]
+        query = qs_ref[r]
+        upstream = upt_ref[r]
         near_top = top_ref[r][:1]
-        top = near_top
-        if width:
-            scores = dot_nt(joined(halves(kv_s, 0, tiles), 0), query) * SCORE_SCALE
-            row = lax.broadcasted_iota(jnp.int32, (STEP * TILE, WIDE), 0)
-            last = jnp.where(row < (count - sure) * TILE, scores[sure * TILE :], FLOOR)
-            scores = joined([scores[: sure * TILE], last], 0) if sure else last
-            s_buf[: width * TILE] = scores
-            top = jnp.maximum(top, jnp.max(fold(scores, jnp.max), axis=0, keepdims=True))
+        tops = top_ref[r]
+        for lo, hi in parts:
+            scores = dot_nt(joined(halves(kv_s, 0, tiles[lo:hi]), 0), query) * SCORE_SCALE
+            if hi > sure + 1:
+                scores = only(scores, count - lo)
+            s_buf[lo * TILE : hi * TILE] = scores
+            tops = jnp.maximum(tops, fold(scores, jnp.max))
+        top = jnp.max(tops, axis=0, keepdims=True)
         shrink = jnp.exp2(near_top - top)
         total = total_ref[r] * shrink
         acc = acc_ref[r] * shrink
+        for lo, hi in parts:
+            weights = jnp.exp2(s_buf[lo * TILE : hi * TILE] - top)
+            total = total + fold(weights, jnp.sum)
+            w_buf[lo * TILE : hi * TILE] = weights.astype(jnp.bfloat16)
         if width:
-            weights = jnp.exp2(s_buf[: width * TILE] - top)
-            s_buf[: width * TILE] = weights
-            total = total + fold(weights, jnp.sum)
-            acc = acc + dot(joined([vt_s[t] for t in tiles], 1), weights.astype(jnp.bfloat16))
+            acc = acc + dot(joined([vt_s[t] for t in tiles], 1), w_buf[: width * TILE])
         total = jnp.sum(total, axis=0, keepdims=True)
-        inverse = 1.0 / total
-        attended = (acc * inverse).astype(jnp.bfloat16)
+        attended = (acc * (1.0 / total)).astype(jnp.bfloat16)
         ot_ref[r] = attended
-        delta = attended.astype(jnp.float32) * upstream_t
+        delta = attended.astype(jnp.float32) * upstream.astype(jnp.float32)
         delta = jnp.sum(fold(delta, jnp.sum), axis=0, keepdims=True)
-        lse_ref[r] = spread(top + jnp.log2(total))
+        lse = top + jnp.log2(total)
+        lse_ref[r] = spread(lse)
         delta_ref[r] = spread(delta)
-        if width:
-            probs = s_buf[: width * TILE] * inverse
-            grad_probs = dot(joined(halves(kv_s, 1, tiles), 0), upt_ref[r])
+        for lo, hi in parts:
+            probs = jnp.exp2(s_buf[lo * TILE : hi * TILE] - lse)
+            grad_probs = dot(joined(halves(kv_s, 1, tiles[lo:hi]), 0), upstream)
             grad_scores = (probs * (grad_probs - delta)).astype(jnp.bfloat16)
-            grad_value = dot_nt(probs.astype(jnp.bfloat16), upt_ref[r])
+            grad_value = dot_nt(probs.astype(jnp.bfloat16), upstream)
             grad_key = dot(grad_scores, query)
-            for u, t in enumerate(tiles):
+            for u, t in enumerate(tiles[lo:hi]):
                 for half in range(2):
                     part = slice(u * TILE + half * HALF, u * TILE + (half + 1) * HALF)
                     dv_s[t + 3 * half] += grad_value[part]
@@ -377,18 +381,23 @@
         out_ref[r, :, 0:HD] = attended[:, :TILE].T.astype(jnp.bfloat16)
         out_ref[r, :, HD : 2 * HD] = attended[:, TILE:].T.astype(jnp.bfloat16)
 
-        count, tiles = own_tiles(plan_ref, r)
-        scores = dot_nt(joined([own_s[0, t] for t in tiles], 0), query) * SCORE_SCALE
-        scores = jnp.where(own_seen(count), scores, FLOOR)
-        probs, grad_scores = score_gradients(
-            scores, joined([own_s[1, t] for t in tiles], 0), upstream, lse, delta
-        )
-        grad_value = dot(probs.astype(jnp.bfloat16), upstream)
-        grad_key = dot(grad_scores, query)
-        for u, t in enumerate(tiles):
-            dv_s[t] += grad_value[u * TILE : (u + 1) * TILE]
-            dk_s[t] += grad_key[u * TILE : (u + 1) * TILE]
-        dq_s[...] = dot(joined([kt_s[t] for t in tiles], 1), grad_scores)
+        def own(width):
+            count, tiles = own_tiles(plan_ref, r, width)
+            scores = dot_nt(joined([own_s[0, t] for t in tiles], 0), query) * SCORE_SCALE
+            scores = jnp.where(own_seen(count, width), scores, FLOOR)
+            probs, grad_scores = score_gradients(
+                scores, joined([own_s[1, t] for t in tiles], 0), upstream, lse, delta
+            )
+            grad_value = dot(probs.astype(jnp.bfloat16), upstream)
+            grad_key = dot(grad_scores, query)
+            for u, t in enumerate(tiles):
+                dv_s[t] += grad_value[u * TILE : (u + 1) * TILE]
+                dk_s[t] += grad_key[u * TILE : (u + 1) * TILE]
+            dq_s[...] = dot(joined([kt_s[t] for t in tiles], 1), grad_scores)
+
+        pairs = lax.shift_right_logical(plan_ref[r, OWN_COUNT] + 2, 1)
+        for width in range(2, BT + 1, 2):
+            pl.when(pairs == width // 2)(functools.partial(own, width))
 
         @pl.when(r < EARLY)
         def _():
@@ -493,9 +502,10 @@
             shape((BT, 8, WIDE), F32),
             shape((BT, HD, WIDE), F32),
             shape((BT, HD, WIDE), BF16),
+            shape((BT, WIDE, HD), BF16),
         ),
         in_specs=[SMEM, ANY, VMEM, VMEM],
-        out_specs=(SMEM, VMEM, VMEM, VMEM, VMEM),
+        out_specs=(SMEM, VMEM, VMEM, VMEM, VMEM, VMEM),
         scratch_shapes=[
             pltpu.VMEM((2, BT, TILE, HD), BF16),
             pltpu.VMEM((BT, HD, TILE), BF16),
@@ -507,7 +517,7 @@
     )(order, mask, rows, other)
 
 
-def far_part(plan, rows, far, came, top, total, acc, upt):
+def far_part(plan, far, came, top, total, acc, upt, qs):
     return pl.pallas_call(
         far_kernel,
         out_shape=(
@@ -523,12 +533,13 @@
             pltpu.VMEM((2, 2 * FAR, HALF, HD), BF16),
             pltpu.VMEM((2 * FAR, HD, TILE), BF16),
             pltpu.VMEM((FAR * TILE, WIDE), F32),
+            pltpu.VMEM((FAR * TILE, WIDE), BF16),
             pltpu.VMEM((2 * FAR, HALF, HD), F32),
             pltpu.VMEM((2 * FAR, HALF, HD), F32),
         ],
         compiler_params=limit(60),
         cost_estimate=cost(25),
-    )(plan, rows, far, came, top, total, acc, upt)
+    )(plan, far, came, top, total, acc, upt, qs)
 
 
 def rest_part(plan, rows, other, far, came, ot, lse, delta):
@@ -618,7 +629,7 @@
     far, *begun = lax.optimization_barrier((far, *begun))
     plan = begun[0]
     came = to_other_core(far)
-    keep, send, ot, lse, delta = far_part(plan, rows, far, came, *begun[1:])
+    keep, send, ot, lse, delta = far_part(plan, far, came, *begun[1:])
     dfar = simple(pair_sum_kernel, shape((2 * FAR, HALF, HD), BF16), keep, to_other_core(send))
     parts = over_blocks(dfar.reshape(NB, 3, HALF, HD))
     out, keep, send, part = rest_part(plan, rows, other, far, came, ot, lse, delta)

time: 168 us -> 163 us (0.970)
  Pallas kernels: 68.6 us -> 65.9 us
  starting transfers between devices: 25.2 us -> 23.4 us
    pallas_call x1, Pallas kernels: 23.7 us -> 21.8 us  [far_part(): pl.pallas_call(far_kernel, out_shape=(shape((2 * FAR, HALF, HD), BF16), s...]
    all_to_all x3, starting transfers between devices: 15.2 us -> 13.4 us  [over_blocks(): lax.all_to_all(array, ('blk', 'head'), split_axis=0, concat_axis=0, axis_...]
where the time goes in v4:
time: 163 us
  Pallas kernels  65.9 us (40%)
  blocking collectives  58.4 us (36%)
  starting transfers between devices  23.4 us (14%)
  waiting for transfers between devices  9.36 us (6%)
  local copies, waits for them, and re-layouts  4.77 us (3%)
    all_to_all x2, blocking collectives, over_heads(): lax.all_to_all(array, 'head', split_axis=0, concat_axis=0, tiled=True)  43.7 us
    pallas_call x1, Pallas kernels, far_part(): pl.pallas_call(far_kernel, out_shape=(shape((2 * FAR, HALF, HD), BF16), s...  21.8 us
    pallas_call x1, Pallas kernels, rest_part(): pl.pallas_call(rest_kernel, out_shape=(shape((BT, TILE, 640), BF16), shap...  17.9 us
    all_to_all x1, blocking collectives, over_blocks(): lax.all_to_all(array, ('blk', 'head'), split_axis=0, concat_axis=0, axis_...  14.8 us
    all_to_all x3, starting transfers between devices, over_blocks(): lax.all_to_all(array, ('blk', 'head'), split_axis=0, concat_axis=0, axis_...  13.4 us
    pallas_call x1, Pallas kernels, near(): pl.pallas_call(near_kernel, out_shape=(shape((BT, PLAN), jnp.int32), shap...  10.6 us
    ppermute x6, starting transfers between devices, to_other_core(): return lax.ppermute(array, 'blk', [(i, i ^ 1) for i in range(16)])  10 us
    ppermute x6, waiting for transfers between devices, to_other_core(): return lax.ppermute(array, 'blk', [(i, i ^ 1) for i in range(16)])  7.7 us
  transfers between devices with their start and end apart: 9, of which 5 were waited for; matrix products, arithmetic and copies ran while one was open for 0% of the time, Pallas kernels for 23%

profile of v4, /device:TPU:1, one launch (start us, length us, event | category | flops | bytes accessed | tf_op | source)
XLA Modules:
  0.0 162.6 jit_solution(3178357996032540899)
XLA Ops:
  0.6 2.5 %shard_map.93 = (bf16[4,128,640]{2,1,0:T(8,128)(2,1)}, bf16[4,128,640]{2,1,0:T(8,128)(2,1)}) custom-call(bf16[128,2048]{1,0:T(8,128)(2,1)} %bitcast.23, bf16[128,2048]{1,0:T(8,128)(2,1)} %bitcast.24, bf16[128,512]{1,0:T(8,128)(2,1)} %bitcast.25, bf16[128,512]{1,0:T(8,128)(2,1)} %bitcast.26), custom_call_target="tpu_custom_call" | custom-call | tf_op jit(solution)/shard_map/pallas_call | solution.py:459
  3.2 1.5 collective-permute-start
  4.7 1.9 %collective-permute-done.came_ref = bf16[4,128,640]{2,1,0:T(8,128)(2,1)S(1)} collective-permute-done((bf16[4,128,640]{2,1,0:T(8,128)(2,1)}, bf16[4,128,640]{2,1,0:T(8,128)(2,1)S(1)}, u32[]{:S(2)}, u32[]{:S(2)}) %collective-permute-start) | collective-permute-done | bytes 655392 | tf_op jit(solution)/shard_map/ppermute | solution.py:615
  6.6 1.1 copy-done.2
  7.7 0.1 shard_map.94
  7.8 23.1 %all_to_all.30.rows_ref = bf16[8,128,640]{2,1,0:T(8,128)(2,1)S(1)} all-to-all(bf16[8,128,640]{2,1,0:T(8,128)(2,1)S(1)} %shard_map.94), channel_id=1, replica_groups=mesh['blk'=16,'head'=8] {'head'}, dimensions={0} | all-to-all | bytes 2621440 | tf_op jit(solution)/shard_map/all_to_all | solution.py:598
  31.0 2.2 %collective-permute-start.1 = (bf16[8,128,128]{2,1,0:T(8,128)(2,1)S(1)}, bf16[8,128,128]{2,1,0:T(8,128)(2,1)S(1)}, u32[]{:S(2)}, u32[]{:S(2)}) collective-permute-start(bf16[8,128,128]{2,1,0:T(8,128)(2,1)S(1)} %slice.4), channel_id=1, source_target_pairs={{0,8},{8,0},{16,24},{24,16},{32,40},{40,32},{48,56},{56,48},{64,72... | collective-permute-start | bytes 786440 | tf_op jit(solution)/shard_map/ppermute | solution.py:615
  33.2 14.8 %all_to_all.31.pieces_ref = bf16[16,64,128]{2,1,0:T(8,128)(2,1)S(1)} all-to-all(bf16[16,64,128]{2,1,0:T(8,128)(2,1)S(1)} %bitcast.18), channel_id=1, replica_groups={{0,4,16,20,32,36,48,52,64,68,80,84,96,100,112,116},{1,5,17,21,33,37,49,..., dimensions={0} | all-to-all | bytes 524288 | tf_op jit(solution)/shard_map/all_to_all | solution.py:609
  48.0 1.7 %shard_map.95 = bf16[16,3,64,128]{3,2,1,0:T(8,128)(2,1)} custom-call(s32[128]{0:T(128)S(1)} %bitcast.16, bf16[16,64,128]{2,1,0:T(8,128)(2,1)S(1)} %all_to_all.31.pieces_ref), custom_call_target="tpu_custom_call" | custom-call | tf_op jit(solution)/shard_map/pallas_call | solution.py:587
  49.6 3.6 %all-to-all-start.2 = ((bf16[16,3,64,128]{3,2,1,0:T(8,128)(2,1)}), bf16[16,3,64,128]{3,2,1,0:T(8,128)(2,1)S(1)}, u32[]{:S(2)}, u32[]{:S(2)}) async-start(bf16[16,3,64,128]{3,2,1,0:T(8,128)(2,1)} %shard_map.95), calls=%async_computation.2 | async-start | bytes 1572864 | tf_op jit(solution)/shard_map/all_to_all | solution.py:609
  53.3 0.7 copy-done.10
  54.0 10.6 %shard_map.96 = (s32[8,64]{1,0:T(8,128)}, f32[8,8,256]{2,1,0:T(8,128)}, f32[8,8,256]{2,1,0:T(8,128)}, f32[8,128,256]{2,1,0:T(8,128)}, bf16[8,128,256]{2,1,0:T(8,128)(2,1)}, /*index=5*/bf16[8,256,128]{2,1,0:T(8,128)(2,1)}) custom-call(s32[128]{0:T(128)} %bitcast.15, s32[128,128]{1,0:T(8,128)} %bitcast.31, bf16[8,128,640]{2,1,0:T(8,128)(2,1)} %copy-done.7, ...), custom_call_target="tpu_custom_call" | custom-call | flops 12000000000 | bytes 1200000 | tf_op jit(solution)/shard_map/pallas_call | solution.py:497
  64.6 1.7 %all-to-all-done.2 = bf16[16,3,64,128]{3,2,1,0:T(8,128)(2,1)S(1)} async-done(((bf16[16,3,64,128]{3,2,1,0:T(8,128)(2,1)}), bf16[16,3,64,128]{3,2,1,0:T(8,128)(2,1)S(1)}, u32[]{:S(2)}, u32[]{:S(2)}) %all-to-all-start.2) | async-done | bytes 786464 | tf_op jit(solution)/shard_map/all_to_all | solution.py:609
  66.2 2.4 %collective-permute-start.2 = (bf16[48,64,128]{2,1,0:T(8,128)(2,1)S(1)}, bf16[48,64,128]{2,1,0:T(8,128)(2,1)S(1)}, u32[]{:S(2)}, u32[]{:S(2)}) collective-permute-start(bf16[48,64,128]{2,1,0:T(8,128)(2,1)S(1)} %bitcast.19), channel_id=1, source_target_pairs={{0,8},{8,0},{16,24},{24,16},{32,40},{40,32},{48,56},{56,48},{64,72... | collective-permute-start | bytes 2359304 | tf_op jit(solution)/shard_map/ppermute | solution.py:615
  68.6 1.9 %collective-permute-done.2.came_ref = bf16[48,64,128]{2,1,0:T(8,128)(2,1)S(1)} collective-permute-done((bf16[48,64,128]{2,1,0:T(8,128)(2,1)S(1)}, bf16[48,64,128]{2,1,0:T(8,128)(2,1)S(1)}, u32[]{:S(2)}, u32[]{:S(2)}) %collective-permute-start.2) | collective-permute-done | bytes 786464 | tf_op jit(solution)/shard_map/ppermute | solution.py:615
  70.5 0.9 copy-done.9
  71.4 21.8 %shard_map.97 = (bf16[48,64,128]{2,1,0:T(8,128)(2,1)}, bf16[48,64,128]{2,1,0:T(8,128)(2,1)}, bf16[8,128,256]{2,1,0:T(8,128)(2,1)}, f32[8,8,256]{2,1,0:T(8,128)}, f32[8,8,256]{2,1,0:T(8,128)}) custom-call(s32[8,64]{1,0:T(8,128)} %get-tuple-element.47.plan_ref, bf16[48,64,128]{2,1,0:T(8,128)(2,1)} %bitcast.20, bf16[48,64,128]{2,1,0:T(8,128)(2,1)} %copy-done.9, ...), custom_call_target="tpu_custom_call" | custom-call | flops 24999999488 | bytes 2500000 | tf_op jit(solution)/shard_map/pallas_call | solution.py:521
  93.2 0.4 collective-permute-start.3
  93.6 2.1 %collective-permute-done.3.came_ref = bf16[48,64,128]{2,1,0:T(8,128)(2,1)S(1)} collective-permute-done((bf16[48,64,128]{2,1,0:T(8,128)(2,1)}, bf16[48,64,128]{2,1,0:T(8,128)(2,1)S(1)}, u32[]{:S(2)}, u32[]{:S(2)}) %collective-permute-start.3) | collective-permute-done | bytes 786464 | tf_op jit(solution)/shard_map/ppermute | solution.py:615
  95.7 1.1 copy-done.1
  96.9 1.1 shard_map.98
  97.9 4.0 %all-to-all-start.3 = ((bf16[16,3,64,128]{3,2,1,0:T(8,128)(2,1)}), bf16[16,3,64,128]{3,2,1,0:T(8,128)(2,1)S(1)}, u32[]{:S(2)}, u32[]{:S(2)}) async-start(bf16[16,3,64,128]{3,2,1,0:T(8,128)(2,1)} %bitcast.8), calls=%async_computation.3 | async-start | bytes 1572864 | tf_op jit(solution)/shard_map/all_to_all | solution.py:609
  101.9 17.9 %shard_map.99 = (bf16[8,128,640]{2,1,0:T(8,128)(2,1)}, f32[8,128,128]{2,1,0:T(8,128)}, bf16[8,128,128]{2,1,0:T(8,128)(2,1)}, f32[3,128,256]{2,1,0:T(8,128)}) custom-call(s32[8,64]{1,0:T(8,128)} %get-tuple-element.47.plan_ref, bf16[8,128,640]{2,1,0:T(8,128)(2,1)} %copy-done.7, bf16[8,128,128]{2,1,0:T(8,128)(2,1)} %copy-done.10, ...), custom_call_target="tpu_custom_call" | custom-call | flops 17999998976 | bytes 1800000 | tf_op jit(solution)/shard_map/pallas_call | solution.py:546
  119.8 1.6 %shard_map.100 = bf16[16,64,128]{2,1,0:T(8,128)(2,1)} custom-call(s32[128]{0:T(128)S(1)} %bitcast.17, bf16[16,3,64,128]{3,2,1,0:T(8,128)(2,1)S(1)} %all-to-all-done.3.parts_ref), custom_call_target="tpu_custom_call" | custom-call | tf_op jit(solution)/shard_map/pallas_call | solution.py:587
  121.4 5.8 %all-to-all-start.4 = ((bf16[16,64,128]{2,1,0:T(8,128)(2,1)}), bf16[16,64,128]{2,1,0:T(8,128)(2,1)S(1)}, u32[]{:S(2)}, u32[]{:S(2)}) async-start(bf16[16,64,128]{2,1,0:T(8,128)(2,1)} %shard_map.100), calls=%async_computation.4 | async-start | bytes 524288 | tf_op jit(solution)/shard_map/all_to_all | solution.py:609
  127.2 1.3 collective-permute-start.4
  128.5 7.2 %shard_map.101.late_ref = bf16[3,128,256]{2,1,0:T(8,128)(2,1)} custom-call(s32[8,64]{1,0:T(8,128)} %get-tuple-element.47.plan_ref, bf16[8,128,640]{2,1,0:T(8,128)(2,1)} %copy-done.7, bf16[48,64,128]{2,1,0:T(8,128)(2,1)} %bitcast.22, bf16[48,64,128]{2,1,0:T(8,128)(2,1)} %copy-done.9, f32[8,8,256]{2,1,0:T(8,128)} %get-tuple-element.57.lse_ref, ...), custom_call_target="tpu_custom_call" | custom-call | flops 10000000000 | bytes 1000000 | tf_op jit(solution)/shard_map/pallas_call | solution.py:571
  135.8 0.9 copy-done.4
  136.8 20.6 %all_to_all.32.back_ref = bf16[8,128,640]{2,1,0:T(8,128)(2,1)S(1)} all-to-all(bf16[8,128,640]{2,1,0:T(8,128)(2,1)S(1)} %shard_map.102), channel_id=1, replica_groups=mesh['blk'=16,'head'=8] {'head'}, dimensions={0} | all-to-all | bytes 2621440 | tf_op jit(solution)/shard_map/all_to_all | solution.py:598
  157.5 2.2 %collective-permute-start.5 = (bf16[4,128,640]{2,1,0:T(8,128)(2,1)S(1)}, bf16[4,128,640]{2,1,0:T(8,128)(2,1)S(1)}, u32[]{:S(2)}, u32[]{:S(2)}) collective-permute-start(bf16[4,128,640]{2,1,0:T(8,128)(2,1)S(1)} %shard_map.103), channel_id=1, source_target_pairs={{0,8},{8,0},{16,24},{24,16},{32,40},{40,32},{48,56},{56,48},{64,72... | collective-permute-start | bytes 1966088 | tf_op jit(solution)/shard_map/ppermute | solution.py:615
  159.7 1.7 %collective-permute-done.5.came_ref = bf16[4,128,640]{2,1,0:T(8,128)(2,1)S(1)} collective-permute-done((bf16[4,128,640]{2,1,0:T(8,128)(2,1)S(1)}, bf16[4,128,640]{2,1,0:T(8,128)(2,1)S(1)}, u32[]{:S(2)}, u32[]{:S(2)}) %collective-permute-start.5) | collective-permute-done | bytes 655392 | tf_op jit(solution)/shard_map/ppermute | solution.py:615
  161.4 1.2 shard_map.104
  (26 shorter events, 0.3 us)
Async XLA Ops:
  3.2 3.4 %collective-permute-start = (bf16[4,128,640]{2,1,0:T(8,128)(2,1)}, bf16[4,128,640]{2,1,0:T(8,128)(2,1)S(1)}, u32[]{:S(2)}, u32[]{:S(2)}) collective-permute-start(bf16[4,128,640]{2,1,0:T(8,128)(2,1)} %get-tuple-element.40), channel_id=1, source_target_pairs={{0,8},{8,0},{16,24},{24,16},{32,40},{40,32},{48,56},{56,48},{64,72... | collective-permute-start | bytes 1966088 | tf_op jit(solution)/shard_map/ppermute | solution.py:615
  6.6 1.1 copy-start.2
  7.8 40.1 %copy-start.5 = (s32[1,128]{1,0:T(1,128)S(1)}, s32[1,128]{1,0:T(1,128)}, u32[]{:S(2)}) copy-start(s32[1,128]{1,0:T(1,128)} %param.11) | copy-start | bytes 1540
  30.9 18.7 %copy-start.7 = (bf16[8,128,640]{2,1,0:T(8,128)(2,1)}, bf16[8,128,640]{2,1,0:T(8,128)(2,1)S(1)}, u32[]{:S(2)}) copy-start(bf16[8,128,640]{2,1,0:T(8,128)(2,1)S(1)} %all_to_all.30.rows_ref) | copy-start | bytes 3932164
  31.0 22.3 %collective-permute-start.1 = (bf16[8,128,128]{2,1,0:T(8,128)(2,1)S(1)}, bf16[8,128,128]{2,1,0:T(8,128)(2,1)S(1)}, u32[]{:S(2)}, u32[]{:S(2)}) collective-permute-start(bf16[8,128,128]{2,1,0:T(8,128)(2,1)S(1)} %slice.4), channel_id=1, source_target_pairs={{0,8},{8,0},{16,24},{24,16},{32,40},{40,32},{48,56},{56,48},{64,72... | collective-permute-start | bytes 786440 | tf_op jit(solution)/shard_map/ppermute | solution.py:615
  49.6 16.6 %all-to-all-start.2 = ((bf16[16,3,64,128]{3,2,1,0:T(8,128)(2,1)}), bf16[16,3,64,128]{3,2,1,0:T(8,128)(2,1)S(1)}, u32[]{:S(2)}, u32[]{:S(2)}) async-start(bf16[16,3,64,128]{3,2,1,0:T(8,128)(2,1)} %shard_map.95), calls=%async_computation.2 | async-start | bytes 1572864 | tf_op jit(solution)/shard_map/all_to_all | solution.py:609
  53.3 0.7 copy-start.10
  66.2 4.3 %copy-start.8 = (bf16[16,3,64,128]{3,2,1,0:T(8,128)(2,1)}, bf16[16,3,64,128]{3,2,1,0:T(8,128)(2,1)S(1)}, u32[]{:S(2)}) copy-start(bf16[16,3,64,128]{3,2,1,0:T(8,128)(2,1)S(1)} %all-to-all-done.2) | copy-start | bytes 2359300
  66.2 4.3 %collective-permute-start.2 = (bf16[48,64,128]{2,1,0:T(8,128)(2,1)S(1)}, bf16[48,64,128]{2,1,0:T(8,128)(2,1)S(1)}, u32[]{:S(2)}, u32[]{:S(2)}) collective-permute-start(bf16[48,64,128]{2,1,0:T(8,128)(2,1)S(1)} %bitcast.19), channel_id=1, source_target_pairs={{0,8},{8,0},{16,24},{24,16},{32,40},{40,32},{48,56},{56,48},{64,72... | collective-permute-start | bytes 2359304 | tf_op jit(solution)/shard_map/ppermute | solution.py:615
  70.5 0.9 copy-start.9
  93.2 2.5 %collective-permute-start.3 = (bf16[48,64,128]{2,1,0:T(8,128)(2,1)}, bf16[48,64,128]{2,1,0:T(8,128)(2,1)S(1)}, u32[]{:S(2)}, u32[]{:S(2)}) collective-permute-start(bf16[48,64,128]{2,1,0:T(8,128)(2,1)} %get-tuple-element.55), channel_id=1, source_target_pairs={{0,8},{8,0},{16,24},{24,16},{32,40},{40,32},{48,56},{56,48},{64,72... | collective-permute-start | bytes 2359304 | tf_op jit(solution)/shard_map/ppermute | solution.py:615
  95.7 1.1 copy-start.1
  97.9 21.8 %all-to-all-start.3 = ((bf16[16,3,64,128]{3,2,1,0:T(8,128)(2,1)}), bf16[16,3,64,128]{3,2,1,0:T(8,128)(2,1)S(1)}, u32[]{:S(2)}, u32[]{:S(2)}) async-start(bf16[16,3,64,128]{3,2,1,0:T(8,128)(2,1)} %bitcast.8), calls=%async_computation.3 | async-start | bytes 1572864 | tf_op jit(solution)/shard_map/all_to_all | solution.py:609
  101.9 17.9 %copy-start.6 = (s32[1,128]{1,0:T(1,128)S(1)}, s32[1,128]{1,0:T(1,128)}, u32[]{:S(2)}) copy-start(s32[1,128]{1,0:T(1,128)} %param.11) | copy-start | bytes 1540
  119.8 7.4 %copy-start.11 = (bf16[8,128,128]{2,1,0:T(8,128)(2,1)S(1)}, bf16[8,128,128]{2,1,0:T(8,128)(2,1)}, u32[]{:S(2)}) copy-start(bf16[8,128,128]{2,1,0:T(8,128)(2,1)} %get-tuple-element.68) | copy-start | bytes 786436
  121.4 14.4 %all-to-all-start.4 = ((bf16[16,64,128]{2,1,0:T(8,128)(2,1)}), bf16[16,64,128]{2,1,0:T(8,128)(2,1)S(1)}, u32[]{:S(2)}, u32[]{:S(2)}) async-start(bf16[16,64,128]{2,1,0:T(8,128)(2,1)} %shard_map.100), calls=%async_computation.4 | async-start | bytes 524288 | tf_op jit(solution)/shard_map/all_to_all | solution.py:609
  127.2 8.6 %copy-start = (bf16[8,128,640]{2,1,0:T(8,128)(2,1)S(1)}, bf16[8,128,640]{2,1,0:T(8,128)(2,1)}, u32[]{:S(2)}) copy-start(bf16[8,128,640]{2,1,0:T(8,128)(2,1)} %get-tuple-element.63.rows_ref) | copy-start | bytes 3932164
  127.2 8.6 %copy-start.3 = (f32[8,128,128]{2,1,0:T(8,128)S(1)}, f32[8,128,128]{2,1,0:T(8,128)}, u32[]{:S(2)}) copy-start(f32[8,128,128]{2,1,0:T(8,128)} %get-tuple-element.67.keep_ref) | copy-start | bytes 1572868
  127.2 8.5 %collective-permute-start.4 = (bf16[8,128,128]{2,1,0:T(8,128)(2,1)S(1)}, bf16[8,128,128]{2,1,0:T(8,128)(2,1)S(1)}, u32[]{:S(2)}, u32[]{:S(2)}) collective-permute-start(bf16[8,128,128]{2,1,0:T(8,128)(2,1)S(1)} %copy-done.11), channel_id=1, source_target_pairs={{0,8},{8,0},{16,24},{24,16},{32,40},{40,32},{48,56},{56,48},{64,72... | collective-permute-start | bytes 786440 | tf_op jit(solution)/shard_map/ppermute | solution.py:615
  135.8 0.9 copy-start.4
  157.5 3.9 %collective-permute-start.5 = (bf16[4,128,640]{2,1,0:T(8,128)(2,1)S(1)}, bf16[4,128,640]{2,1,0:T(8,128)(2,1)S(1)}, u32[]{:S(2)}, u32[]{:S(2)}) collective-permute-start(bf16[4,128,640]{2,1,0:T(8,128)(2,1)S(1)} %shard_map.103), channel_id=1, source_target_pairs={{0,8},{8,0},{16,24},{24,16},{32,40},{40,32},{48,56},{56,48},{64,72... | collective-permute-start | bytes 1966088 | tf_op jit(solution)/shard_map/ppermute | solution.py:615

commit v5 on v4

--- a/solution.py
+++ b/solution.py
@@ -16,8 +16,6 @@
 FAR = 24
 HALF = 64
 EARLY = 5
-WORK = 8
-REST = 4
 SUB = 4
 STEP = 4
 INV_ROOT = 1.0 / math.sqrt(HD)
@@ -104,11 +102,6 @@
         dv_ref[:, g * HD : (g + 1) * HD] = jnp.where(me == 0, b, a)
 
 
-def pair_sum_kernel(keep_ref, came_ref, out_ref):
-    total = keep_ref[...].astype(jnp.float32) + came_ref[...].astype(jnp.float32)
-    out_ref[...] = total.astype(jnp.bfloat16)
-
-
 def add_kernel(rows_ref, late_ref, keep_ref, came_ref, home_ref, out_ref):
     out_ref[EARLY:, :, 256:512] = late_ref[...]
     total = keep_ref[...] + came_ref[...].astype(jnp.float32) + home_ref[...].astype(jnp.float32)
@@ -160,9 +153,9 @@
     return joined([rows_ref[r, :, lo : lo + HD], rows_ref[r, :, lo + HD : lo + 2 * HD]], 0)
 
 
-def own_seen(count, width):
-    k_pos = lax.broadcasted_iota(jnp.int32, (width * TILE, WIDE), 0)
-    q_pos = lax.broadcasted_iota(jnp.int32, (width * TILE, WIDE), 1) % TILE
+def own_seen(count, lo, hi):
+    k_pos = lax.broadcasted_iota(jnp.int32, ((hi - lo) * TILE, WIDE), 0) + lo * TILE
+    q_pos = lax.broadcasted_iota(jnp.int32, ((hi - lo) * TILE, WIDE), 1) % TILE
     limit = jnp.where(k_pos < TILE, q_pos + 1, (count + 1) * TILE)
     return k_pos < limit
 
@@ -208,41 +201,22 @@
     def _(r):
         query = stacked(rows_ref, r, 0)
         qs_ref[r] = query
-        count, tiles = own_tiles(plan_ref, r, BT)
-        scores = dot_nt(joined([own_s[0, t] for t in tiles], 0), query) * SCORE_SCALE
-        scores = jnp.where(own_seen(count, BT), scores, FLOOR)
-        top = jnp.max(fold(scores, jnp.max), axis=0, keepdims=True)
-        weights = jnp.exp2(scores - top)
-        top_ref[r] = spread(top)
-        total_ref[r] = fold(weights, jnp.sum)
-        acc_ref[r] = dot(joined([vt_s[t] for t in tiles], 1), weights.astype(jnp.bfloat16))
+
+        def own(width):
+            count, tiles = own_tiles(plan_ref, r, width)
+            scores = dot_nt(joined([own_s[0, t] for t in tiles], 0), query) * SCORE_SCALE
+            scores = jnp.where(own_seen(count, 0, width), scores, FLOOR)
+            top = jnp.max(fold(scores, jnp.max), axis=0, keepdims=True)
+            weights = jnp.exp2(scores - top)
+            top_ref[r] = spread(top)
+            total_ref[r] = fold(weights, jnp.sum)
+            acc_ref[r] = dot(joined([vt_s[t] for t in tiles], 1), weights.astype(jnp.bfloat16))
+
+        pairs = lax.shift_right_logical(plan_ref[r, OWN_COUNT] + 2, 1)
+        for width in range(2, BT + 1, 2):
+            pl.when(pairs == width // 2)(functools.partial(own, width))
+
         upt_ref[r] = joined([rows_ref[r, :, 256:384].T, rows_ref[r, :, 384:512].T], 1)
-
-
-def far_steps(plan_ref, r, step):
-    count = plan_ref[r, FAR_COUNT]
-    whole = lax.shift_right_logical(count, 3)
-    rest = count & (WORK - 1)
-
-    @pl.loop(0, whole)
-    def _(g):
-        step(g * WORK, [plan_ref[r, FAR_LIST + g * WORK + u] for u in range(WORK)], None)
-
-    def partly(width):
-        base = whole * WORK
-        tiles = [
-            jnp.where(u < rest, plan_ref[r, FAR_LIST + jnp.minimum(base + u, FAR - 1)], 0)
-            for u in range(width)
-        ]
-        step(base, tiles, rest)
-
-    @pl.when(rest > REST)
-    def _():
-        partly(WORK)
-
-    @pl.when((rest > 0) & (rest <= REST))
-    def _():
-        partly(REST)
 
 
 def halves(ref, part, tiles):
@@ -250,8 +224,6 @@
 
 
 def only(scores, live):
-    if live is None:
-        return scores
     row = lax.broadcasted_iota(jnp.int32, scores.shape, 0)
     return jnp.where(row < live * TILE, scores, FLOOR)
 
@@ -272,18 +244,15 @@
             vt_s[t * 6 + j] = joined(halves(kv_s, 1, [t * 6 + j]), 0).T
 
     def work(r, width):
-        count = plan_ref[r, FAR_COUNT]
-        listed = [plan_ref[r, FAR_LIST + u] for u in range(width)]
-        sure = width - STEP
-        tiles = [t if u <= sure else jnp.where(u < count, t, 0) for u, t in enumerate(listed)]
-        parts = [(lo, min(lo + SUB, width)) for lo in range(0, width, SUB)]
+        count, tiles = listed_tiles(plan_ref, r, width)
+        parts = parts_of(width)
         query = qs_ref[r]
         upstream = upt_ref[r]
         near_top = top_ref[r][:1]
         tops = top_ref[r]
         for lo, hi in parts:
             scores = dot_nt(joined(halves(kv_s, 0, tiles[lo:hi]), 0), query) * SCORE_SCALE
-            if hi > sure + 1:
+            if hi > width - STEP + 1:
                 scores = only(scores, count - lo)
             s_buf[lo * TILE : hi * TILE] = scores
             tops = jnp.maximum(tops, fold(scores, jnp.max))
@@ -322,9 +291,7 @@
 
     @pl.loop(0, BT)
     def _(r):
-        steps = lax.shift_right_logical(plan_ref[r, FAR_COUNT] + STEP - 1, 2)
-        for width in range(0, FAR + 1, STEP):
-            pl.when(steps == width // STEP)(functools.partial(work, r, width))
+        by_width(plan_ref, r, functools.partial(work, r), 0)
 
     grad_key = (dk_s[...] * INV_ROOT).astype(jnp.bfloat16)
     grad_value = dv_s[...].astype(jnp.bfloat16)
@@ -338,14 +305,35 @@
     return probs, (probs * (grad_probs - delta)).astype(jnp.bfloat16)
 
 
+def listed_tiles(plan_ref, r, width):
+    count = plan_ref[r, FAR_COUNT]
+    listed = [plan_ref[r, FAR_LIST + u] for u in range(width)]
+    sure = width - STEP
+    return count, [t if u <= sure else jnp.where(u < count, t, 0) for u, t in enumerate(listed)]
+
+
+def parts_of(width):
+    return [(lo, min(lo + SUB, width)) for lo in range(0, width, SUB)]
+
+
+def by_width(plan_ref, r, work, least):
+    steps = lax.div(plan_ref[r, FAR_COUNT] + STEP - 1, STEP)
+    for width in range(least, FAR + 1, STEP):
+        pl.when(steps == width // STEP)(functools.partial(work, width))
+
+
 def far_queries(plan_ref, kv_s, fkt_s, dq_s, r, query, upstream, lse, delta):
-    def step(slot, tiles, live):
-        scores = only(dot_nt(joined(halves(kv_s, 0, tiles), 0), query) * SCORE_SCALE, live)
-        value = joined(halves(kv_s, 1, tiles), 0)
-        _, grad_scores = score_gradients(scores, value, upstream, lse, delta)
-        dq_s[...] += dot(joined([fkt_s[t] for t in tiles], 1), grad_scores)
-
-    far_steps(plan_ref, r, step)
+    def work(width):
+        count, tiles = listed_tiles(plan_ref, r, width)
+        for lo, hi in parts_of(width):
+            scores = dot_nt(joined(halves(kv_s, 0, tiles[lo:hi]), 0), query) * SCORE_SCALE
+            if hi > width - STEP + 1:
+                scores = only(scores, count - lo)
+            value = joined(halves(kv_s, 1, tiles[lo:hi]), 0)
+            _, grad_scores = score_gradients(scores, value, upstream, lse, delta)
+            dq_s[...] += dot(joined([fkt_s[t] for t in tiles[lo:hi]], 1), grad_scores)
+
+    by_width(plan_ref, r, work, STEP)
 
 
 def turned(dq_s):
@@ -383,17 +371,22 @@
 
         def own(width):
             count, tiles = own_tiles(plan_ref, r, width)
-            scores = dot_nt(joined([own_s[0, t] for t in tiles], 0), query) * SCORE_SCALE
-            scores = jnp.where(own_seen(count, width), scores, FLOOR)
-            probs, grad_scores = score_gradients(
-                scores, joined([own_s[1, t] for t in tiles], 0), upstream, lse, delta
-            )
-            grad_value = dot(probs.astype(jnp.bfloat16), upstream)
-            grad_key = dot(grad_scores, query)
-            for u, t in enumerate(tiles):
-                dv_s[t] += grad_value[u * TILE : (u + 1) * TILE]
-                dk_s[t] += grad_key[u * TILE : (u + 1) * TILE]
-            dq_s[...] = dot(joined([kt_s[t] for t in tiles], 1), grad_scores)
+            dq = None
+            for lo, hi in parts_of(width):
+                part = tiles[lo:hi]
+                scores = dot_nt(joined([own_s[0, t] for t in part], 0), query) * SCORE_SCALE
+                scores = jnp.where(own_seen(count, lo, hi), scores, FLOOR)
+                probs, grad_scores = score_gradients(
+                    scores, joined([own_s[1, t] for t in part], 0), upstream, lse, delta
+                )
+                grad_value = dot(probs.astype(jnp.bfloat16), upstream)
+                grad_key = dot(grad_scores, query)
+                for u, t in enumerate(part):
+                    dv_s[t] += grad_value[u * TILE : (u + 1) * TILE]
+                    dk_s[t] += grad_key[u * TILE : (u + 1) * TILE]
+                term = dot(joined([kt_s[t] for t in part], 1), grad_scores)
+                dq = term if dq is None else dq + term
+            dq_s[...] = dq
 
         pairs = lax.shift_right_logical(plan_ref[r, OWN_COUNT] + 2, 1)
         for width in range(2, BT + 1, 2):
@@ -630,7 +623,7 @@
     plan = begun[0]
     came = to_other_core(far)
     keep, send, ot, lse, delta = far_part(plan, far, came, *begun[1:])
-    dfar = simple(pair_sum_kernel, shape((2 * FAR, HALF, HD), BF16), keep, to_other_core(send))
+    dfar = (keep.astype(F32) + to_other_core(send).astype(F32)).astype(BF16)
     parts = over_blocks(dfar.reshape(NB, 3, HALF, HD))
     out, keep, send, part = rest_part(plan, rows, other, far, came, ot, lse, delta)
     parts, out, keep, send, part = lax.optimization_barrier((parts, out, keep, send, part))

time: 163 us -> 162 us (level)
  Pallas kernels: 65.9 us -> 60 us
  other arithmetic: 0 us -> 2.35 us
  starting transfers between devices: 23.4 us -> 25.7 us
    convert_element_type x0 -> x1, other arithmetic: none -> 2.35 us  [on_device(): dfar = (keep.astype(F32) + to_other_core(send).astype(F32)).astype(BF16)]
    all_to_all x3, starting transfers between devices: 13.4 us -> 15.3 us  [over_blocks(): lax.all_to_all(array, ('blk', 'head'), split_axis=0, concat_axis=0, axis_...]
    pallas_call x1, Pallas kernels: 17.9 us -> 15.9 us  [rest_part(): pl.pallas_call(rest_kernel, out_shape=(shape((BT, TILE, 640), BF16), shap...]
    pallas_call x1, Pallas kernels: 21.8 us -> 19.9 us  [far_part(): pl.pallas_call(far_kernel, out_shape=(shape((2 * FAR, HALF, HD), BF16), s...]
    unnamed x24 -> x22, local copies, waits for them, and re-layouts: 4.73 us -> 3.61 us
  transfers between devices with their start and end apart: 9 -> 9, of which waited for: 5 -> 5; matrix products, arithmetic and copies ran while one was open for 0% -> 0% of each run, Pallas kernels for 23% -> 21%
where the time goes in v5:
time: 162 us; the launch traced here: 161 us
  Pallas kernels  60 us (37%)
  blocking collectives  58.4 us (36%)
  starting transfers between devices  25.7 us (16%)
  waiting for transfers between devices  10.4 us (6%)
  local copies, waits for them, and re-layouts  3.65 us (2%)
  other arithmetic  2.35 us (1%)
    all_to_all x2, blocking collectives, over_heads(): lax.all_to_all(array, 'head', split_axis=0, concat_axis=0, tiled=True)  43.6 us
    pallas_call x1, Pallas kernels, far_part(): pl.pallas_call(far_kernel, out_shape=(shape((2 * FAR, HALF, HD), BF16), s...  19.9 us
    pallas_call x1, Pallas kernels, rest_part(): pl.pallas_call(rest_kernel, out_shape=(shape((BT, TILE, 640), BF16), shap...  15.9 us
    all_to_all x3, starting transfers between devices, over_blocks(): lax.all_to_all(array, ('blk', 'head'), split_axis=0, concat_axis=0, axis_...  15.3 us
    all_to_all x1, blocking collectives, over_blocks(): lax.all_to_all(array, ('blk', 'head'), split_axis=0, concat_axis=0, axis_...  14.8 us
    ppermute x6, starting transfers between devices, to_other_core(): return lax.ppermute(array, 'blk', [(i, i ^ 1) for i in range(16)])  10.4 us
    pallas_call x1, Pallas kernels, near(): pl.pallas_call(near_kernel, out_shape=(shape((BT, PLAN), jnp.int32), shap...  9.57 us
    ppermute x6, waiting for transfers between devices, to_other_core(): return lax.ppermute(array, 'blk', [(i, i ^ 1) for i in range(16)])  7.7 us
  transfers between devices with their start and end apart: 9, of which 5 were waited for; matrix products, arithmetic and copies ran while one was open for 0% of the time, Pallas kernels for 21%

profile of v5, /device:TPU:1, one launch (start us, length us, event | category | flops | bytes accessed | tf_op | source)
XLA Modules:
  0.0 161.2 jit_solution(13984419297469412982)
XLA Ops:
  0.6 2.5 %shard_map.93 = (bf16[4,128,640]{2,1,0:T(8,128)(2,1)}, bf16[4,128,640]{2,1,0:T(8,128)(2,1)}) custom-call(bf16[128,2048]{1,0:T(8,128)(2,1)} %bitcast.23, bf16[128,2048]{1,0:T(8,128)(2,1)} %bitcast.24, bf16[128,512]{1,0:T(8,128)(2,1)} %bitcast.25, bf16[128,512]{1,0:T(8,128)(2,1)} %bitcast.26), custom_call_target="tpu_custom_call" | custom-call | tf_op jit(solution)/shard_map/pallas_call | solution.py:452
  3.2 1.5 collective-permute-start
  4.7 1.9 %collective-permute-done.came_ref = bf16[4,128,640]{2,1,0:T(8,128)(2,1)S(1)} collective-permute-done((bf16[4,128,640]{2,1,0:T(8,128)(2,1)}, bf16[4,128,640]{2,1,0:T(8,128)(2,1)S(1)}, u32[]{:S(2)}, u32[]{:S(2)}) %collective-permute-start) | collective-permute-done | bytes 655392 | tf_op jit(solution)/shard_map/ppermute | solution.py:608
  6.6 1.1 copy-done.1
  7.7 0.1 shard_map.94
  7.8 23.1 %all_to_all.30.rows_ref = bf16[8,128,640]{2,1,0:T(8,128)(2,1)S(1)} all-to-all(bf16[8,128,640]{2,1,0:T(8,128)(2,1)S(1)} %shard_map.94), channel_id=1, replica_groups=mesh['blk'=16,'head'=8] {'head'}, dimensions={0} | all-to-all | bytes 2621440 | tf_op jit(solution)/shard_map/all_to_all | solution.py:591
  31.0 2.2 %collective-permute-start.1 = (bf16[8,128,128]{2,1,0:T(8,128)(2,1)S(1)}, bf16[8,128,128]{2,1,0:T(8,128)(2,1)S(1)}, u32[]{:S(2)}, u32[]{:S(2)}) collective-permute-start(bf16[8,128,128]{2,1,0:T(8,128)(2,1)S(1)} %slice.4), channel_id=1, source_target_pairs={{0,8},{8,0},{16,24},{24,16},{32,40},{40,32},{48,56},{56,48},{64,72... | collective-permute-start | bytes 786440 | tf_op jit(solution)/shard_map/ppermute | solution.py:608
  33.2 14.8 %all_to_all.31.pieces_ref = bf16[16,64,128]{2,1,0:T(8,128)(2,1)S(1)} all-to-all(bf16[16,64,128]{2,1,0:T(8,128)(2,1)S(1)} %bitcast.18), channel_id=1, replica_groups={{0,4,16,20,32,36,48,52,64,68,80,84,96,100,112,116},{1,5,17,21,33,37,49,..., dimensions={0} | all-to-all | bytes 524288 | tf_op jit(solution)/shard_map/all_to_all | solution.py:602
  48.0 1.7 %shard_map.95 = bf16[16,3,64,128]{3,2,1,0:T(8,128)(2,1)} custom-call(s32[128]{0:T(128)S(1)} %bitcast.16, bf16[16,64,128]{2,1,0:T(8,128)(2,1)S(1)} %all_to_all.31.pieces_ref), custom_call_target="tpu_custom_call" | custom-call | tf_op jit(solution)/shard_map/pallas_call | solution.py:580
  49.7 3.6 %all-to-all-start.2 = ((bf16[16,3,64,128]{3,2,1,0:T(8,128)(2,1)}), bf16[16,3,64,128]{3,2,1,0:T(8,128)(2,1)S(1)}, u32[]{:S(2)}, u32[]{:S(2)}) async-start(bf16[16,3,64,128]{3,2,1,0:T(8,128)(2,1)} %shard_map.95), calls=%async_computation.2 | async-start | bytes 1572864 | tf_op jit(solution)/shard_map/all_to_all | solution.py:602
  53.3 0.7 copy-done.9
  54.0 9.6 %shard_map.96 = (s32[8,64]{1,0:T(8,128)}, f32[8,8,256]{2,1,0:T(8,128)}, f32[8,8,256]{2,1,0:T(8,128)}, f32[8,128,256]{2,1,0:T(8,128)}, bf16[8,128,256]{2,1,0:T(8,128)(2,1)}, /*index=5*/bf16[8,256,128]{2,1,0:T(8,128)(2,1)}) custom-call(s32[128]{0:T(128)} %bitcast.15, s32[128,128]{1,0:T(8,128)} %bitcast.31, bf16[8,128,640]{2,1,0:T(8,128)(2,1)} %copy-done.6, ...), custom_call_target="tpu_custom_call" | custom-call | flops 12000000000 | bytes 1200000 | tf_op jit(solution)/shard_map/pallas_call | solution.py:490
  63.6 2.7 %all-to-all-done.2 = bf16[16,3,64,128]{3,2,1,0:T(8,128)(2,1)S(1)} async-done(((bf16[16,3,64,128]{3,2,1,0:T(8,128)(2,1)}), bf16[16,3,64,128]{3,2,1,0:T(8,128)(2,1)S(1)}, u32[]{:S(2)}, u32[]{:S(2)}) %all-to-all-start.2) | async-done | bytes 786464 | tf_op jit(solution)/shard_map/all_to_all | solution.py:602
  66.2 2.4 %collective-permute-start.2 = (bf16[48,64,128]{2,1,0:T(8,128)(2,1)S(1)}, bf16[48,64,128]{2,1,0:T(8,128)(2,1)S(1)}, u32[]{:S(2)}, u32[]{:S(2)}) collective-permute-start(bf16[48,64,128]{2,1,0:T(8,128)(2,1)S(1)} %bitcast.19), channel_id=1, source_target_pairs={{0,8},{8,0},{16,24},{24,16},{32,40},{40,32},{48,56},{56,48},{64,72... | collective-permute-start | bytes 2359304 | tf_op jit(solution)/shard_map/ppermute | solution.py:608
  68.6 1.9 %collective-permute-done.2.came_ref = bf16[48,64,128]{2,1,0:T(8,128)(2,1)S(1)} collective-permute-done((bf16[48,64,128]{2,1,0:T(8,128)(2,1)S(1)}, bf16[48,64,128]{2,1,0:T(8,128)(2,1)S(1)}, u32[]{:S(2)}, u32[]{:S(2)}) %collective-permute-start.2) | collective-permute-done | bytes 786464 | tf_op jit(solution)/shard_map/ppermute | solution.py:608
  70.5 0.9 copy-done.8
  71.4 19.9 %shard_map.97 = (bf16[48,64,128]{2,1,0:T(8,128)(2,1)}, bf16[48,64,128]{2,1,0:T(8,128)(2,1)}, bf16[8,128,256]{2,1,0:T(8,128)(2,1)}, f32[8,8,256]{2,1,0:T(8,128)}, f32[8,8,256]{2,1,0:T(8,128)}) custom-call(s32[8,64]{1,0:T(8,128)} %get-tuple-element.47.plan_ref, bf16[48,64,128]{2,1,0:T(8,128)(2,1)} %bitcast.20, bf16[48,64,128]{2,1,0:T(8,128)(2,1)} %copy-done.8, ...), custom_call_target="tpu_custom_call" | custom-call | flops 24999999488 | bytes 2500000 | tf_op jit(solution)/shard_map/pallas_call | solution.py:514
  91.3 0.4 collective-permute-start.3
  91.7 2.1 %collective-permute-done.3 = bf16[48,64,128]{2,1,0:T(8,128)(2,1)S(1)} collective-permute-done((bf16[48,64,128]{2,1,0:T(8,128)(2,1)}, bf16[48,64,128]{2,1,0:T(8,128)(2,1)S(1)}, u32[]{:S(2)}, u32[]{:S(2)}) %collective-permute-start.3) | collective-permute-done | bytes 786464 | tf_op jit(solution)/shard_map/ppermute | solution.py:608
  93.9 2.3 %add_convert_fusion = bf16[48,64,128]{2,1,0:T(8,128)(2,1)} fusion(bf16[48,64,128]{2,1,0:T(8,128)(2,1)S(1)} %collective-permute-done.3, bf16[48,64,128]{2,1,0:T(8,128)(2,1)} %get-tuple-element.54), kind=kLoop, calls=%fused_computation | loop fusion | flops 1572864 | bytes 2359296 | tf_op jit(solution)/shard_map/convert_element_type | solution.py:626
  96.2 4.8 %all-to-all-start.3 = ((bf16[16,3,64,128]{3,2,1,0:T(8,128)(2,1)}), bf16[16,3,64,128]{3,2,1,0:T(8,128)(2,1)S(1)}, u32[]{:S(2)}, u32[]{:S(2)}) async-start(bf16[16,3,64,128]{3,2,1,0:T(8,128)(2,1)} %bitcast.8), calls=%async_computation.3 | async-start | bytes 1572864 | tf_op jit(solution)/shard_map/all_to_all | solution.py:602
  101.1 15.9 %shard_map.98 = (bf16[8,128,640]{2,1,0:T(8,128)(2,1)}, f32[8,128,128]{2,1,0:T(8,128)}, bf16[8,128,128]{2,1,0:T(8,128)(2,1)}, f32[3,128,256]{2,1,0:T(8,128)}) custom-call(s32[8,64]{1,0:T(8,128)} %get-tuple-element.47.plan_ref, bf16[8,128,640]{2,1,0:T(8,128)(2,1)} %copy-done.6, bf16[8,128,128]{2,1,0:T(8,128)(2,1)} %copy-done.9, bf16[48,64,128]{2,1,0:T(8,128)(2,1)} %bitcast.21, ...), custom_call_target="tpu_custom_call" | custom-call | flops 17999998976 | bytes 1800000 | tf_op jit(solution)/shard_map/pallas_call | solution.py:539
  117.0 1.6 %shard_map.99 = bf16[16,64,128]{2,1,0:T(8,128)(2,1)} custom-call(s32[128]{0:T(128)S(1)} %bitcast.17, bf16[16,3,64,128]{3,2,1,0:T(8,128)(2,1)S(1)} %all-to-all-done.3.parts_ref), custom_call_target="tpu_custom_call" | custom-call | tf_op jit(solution)/shard_map/pallas_call | solution.py:580
  118.6 6.9 %all-to-all-start.4 = ((bf16[16,64,128]{2,1,0:T(8,128)(2,1)}), bf16[16,64,128]{2,1,0:T(8,128)(2,1)S(1)}, u32[]{:S(2)}, u32[]{:S(2)}) async-start(bf16[16,64,128]{2,1,0:T(8,128)(2,1)} %shard_map.99), calls=%async_computation.4 | async-start | bytes 524288 | tf_op jit(solution)/shard_map/all_to_all | solution.py:602
  125.5 1.5 collective-permute-start.4
  127.1 7.2 %shard_map.100.late_ref = bf16[3,128,256]{2,1,0:T(8,128)(2,1)} custom-call(s32[8,64]{1,0:T(8,128)} %get-tuple-element.47.plan_ref, bf16[8,128,640]{2,1,0:T(8,128)(2,1)} %copy-done.6, bf16[48,64,128]{2,1,0:T(8,128)(2,1)} %bitcast.22, bf16[48,64,128]{2,1,0:T(8,128)(2,1)} %copy-done.8, f32[8,8,256]{2,1,0:T(8,128)} %get-tuple-element.57.lse_ref, ...), custom_call_target="tpu_custom_call" | custom-call | flops 10000000000 | bytes 1000000 | tf_op jit(solution)/shard_map/pallas_call | solution.py:564
  134.4 0.9 copy-done.3
  135.3 0.1 shard_map.101
  135.4 20.5 %all_to_all.32.back_ref = bf16[8,128,640]{2,1,0:T(8,128)(2,1)S(1)} all-to-all(bf16[8,128,640]{2,1,0:T(8,128)(2,1)S(1)} %shard_map.101), channel_id=1, replica_groups=mesh['blk'=16,'head'=8] {'head'}, dimensions={0} | all-to-all | bytes 2621440 | tf_op jit(solution)/shard_map/all_to_all | solution.py:591
  156.0 2.3 %collective-permute-start.5 = (bf16[4,128,640]{2,1,0:T(8,128)(2,1)S(1)}, bf16[4,128,640]{2,1,0:T(8,128)(2,1)S(1)}, u32[]{:S(2)}, u32[]{:S(2)}) collective-permute-start(bf16[4,128,640]{2,1,0:T(8,128)(2,1)S(1)} %shard_map.102), channel_id=1, source_target_pairs={{0,8},{8,0},{16,24},{24,16},{32,40},{40,32},{48,56},{56,48},{64,72... | collective-permute-start | bytes 1966088 | tf_op jit(solution)/shard_map/ppermute | solution.py:608
  158.3 1.7 %collective-permute-done.5.came_ref = bf16[4,128,640]{2,1,0:T(8,128)(2,1)S(1)} collective-permute-done((bf16[4,128,640]{2,1,0:T(8,128)(2,1)S(1)}, bf16[4,128,640]{2,1,0:T(8,128)(2,1)S(1)}, u32[]{:S(2)}, u32[]{:S(2)}) %collective-permute-start.5) | collective-permute-done | bytes 655392 | tf_op jit(solution)/shard_map/ppermute | solution.py:608
  160.0 1.2 shard_map.103
  (24 shorter events, 0.1 us)
Async XLA Ops:
  3.2 3.4 %collective-permute-start = (bf16[4,128,640]{2,1,0:T(8,128)(2,1)}, bf16[4,128,640]{2,1,0:T(8,128)(2,1)S(1)}, u32[]{:S(2)}, u32[]{:S(2)}) collective-permute-start(bf16[4,128,640]{2,1,0:T(8,128)(2,1)} %get-tuple-element.40), channel_id=1, source_target_pairs={{0,8},{8,0},{16,24},{24,16},{32,40},{40,32},{48,56},{56,48},{64,72... | collective-permute-start | bytes 1966088 | tf_op jit(solution)/shard_map/ppermute | solution.py:608
  6.6 1.1 copy-start.1
  7.8 40.1 %copy-start.4 = (s32[1,128]{1,0:T(1,128)S(1)}, s32[1,128]{1,0:T(1,128)}, u32[]{:S(2)}) copy-start(s32[1,128]{1,0:T(1,128)} %param.11) | copy-start | bytes 1540
  30.9 18.8 %copy-start.6 = (bf16[8,128,640]{2,1,0:T(8,128)(2,1)}, bf16[8,128,640]{2,1,0:T(8,128)(2,1)S(1)}, u32[]{:S(2)}) copy-start(bf16[8,128,640]{2,1,0:T(8,128)(2,1)S(1)} %all_to_all.30.rows_ref) | copy-start | bytes 3932164
  31.0 22.3 %collective-permute-start.1 = (bf16[8,128,128]{2,1,0:T(8,128)(2,1)S(1)}, bf16[8,128,128]{2,1,0:T(8,128)(2,1)S(1)}, u32[]{:S(2)}, u32[]{:S(2)}) collective-permute-start(bf16[8,128,128]{2,1,0:T(8,128)(2,1)S(1)} %slice.4), channel_id=1, source_target_pairs={{0,8},{8,0},{16,24},{24,16},{32,40},{40,32},{48,56},{56,48},{64,72... | collective-permute-start | bytes 786440 | tf_op jit(solution)/shard_map/ppermute | solution.py:608
  49.7 16.6 %all-to-all-start.2 = ((bf16[16,3,64,128]{3,2,1,0:T(8,128)(2,1)}), bf16[16,3,64,128]{3,2,1,0:T(8,128)(2,1)S(1)}, u32[]{:S(2)}, u32[]{:S(2)}) async-start(bf16[16,3,64,128]{3,2,1,0:T(8,128)(2,1)} %shard_map.95), calls=%async_computation.2 | async-start | bytes 1572864 | tf_op jit(solution)/shard_map/all_to_all | solution.py:602
  53.3 0.7 copy-start.9
  66.2 4.3 %copy-start.7 = (bf16[16,3,64,128]{3,2,1,0:T(8,128)(2,1)}, bf16[16,3,64,128]{3,2,1,0:T(8,128)(2,1)S(1)}, u32[]{:S(2)}) copy-start(bf16[16,3,64,128]{3,2,1,0:T(8,128)(2,1)S(1)} %all-to-all-done.2) | copy-start | bytes 2359300
  66.2 4.3 %collective-permute-start.2 = (bf16[48,64,128]{2,1,0:T(8,128)(2,1)S(1)}, bf16[48,64,128]{2,1,0:T(8,128)(2,1)S(1)}, u32[]{:S(2)}, u32[]{:S(2)}) collective-permute-start(bf16[48,64,128]{2,1,0:T(8,128)(2,1)S(1)} %bitcast.19), channel_id=1, source_target_pairs={{0,8},{8,0},{16,24},{24,16},{32,40},{40,32},{48,56},{56,48},{64,72... | collective-permute-start | bytes 2359304 | tf_op jit(solution)/shard_map/ppermute | solution.py:608
  70.5 0.9 copy-start.8
  91.3 2.5 %collective-permute-start.3 = (bf16[48,64,128]{2,1,0:T(8,128)(2,1)}, bf16[48,64,128]{2,1,0:T(8,128)(2,1)S(1)}, u32[]{:S(2)}, u32[]{:S(2)}) collective-permute-start(bf16[48,64,128]{2,1,0:T(8,128)(2,1)} %get-tuple-element.55), channel_id=1, source_target_pairs={{0,8},{8,0},{16,24},{24,16},{32,40},{40,32},{48,56},{56,48},{64,72... | collective-permute-start | bytes 2359304 | tf_op jit(solution)/shard_map/ppermute | solution.py:608
  96.2 20.8 %all-to-all-start.3 = ((bf16[16,3,64,128]{3,2,1,0:T(8,128)(2,1)}), bf16[16,3,64,128]{3,2,1,0:T(8,128)(2,1)S(1)}, u32[]{:S(2)}, u32[]{:S(2)}) async-start(bf16[16,3,64,128]{3,2,1,0:T(8,128)(2,1)} %bitcast.8), calls=%async_computation.3 | async-start | bytes 1572864 | tf_op jit(solution)/shard_map/all_to_all | solution.py:602
  101.1 15.9 %copy-start.5 = (s32[1,128]{1,0:T(1,128)S(1)}, s32[1,128]{1,0:T(1,128)}, u32[]{:S(2)}) copy-start(s32[1,128]{1,0:T(1,128)} %param.11) | copy-start | bytes 1540
  117.0 8.5 %copy-start.10 = (bf16[8,128,128]{2,1,0:T(8,128)(2,1)S(1)}, bf16[8,128,128]{2,1,0:T(8,128)(2,1)}, u32[]{:S(2)}) copy-start(bf16[8,128,128]{2,1,0:T(8,128)(2,1)} %get-tuple-element.68) | copy-start | bytes 786436
  118.6 15.7 %all-to-all-start.4 = ((bf16[16,64,128]{2,1,0:T(8,128)(2,1)}), bf16[16,64,128]{2,1,0:T(8,128)(2,1)S(1)}, u32[]{:S(2)}, u32[]{:S(2)}) async-start(bf16[16,64,128]{2,1,0:T(8,128)(2,1)} %shard_map.99), calls=%async_computation.4 | async-start | bytes 524288 | tf_op jit(solution)/shard_map/all_to_all | solution.py:602
  125.5 8.8 %copy-start = (bf16[8,128,640]{2,1,0:T(8,128)(2,1)S(1)}, bf16[8,128,640]{2,1,0:T(8,128)(2,1)}, u32[]{:S(2)}) copy-start(bf16[8,128,640]{2,1,0:T(8,128)(2,1)} %get-tuple-element.63.rows_ref) | copy-start | bytes 3932164
  125.5 8.8 %copy-start.2 = (f32[8,128,128]{2,1,0:T(8,128)S(1)}, f32[8,128,128]{2,1,0:T(8,128)}, u32[]{:S(2)}) copy-start(f32[8,128,128]{2,1,0:T(8,128)} %get-tuple-element.67.keep_ref) | copy-start | bytes 1572868
  125.5 8.8 %collective-permute-start.4 = (bf16[8,128,128]{2,1,0:T(8,128)(2,1)S(1)}, bf16[8,128,128]{2,1,0:T(8,128)(2,1)S(1)}, u32[]{:S(2)}, u32[]{:S(2)}) collective-permute-start(bf16[8,128,128]{2,1,0:T(8,128)(2,1)S(1)} %copy-done.10), channel_id=1, source_target_pairs={{0,8},{8,0},{16,24},{24,16},{32,40},{40,32},{48,56},{56,48},{64,72... | collective-permute-start | bytes 786440 | tf_op jit(solution)/shard_map/ppermute | solution.py:608
  134.4 0.9 copy-start.3
  156.0 4.0 %collective-permute-start.5 = (bf16[4,128,640]{2,1,0:T(8,128)(2,1)S(1)}, bf16[4,128,640]{2,1,0:T(8,128)(2,1)S(1)}, u32[]{:S(2)}, u32[]{:S(2)}) collective-permute-start(bf16[4,128,640]{2,1,0:T(8,128)(2,1)S(1)} %shard_map.102), channel_id=1, source_target_pairs={{0,8},{8,0},{16,24},{24,16},{32,40},{40,32},{48,56},{56,48},{64,72... | collective-permute-start | bytes 1966088 | tf_op jit(solution)/shard_map/ppermute | solution.py:608

commit v6 on v5

--- a/solution.py
+++ b/solution.py
@@ -293,15 +293,17 @@
     def _(r):
         by_width(plan_ref, r, functools.partial(work, r), 0)
 
-    grad_key = (dk_s[...] * INV_ROOT).astype(jnp.bfloat16)
-    grad_value = dv_s[...].astype(jnp.bfloat16)
-    keep_ref[...] = jnp.where(core() == 0, grad_key, grad_value)
-    send_ref[...] = jnp.where(core() == 0, grad_value, grad_key)
+    def cast(key_ref, value_ref):
+        key_ref[...] = (dk_s[...] * INV_ROOT).astype(jnp.bfloat16)
+        value_ref[...] = dv_s[...].astype(jnp.bfloat16)
+
+    pl.when(core() == 0)(lambda: cast(keep_ref, send_ref))
+    pl.when(core() == 1)(lambda: cast(send_ref, keep_ref))
 
 
 def score_gradients(scores, value, upstream, lse, delta):
     probs = jnp.exp2(scores - lse)
-    grad_probs = dot_nt(value, upstream)
+    grad_probs = dot(value, upstream)
     return probs, (probs * (grad_probs - delta)).astype(jnp.bfloat16)
 
 
@@ -342,7 +344,7 @@
 
 
 def rest_kernel(
-    plan_ref, rows_ref, other_ref, far_ref, came_ref, ot_ref, lse_ref, delta_ref,
+    plan_ref, qs_ref, upt_ref, own_ref, other_ref, far_ref, came_ref, ot_ref, lse_ref, delta_ref,
     out_ref, keep_ref, send_ref, part_ref,
     own_s, kv_s, kt_s, fkt_s, dk_s, dv_s, dq_s,
 ):
@@ -353,7 +355,7 @@
 
     @pl.loop(0, BT)
     def _(t):
-        own_s[core(), t] = rows_ref[t, :, 512:640]
+        own_s[core(), t] = own_ref[t]
         own_s[1 - core(), t] = other_ref[t]
         kt_s[t] = own_s[0, t].T
         for j in range(3):
@@ -361,8 +363,8 @@
 
     @pl.loop(0, BT)
     def _(r):
-        query = stacked(rows_ref, r, 0)
-        upstream = stacked(rows_ref, r, 256)
+        query = qs_ref[r]
+        upstream = upt_ref[r]
         lse = lse_ref[r][:1]
         delta = delta_ref[r][:1]
         attended = ot_ref[r].astype(jnp.float32)
@@ -379,7 +381,7 @@
                 probs, grad_scores = score_gradients(
                     scores, joined([own_s[1, t] for t in part], 0), upstream, lse, delta
                 )
-                grad_value = dot(probs.astype(jnp.bfloat16), upstream)
+                grad_value = dot_nt(probs.astype(jnp.bfloat16), upstream)
                 grad_key = dot(grad_scores, query)
                 for u, t in enumerate(part):
                     dv_s[t] += grad_value[u * TILE : (u + 1) * TILE]
@@ -408,7 +410,7 @@
 
 
 def late_kernel(
-    plan_ref, rows_ref, far_ref, came_ref, lse_ref, delta_ref, part_ref, late_ref, kv_s, fkt_s, dq_s
+    plan_ref, qs_ref, upt_ref, far_ref, came_ref, lse_ref, delta_ref, part_ref, late_ref, kv_s, fkt_s, dq_s
 ):
     kv_s[core()] = far_ref[...]
     kv_s[1 - core()] = came_ref[...]
@@ -420,8 +422,8 @@
 
     @pl.loop(EARLY, BT)
     def _(r):
-        query = stacked(rows_ref, r, 0)
-        upstream = stacked(rows_ref, r, 256)
+        query = qs_ref[r]
+        upstream = upt_ref[r]
         dq_s[...] = part_ref[r - EARLY]
         far_queries(
             plan_ref, kv_s, fkt_s, dq_s, r, query, upstream, lse_ref[r][:1], delta_ref[r][:1]
@@ -535,7 +537,7 @@
     )(plan, far, came, top, total, acc, upt, qs)
 
 
-def rest_part(plan, rows, other, far, came, ot, lse, delta):
+def rest_part(plan, qs, upt, own, other, far, came, ot, lse, delta):
     return pl.pallas_call(
         rest_kernel,
         out_shape=(
@@ -544,7 +546,7 @@
             shape((BT, TILE, HD), BF16),
             shape((BT - EARLY, HD, WIDE), F32),
         ),
-        in_specs=[SMEM] + [VMEM] * 7,
+        in_specs=[SMEM] + [VMEM] * 9,
         out_specs=(VMEM,) * 4,
         scratch_shapes=[
             pltpu.VMEM((2, BT, TILE, HD), BF16),
@@ -557,14 +559,14 @@
         ],
         compiler_params=limit(60),
         cost_estimate=cost(18),
-    )(plan, rows, other, far, came, ot, lse, delta)
-
-
-def late_part(plan, rows, far, came, lse, delta, part):
+    )(plan, qs, upt, own, other, far, came, ot, lse, delta)
+
+
+def late_part(plan, qs, upt, far, came, lse, delta, part):
     return pl.pallas_call(
         late_kernel,
         out_shape=shape((BT - EARLY, TILE, WIDE), BF16),
-        in_specs=[SMEM] + [VMEM] * 6,
+        in_specs=[SMEM] + [VMEM] * 7,
         out_specs=VMEM,
         scratch_shapes=[
             pltpu.VMEM((2, 2 * FAR, HALF, HD), BF16),
@@ -573,7 +575,7 @@
         ],
         compiler_params=limit(60),
         cost_estimate=cost(10),
-    )(plan, rows, far, came, lse, delta, part)
+    )(plan, qs, upt, far, came, lse, delta, part)
 
 
 def routed(kernel, order, array, out_shape):
@@ -620,17 +622,17 @@
     far = over_blocks(chosen).reshape(2 * FAR, HALF, HD)
     begun = near(order, tile_mask[0], rows, other)
     far, *begun = lax.optimization_barrier((far, *begun))
-    plan = begun[0]
+    plan, upt, qs = begun[0], begun[4], begun[5]
     came = to_other_core(far)
     keep, send, ot, lse, delta = far_part(plan, far, came, *begun[1:])
     dfar = (keep.astype(F32) + to_other_core(send).astype(F32)).astype(BF16)
     parts = over_blocks(dfar.reshape(NB, 3, HALF, HD))
-    out, keep, send, part = rest_part(plan, rows, other, far, came, ot, lse, delta)
+    out, keep, send, part = rest_part(plan, qs, upt, own, other, far, came, ot, lse, delta)
     parts, out, keep, send, part = lax.optimization_barrier((parts, out, keep, send, part))
     summed = routed(sum_kernel, order, parts, (NB, HALF, HD))
     summed, part = lax.optimization_barrier((summed, part))
     home = over_blocks(summed).reshape(BT, TILE, HD)
-    late = late_part(plan, rows, far, came, lse, delta, part)
+    late = late_part(plan, qs, upt, far, came, lse, delta, part)
     back = over_heads(add_home(out, late, keep, to_other_core(send), home))
     came = to_other_core(simple(pick_kernel, shape((4, TILE, 640), BF16), back))
     wide, slim = shape((TILE, 2048), BF16), shape((TILE, 512), BF16)

time: 162 us -> 165 us (1.019)
  starting transfers between devices: 25.7 us -> 29.2 us
    all_to_all x3, starting transfers between devices: 15.3 us -> 18.7 us  [over_blocks(): lax.all_to_all(array, ('blk', 'head'), split_axis=0, concat_axis=0, axis_...]
    unnamed x22 -> x24, local copies, waits for them, and re-layouts: 3.61 us -> 3.67 us
where the time goes in v6:
time: 165 us; the launch traced here: 164 us
  Pallas kernels  60 us (36%)
  blocking collectives  57.5 us (35%)
  starting transfers between devices  29.2 us (18%)
  waiting for transfers between devices  10.6 us (6%)
  local copies, waits for them, and re-layouts  3.71 us (2%)
  other arithmetic  2.36 us (1%)
    all_to_all x2, blocking collectives, over_heads(): lax.all_to_all(array, 'head', split_axis=0, concat_axis=0, tiled=True)  42.7 us
    pallas_call x1, Pallas kernels, far_part(): pl.pallas_call(far_kernel, out_shape=(shape((2 * FAR, HALF, HD), BF16), s...  20.5 us
    all_to_all x3, starting transfers between devices, over_blocks(): lax.all_to_all(array, ('blk', 'head'), split_axis=0, concat_axis=0, axis_...  18.7 us
    pallas_call x1, Pallas kernels, rest_part(): pl.pallas_call(rest_kernel, out_shape=(shape((BT, TILE, 640), BF16), shap...  15.4 us
    all_to_all x1, blocking collectives, over_blocks(): lax.all_to_all(array, ('blk', 'head'), split_axis=0, concat_axis=0, axis_...  14.8 us
    ppermute x6, starting transfers between devices, to_other_core(): return lax.ppermute(array, 'blk', [(i, i ^ 1) for i in range(16)])  10.5 us
    pallas_call x1, Pallas kernels, near(): pl.pallas_call(near_kernel, out_shape=(shape((BT, PLAN), jnp.int32), shap...  9.37 us
    ppermute x6, waiting for transfers between devices, to_other_core(): return lax.ppermute(array, 'blk', [(i, i ^ 1) for i in range(16)])  7.7 us
  transfers between devices with their start and end apart: 9, of which 5 were waited for; matrix products, arithmetic and copies ran while one was open for 0% of the time, Pallas kernels for 21%

profile of v6, /device:TPU:1, one launch (start us, length us, event | category | flops | bytes accessed | tf_op | source)
XLA Modules:
  0.0 164.1 jit_solution(2738865104880761140)
XLA Ops:
  0.6 2.5 %shard_map.93 = (bf16[4,128,640]{2,1,0:T(8,128)(2,1)}, bf16[4,128,640]{2,1,0:T(8,128)(2,1)}) custom-call(bf16[128,2048]{1,0:T(8,128)(2,1)} %bitcast.23, bf16[128,2048]{1,0:T(8,128)(2,1)} %bitcast.24, bf16[128,512]{1,0:T(8,128)(2,1)} %bitcast.25, bf16[128,512]{1,0:T(8,128)(2,1)} %bitcast.26), custom_call_target="tpu_custom_call" | custom-call | tf_op jit(solution)/shard_map/pallas_call | solution.py:454
  3.2 1.5 collective-permute-start
  4.7 1.9 %collective-permute-done.came_ref = bf16[4,128,640]{2,1,0:T(8,128)(2,1)S(1)} collective-permute-done((bf16[4,128,640]{2,1,0:T(8,128)(2,1)}, bf16[4,128,640]{2,1,0:T(8,128)(2,1)S(1)}, u32[]{:S(2)}, u32[]{:S(2)}) %collective-permute-start) | collective-permute-done | bytes 655392 | tf_op jit(solution)/shard_map/ppermute | solution.py:610
  6.6 1.1 copy-done.1
  7.7 0.1 shard_map.94
  7.8 23.1 %all_to_all.30.rows_ref = bf16[8,128,640]{2,1,0:T(8,128)(2,1)S(1)} all-to-all(bf16[8,128,640]{2,1,0:T(8,128)(2,1)S(1)} %shard_map.94), channel_id=1, replica_groups=mesh['blk'=16,'head'=8] {'head'}, dimensions={0} | all-to-all | bytes 2621440 | tf_op jit(solution)/shard_map/all_to_all | solution.py:593
  31.0 2.2 %collective-permute-start.1 = (bf16[8,128,128]{2,1,0:T(8,128)(2,1)S(1)}, bf16[8,128,128]{2,1,0:T(8,128)(2,1)S(1)}, u32[]{:S(2)}, u32[]{:S(2)}) collective-permute-start(bf16[8,128,128]{2,1,0:T(8,128)(2,1)S(1)} %slice.4.own_ref), channel_id=1, source_target_pairs={{0,8},{8,0},{16,24},{24,16},{32,40},{40,32},{48,56},{56,48},{64,72... | collective-permute-start | bytes 786440 | tf_op jit(solution)/shard_map/ppermute | solution.py:610
  33.2 14.8 %all_to_all.31.pieces_ref = bf16[16,64,128]{2,1,0:T(8,128)(2,1)S(1)} all-to-all(bf16[16,64,128]{2,1,0:T(8,128)(2,1)S(1)} %bitcast.18), channel_id=1, replica_groups={{0,4,16,20,32,36,48,52,64,68,80,84,96,100,112,116},{1,5,17,21,33,37,49,..., dimensions={0} | all-to-all | bytes 524288 | tf_op jit(solution)/shard_map/all_to_all | solution.py:604
  48.0 1.7 %shard_map.95 = bf16[16,3,64,128]{3,2,1,0:T(8,128)(2,1)} custom-call(s32[128]{0:T(128)S(1)} %bitcast.16, bf16[16,64,128]{2,1,0:T(8,128)(2,1)S(1)} %all_to_all.31.pieces_ref), custom_call_target="tpu_custom_call" | custom-call | tf_op jit(solution)/shard_map/pallas_call | solution.py:582
  49.6 3.6 %all-to-all-start.2 = ((bf16[16,3,64,128]{3,2,1,0:T(8,128)(2,1)}), bf16[16,3,64,128]{3,2,1,0:T(8,128)(2,1)S(1)}, u32[]{:S(2)}, u32[]{:S(2)}) async-start(bf16[16,3,64,128]{3,2,1,0:T(8,128)(2,1)} %shard_map.95), calls=%async_computation.2 | async-start | bytes 1572864 | tf_op jit(solution)/shard_map/all_to_all | solution.py:604
  53.3 0.7 copy-done.10
  54.0 9.4 %shard_map.96 = (s32[8,64]{1,0:T(8,128)}, f32[8,8,256]{2,1,0:T(8,128)}, f32[8,8,256]{2,1,0:T(8,128)}, f32[8,128,256]{2,1,0:T(8,128)}, bf16[8,128,256]{2,1,0:T(8,128)(2,1)}, /*index=5*/bf16[8,256,128]{2,1,0:T(8,128)(2,1)}) custom-call(s32[128]{0:T(128)} %bitcast.15, s32[128,128]{1,0:T(8,128)} %bitcast.31, bf16[8,128,640]{2,1,0:T(8,128)(2,1)} %copy-done.6, ...), custom_call_target="tpu_custom_call" | custom-call | flops 12000000000 | bytes 1200000 | tf_op jit(solution)/shard_map/pallas_call | solution.py:492
  63.3 2.9 %all-to-all-done.2 = bf16[16,3,64,128]{3,2,1,0:T(8,128)(2,1)S(1)} async-done(((bf16[16,3,64,128]{3,2,1,0:T(8,128)(2,1)}), bf16[16,3,64,128]{3,2,1,0:T(8,128)(2,1)S(1)}, u32[]{:S(2)}, u32[]{:S(2)}) %all-to-all-start.2) | async-done | bytes 786464 | tf_op jit(solution)/shard_map/all_to_all | solution.py:604
  66.2 2.4 %collective-permute-start.2 = (bf16[48,64,128]{2,1,0:T(8,128)(2,1)S(1)}, bf16[48,64,128]{2,1,0:T(8,128)(2,1)S(1)}, u32[]{:S(2)}, u32[]{:S(2)}) collective-permute-start(bf16[48,64,128]{2,1,0:T(8,128)(2,1)S(1)} %bitcast.19), channel_id=1, source_target_pairs={{0,8},{8,0},{16,24},{24,16},{32,40},{40,32},{48,56},{56,48},{64,72... | collective-permute-start | bytes 2359304 | tf_op jit(solution)/shard_map/ppermute | solution.py:610
  68.6 1.9 %collective-permute-done.2.came_ref = bf16[48,64,128]{2,1,0:T(8,128)(2,1)S(1)} collective-permute-done((bf16[48,64,128]{2,1,0:T(8,128)(2,1)S(1)}, bf16[48,64,128]{2,1,0:T(8,128)(2,1)S(1)}, u32[]{:S(2)}, u32[]{:S(2)}) %collective-permute-start.2) | collective-permute-done | bytes 786464 | tf_op jit(solution)/shard_map/ppermute | solution.py:610
  70.5 0.9 copy-done.9
  71.5 20.5 %shard_map.97 = (bf16[48,64,128]{2,1,0:T(8,128)(2,1)}, bf16[48,64,128]{2,1,0:T(8,128)(2,1)}, bf16[8,128,256]{2,1,0:T(8,128)(2,1)}, f32[8,8,256]{2,1,0:T(8,128)}, f32[8,8,256]{2,1,0:T(8,128)}) custom-call(s32[8,64]{1,0:T(8,128)} %get-tuple-element.47.plan_ref, bf16[48,64,128]{2,1,0:T(8,128)(2,1)} %bitcast.20, bf16[48,64,128]{2,1,0:T(8,128)(2,1)} %copy-done.9, ...), custom_call_target="tpu_custom_call" | custom-call | flops 24999999488 | bytes 2500000 | tf_op jit(solution)/shard_map/pallas_call | solution.py:516
  91.9 0.4 collective-permute-start.3
  92.3 2.1 %collective-permute-done.3 = bf16[48,64,128]{2,1,0:T(8,128)(2,1)S(1)} collective-permute-done((bf16[48,64,128]{2,1,0:T(8,128)(2,1)}, bf16[48,64,128]{2,1,0:T(8,128)(2,1)S(1)}, u32[]{:S(2)}, u32[]{:S(2)}) %collective-permute-start.3) | collective-permute-done | bytes 786464 | tf_op jit(solution)/shard_map/ppermute | solution.py:610
  94.4 2.4 %add_convert_fusion = bf16[48,64,128]{2,1,0:T(8,128)(2,1)} fusion(bf16[48,64,128]{2,1,0:T(8,128)(2,1)S(1)} %collective-permute-done.3, bf16[48,64,128]{2,1,0:T(8,128)(2,1)} %get-tuple-element.54), kind=kLoop, calls=%fused_computation | loop fusion | flops 1572864 | bytes 2359296 | tf_op jit(solution)/shard_map/convert_element_type | solution.py:628
  96.8 6.5 %all-to-all-start.3 = ((bf16[16,3,64,128]{3,2,1,0:T(8,128)(2,1)}), bf16[16,3,64,128]{3,2,1,0:T(8,128)(2,1)S(1)}, u32[]{:S(2)}, u32[]{:S(2)}) async-start(bf16[16,3,64,128]{3,2,1,0:T(8,128)(2,1)} %bitcast.8), calls=%async_computation.3 | async-start | bytes 1572864 | tf_op jit(solution)/shard_map/all_to_all | solution.py:604
  103.3 15.4 %shard_map.98 = (bf16[8,128,640]{2,1,0:T(8,128)(2,1)}, f32[8,128,128]{2,1,0:T(8,128)}, bf16[8,128,128]{2,1,0:T(8,128)(2,1)}, f32[3,128,256]{2,1,0:T(8,128)}) custom-call(s32[8,64]{1,0:T(8,128)} %get-tuple-element.47.plan_ref, bf16[8,256,128]{2,1,0:T(8,128)(2,1)} %get-tuple-element.53.qs_ref, bf16[8,128,256]{2,1,0:T(8,128)(2,1)} %get-tuple-element.52.upt_ref, ...), custom_call_target="tpu_custom_call" | custom-call | flops 17999998976 | bytes 1800000 | tf_op jit(solution)/shard_map/pallas_call | solution.py:541
  118.8 1.6 shard_map.99
  120.4 8.5 %all-to-all-start.4 = ((bf16[16,64,128]{2,1,0:T(8,128)(2,1)}), bf16[16,64,128]{2,1,0:T(8,128)(2,1)S(1)}, u32[]{:S(2)}, u32[]{:S(2)}) async-start(bf16[16,64,128]{2,1,0:T(8,128)(2,1)} %shard_map.99), calls=%async_computation.4 | async-start | bytes 524288 | tf_op jit(solution)/shard_map/all_to_all | solution.py:604
  129.0 1.5 collective-permute-start.4
  130.5 7.4 %shard_map.100.late_ref = bf16[3,128,256]{2,1,0:T(8,128)(2,1)} custom-call(s32[8,64]{1,0:T(8,128)} %get-tuple-element.47.plan_ref, bf16[8,256,128]{2,1,0:T(8,128)(2,1)} %get-tuple-element.53.qs_ref, bf16[8,128,256]{2,1,0:T(8,128)(2,1)} %get-tuple-element.52.upt_ref, bf16[48,64,128]{2,1,0:T(8,128)(2,1)} %bitcast.22, bf16[48,64,128]{2,1,0:T(8,128)(2,1)} %copy-done.9, ...), custom_call_target="tpu_custom_call" | custom-call | flops 10000000000 | bytes 1000000 | tf_op jit(solution)/shard_map/pallas_call | solution.py:566
  138.0 0.9 copy-done.3
  138.9 0.1 shard_map.101
  139.0 19.6 %all_to_all.32.back_ref = bf16[8,128,640]{2,1,0:T(8,128)(2,1)S(1)} all-to-all(bf16[8,128,640]{2,1,0:T(8,128)(2,1)S(1)} %shard_map.101), channel_id=1, replica_groups=mesh['blk'=16,'head'=8] {'head'}, dimensions={0} | all-to-all | bytes 2621440 | tf_op jit(solution)/shard_map/all_to_all | solution.py:593
  158.7 2.5 %collective-permute-start.5 = (bf16[4,128,640]{2,1,0:T(8,128)(2,1)S(1)}, bf16[4,128,640]{2,1,0:T(8,128)(2,1)S(1)}, u32[]{:S(2)}, u32[]{:S(2)}) collective-permute-start(bf16[4,128,640]{2,1,0:T(8,128)(2,1)S(1)} %shard_map.102), channel_id=1, source_target_pairs={{0,8},{8,0},{16,24},{24,16},{32,40},{40,32},{48,56},{56,48},{64,72... | collective-permute-start | bytes 1966088 | tf_op jit(solution)/shard_map/ppermute | solution.py:610
  161.2 1.7 %collective-permute-done.5.came_ref = bf16[4,128,640]{2,1,0:T(8,128)(2,1)S(1)} collective-permute-done((bf16[4,128,640]{2,1,0:T(8,128)(2,1)S(1)}, bf16[4,128,640]{2,1,0:T(8,128)(2,1)S(1)}, u32[]{:S(2)}, u32[]{:S(2)}) %collective-permute-start.5) | collective-permute-done | bytes 655392 | tf_op jit(solution)/shard_map/ppermute | solution.py:610
  162.9 1.2 shard_map.103
  (26 shorter events, 0.2 us)
Async XLA Ops:
  3.2 3.4 %collective-permute-start = (bf16[4,128,640]{2,1,0:T(8,128)(2,1)}, bf16[4,128,640]{2,1,0:T(8,128)(2,1)S(1)}, u32[]{:S(2)}, u32[]{:S(2)}) collective-permute-start(bf16[4,128,640]{2,1,0:T(8,128)(2,1)} %get-tuple-element.40), channel_id=1, source_target_pairs={{0,8},{8,0},{16,24},{24,16},{32,40},{40,32},{48,56},{56,48},{64,72... | collective-permute-start | bytes 1966088 | tf_op jit(solution)/shard_map/ppermute | solution.py:610
  6.6 1.1 copy-start.1
  7.8 40.2 %copy-start.4 = (s32[1,128]{1,0:T(1,128)S(1)}, s32[1,128]{1,0:T(1,128)}, u32[]{:S(2)}) copy-start(s32[1,128]{1,0:T(1,128)} %param.11) | copy-start | bytes 1540
  30.9 18.7 %copy-start.6 = (bf16[8,128,640]{2,1,0:T(8,128)(2,1)}, bf16[8,128,640]{2,1,0:T(8,128)(2,1)S(1)}, u32[]{:S(2)}) copy-start(bf16[8,128,640]{2,1,0:T(8,128)(2,1)S(1)} %all_to_all.30.rows_ref) | copy-start | bytes 3932164
  31.0 18.7 %copy-start.7 = (bf16[8,128,128]{2,1,0:T(8,128)(2,1)}, bf16[8,128,128]{2,1,0:T(8,128)(2,1)S(1)}, u32[]{:S(2)}) copy-start(bf16[8,128,128]{2,1,0:T(8,128)(2,1)S(1)} %slice.4.own_ref) | copy-start | bytes 786436
  31.0 22.3 %collective-permute-start.1 = (bf16[8,128,128]{2,1,0:T(8,128)(2,1)S(1)}, bf16[8,128,128]{2,1,0:T(8,128)(2,1)S(1)}, u32[]{:S(2)}, u32[]{:S(2)}) collective-permute-start(bf16[8,128,128]{2,1,0:T(8,128)(2,1)S(1)} %slice.4.own_ref), channel_id=1, source_target_pairs={{0,8},{8,0},{16,24},{24,16},{32,40},{40,32},{48,56},{56,48},{64,72... | collective-permute-start | bytes 786440 | tf_op jit(solution)/shard_map/ppermute | solution.py:610
  49.6 16.6 %all-to-all-start.2 = ((bf16[16,3,64,128]{3,2,1,0:T(8,128)(2,1)}), bf16[16,3,64,128]{3,2,1,0:T(8,128)(2,1)S(1)}, u32[]{:S(2)}, u32[]{:S(2)}) async-start(bf16[16,3,64,128]{3,2,1,0:T(8,128)(2,1)} %shard_map.95), calls=%async_computation.2 | async-start | bytes 1572864 | tf_op jit(solution)/shard_map/all_to_all | solution.py:604
  53.3 0.7 copy-start.10
  66.2 4.3 %copy-start.8 = (bf16[16,3,64,128]{3,2,1,0:T(8,128)(2,1)}, bf16[16,3,64,128]{3,2,1,0:T(8,128)(2,1)S(1)}, u32[]{:S(2)}) copy-start(bf16[16,3,64,128]{3,2,1,0:T(8,128)(2,1)S(1)} %all-to-all-done.2) | copy-start | bytes 2359300
  66.2 4.3 %collective-permute-start.2 = (bf16[48,64,128]{2,1,0:T(8,128)(2,1)S(1)}, bf16[48,64,128]{2,1,0:T(8,128)(2,1)S(1)}, u32[]{:S(2)}, u32[]{:S(2)}) collective-permute-start(bf16[48,64,128]{2,1,0:T(8,128)(2,1)S(1)} %bitcast.19), channel_id=1, source_target_pairs={{0,8},{8,0},{16,24},{24,16},{32,40},{40,32},{48,56},{56,48},{64,72... | collective-permute-start | bytes 2359304 | tf_op jit(solution)/shard_map/ppermute | solution.py:610
  70.5 0.9 copy-start.9
  91.9 2.5 %collective-permute-start.3 = (bf16[48,64,128]{2,1,0:T(8,128)(2,1)}, bf16[48,64,128]{2,1,0:T(8,128)(2,1)S(1)}, u32[]{:S(2)}, u32[]{:S(2)}) collective-permute-start(bf16[48,64,128]{2,1,0:T(8,128)(2,1)} %get-tuple-element.55), channel_id=1, source_target_pairs={{0,8},{8,0},{16,24},{24,16},{32,40},{40,32},{48,56},{56,48},{64,72... | collective-permute-start | bytes 2359304 | tf_op jit(solution)/shard_map/ppermute | solution.py:610
  96.8 22.0 %all-to-all-start.3 = ((bf16[16,3,64,128]{3,2,1,0:T(8,128)(2,1)}), bf16[16,3,64,128]{3,2,1,0:T(8,128)(2,1)S(1)}, u32[]{:S(2)}, u32[]{:S(2)}) async-start(bf16[16,3,64,128]{3,2,1,0:T(8,128)(2,1)} %bitcast.8), calls=%async_computation.3 | async-start | bytes 1572864 | tf_op jit(solution)/shard_map/all_to_all | solution.py:604
  103.3 15.5 %copy-start.5 = (s32[1,128]{1,0:T(1,128)S(1)}, s32[1,128]{1,0:T(1,128)}, u32[]{:S(2)}) copy-start(s32[1,128]{1,0:T(1,128)} %param.11) | copy-start | bytes 1540
  118.8 10.2 %copy-start.11 = (bf16[8,128,128]{2,1,0:T(8,128)(2,1)S(1)}, bf16[8,128,128]{2,1,0:T(8,128)(2,1)}, u32[]{:S(2)}) copy-start(bf16[8,128,128]{2,1,0:T(8,128)(2,1)} %get-tuple-element.68) | copy-start | bytes 786436
  120.4 17.5 %all-to-all-start.4 = ((bf16[16,64,128]{2,1,0:T(8,128)(2,1)}), bf16[16,64,128]{2,1,0:T(8,128)(2,1)S(1)}, u32[]{:S(2)}, u32[]{:S(2)}) async-start(bf16[16,64,128]{2,1,0:T(8,128)(2,1)} %shard_map.99), calls=%async_computation.4 | async-start | bytes 524288 | tf_op jit(solution)/shard_map/all_to_all | solution.py:604
  129.0 9.0 %copy-start = (bf16[8,128,640]{2,1,0:T(8,128)(2,1)S(1)}, bf16[8,128,640]{2,1,0:T(8,128)(2,1)}, u32[]{:S(2)}) copy-start(bf16[8,128,640]{2,1,0:T(8,128)(2,1)} %get-tuple-element.63.rows_ref) | copy-start | bytes 3932164
  129.0 9.0 %copy-start.2 = (f32[8,128,128]{2,1,0:T(8,128)S(1)}, f32[8,128,128]{2,1,0:T(8,128)}, u32[]{:S(2)}) copy-start(f32[8,128,128]{2,1,0:T(8,128)} %get-tuple-element.67.keep_ref) | copy-start | bytes 1572868
  129.0 9.0 %collective-permute-start.4 = (bf16[8,128,128]{2,1,0:T(8,128)(2,1)S(1)}, bf16[8,128,128]{2,1,0:T(8,128)(2,1)S(1)}, u32[]{:S(2)}, u32[]{:S(2)}) collective-permute-start(bf16[8,128,128]{2,1,0:T(8,128)(2,1)S(1)} %copy-done.11), channel_id=1, source_target_pairs={{0,8},{8,0},{16,24},{24,16},{32,40},{40,32},{48,56},{56,48},{64,72... | collective-permute-start | bytes 786440 | tf_op jit(solution)/shard_map/ppermute | solution.py:610
  138.0 0.9 copy-start.3
  158.7 4.2 %collective-permute-start.5 = (bf16[4,128,640]{2,1,0:T(8,128)(2,1)S(1)}, bf16[4,128,640]{2,1,0:T(8,128)(2,1)S(1)}, u32[]{:S(2)}, u32[]{:S(2)}) collective-permute-start(bf16[4,128,640]{2,1,0:T(8,128)(2,1)S(1)} %shard_map.102), channel_id=1, source_target_pairs={{0,8},{8,0},{16,24},{24,16},{32,40},{40,32},{48,56},{56,48},{64,72... | collective-permute-start | bytes 1966088 | tf_op jit(solution)/shard_map/ppermute | solution.py:610
